TPU v7x, 128 devices: a whole 4x4x4 slice. The times are simulated.
128 devices in a mesh: ctx: 8 (over z_hi, x), fsdp: 16 (over y, z_lo, core).
Axes of the slice: x: 4, y: 4, z: 4 (z_hi: 2, z_lo: 2; z = z_hi * 2 + z_lo), core: 2. Of those that a mesh axis runs over, the one named last changes fastest.
Arguments:
- tokens: bfloat16 [16, 16, 128, 768], P('fsdp', 'ctx'), may hold values from -6 to 6
- lengths: int32 [16], P('fsdp'), may hold values from 1024 to 2048, as said below
- block_map: int32 [16], replicated, may hold values from 0 to 15, as said below
- first_gain: bfloat16 [768], P('fsdp'), may hold values from 0.25 to 1.75
- first_shift: bfloat16 [768], P('fsdp'), may hold values from -1.75 to 1.75
- query_weight: bfloat16 [768, 768], P('fsdp'), may hold values from -0.21875 to 0.21875
- query_bias: bfloat16 [768], P('fsdp'), may hold values from -1.75 to 1.75
- keyval_weight: bfloat16 [768, 128], P('fsdp'), may hold values from -0.21875 to 0.21875
- value_bias: bfloat16 [64], P('fsdp'), may hold values from -3 to 3
- output_weight: bfloat16 [768, 768], P('fsdp'), may hold values from -1.75 to 1.75
- output_bias: bfloat16 [768], P('fsdp'), may hold values from -1.75 to 1.75
- second_gain: bfloat16 [768], P('fsdp'), may hold values from 0.25 to 1.75
- second_shift: bfloat16 [768], P('fsdp'), may hold values from -1.75 to 1.75
- up_weight: bfloat16 [768, 3072], P('fsdp'), may hold values from -0.21875 to 0.21875
- up_bias: bfloat16 [3072], P('fsdp'), may hold values from -1.75 to 1.75
- down_weight: bfloat16 [3072, 768], P('fsdp'), may hold values from -0.109375 to 0.109375
- down_bias: bfloat16 [768], P('fsdp'), may hold values from -1.75 to 1.75
- cotangent: float32 [16, 16, 128, 768], P('fsdp', 'ctx'), may hold values from -6 to 6
Outputs:
- layer_out: bfloat16 [16, 16, 128, 768], P('fsdp', 'ctx')
- input_grad: float32 [16, 16, 128, 768], P('fsdp', 'ctx')
- first_gain_grad: float32 [768], P('fsdp')
- first_shift_grad: float32 [768], P('fsdp')
- query_weight_grad: float32 [768, 768], P('fsdp')
- query_bias_grad: float32 [768], P('fsdp')
- keyval_weight_grad: float32 [768, 128], P('fsdp')
- value_bias_grad: float32 [64], P('fsdp')
- output_weight_grad: float32 [768, 768], P('fsdp')
- output_bias_grad: float32 [768], P('fsdp')
- second_gain_grad: float32 [768], P('fsdp')
- second_shift_grad: float32 [768], P('fsdp')
- up_weight_grad: float32 [768, 3072], P('fsdp')
- up_bias_grad: float32 [3072], P('fsdp')
- down_weight_grad: float32 [3072, 768], P('fsdp')
- down_bias_grad: float32 [768], P('fsdp')
Inputs may be any that keep to these rules, and one draw needn't show every extreme that they name: `lengths`: every draw has a sequence of exactly 2048 valid tokens, which one drawn from the seed. `block_map`: each block once; slots 2c and 2c + 1 hold a block b and its mirror 16 - 1 - b.
All inputs are finite; a program needn't handle non-finite values.
Results may differ from a plain program's by a relative error of at most 0.024.
Values may be sent and summed in bfloat16 or wider, within the bound.
A program may use at most 128 MiB of HBM per device.

v0:
```python
import math

import jax
import jax.numpy as jnp
from jax import lax
from jax.sharding import PartitionSpec as P

EPS = 1e-05
MASKED = -1e30


def layer_norm(values, gain_vec, bias_vec):
    centre = values - jnp.mean(values, -1, keepdims=True)
    spread = jnp.mean(centre * centre, -1, keepdims=True)
    return centre * lax.rsqrt(spread + EPS) * gain_vec + bias_vec


def gelu_tanh(values):
    return jax.nn.gelu(values, approximate=True)


def inner_rows(left, right):
    return lax.dot_general(
        left, right, (((0,), (0,)), ((), ())), preferred_element_type=jnp.float32
    )


def inner_cols(left, right):
    return lax.dot_general(
        left, right, (((1,), (1,)), ((), ())), preferred_element_type=jnp.float32
    )


def fetch_attention(
    first_gain,
    first_shift,
    query_weight,
    query_bias,
    keyval_weight,
    value_bias,
    output_weight,
    output_bias,
):
    return (
        lax.all_gather(first_gain, "fsdp", axis=0, tiled=True),
        lax.all_gather(first_shift, "fsdp", axis=0, tiled=True),
        lax.all_gather(query_weight, "fsdp", axis=0, tiled=True),
        lax.all_gather(query_bias, "fsdp", axis=0, tiled=True),
        lax.all_gather(keyval_weight, "fsdp", axis=0, tiled=True),
        lax.all_gather(value_bias, "fsdp", axis=0, tiled=True),
        lax.all_gather(output_weight, "fsdp", axis=0, tiled=True),
        lax.all_gather(output_bias, "fsdp", axis=0, tiled=True),
    )


def fetch_mlp(second_gain, second_shift, up_weight, up_bias, down_weight, down_bias):
    return (
        lax.all_gather(second_gain, "fsdp", axis=0, tiled=True),
        lax.all_gather(second_shift, "fsdp", axis=0, tiled=True),
        lax.all_gather(up_weight, "fsdp", axis=0, tiled=True),
        lax.all_gather(up_bias, "fsdp", axis=0, tiled=True),
        lax.all_gather(down_weight, "fsdp", axis=0, tiled=True),
        lax.all_gather(down_bias, "fsdp", axis=0, tiled=True),
    )


def attend_forward(query_rows, keyval, seq_length, query_pos, key_pos):
    head_dim = query_rows.shape[1]
    score_scale = head_dim ** (-0.5)
    key_part = keyval[:, :head_dim]
    value_part = keyval[:, head_dim:]
    key_live = key_pos < seq_length
    block_rows = math.gcd(512, query_rows.shape[0])

    def one_block(pieces):
        query_blk, pos_blk = pieces
        scores = inner_cols(query_blk, key_part) * score_scale
        allowed = (key_pos[None, :] <= pos_blk[:, None]) & key_live[None, :]
        scores = jnp.where(allowed, scores, MASKED)
        row_max = jnp.max(scores, -1, keepdims=True)
        expo_vals = jnp.exp(scores - row_max)
        row_total = jnp.sum(expo_vals, -1, keepdims=True)
        prob_low = (expo_vals / row_total).astype(jnp.bfloat16)
        return (
            jnp.dot(prob_low, value_part, preferred_element_type=jnp.float32),
            (row_max + jnp.log(row_total))[:, 0],
        )

    outputs, logsum = lax.map(
        one_block, (query_rows.reshape(-1, block_rows, head_dim), query_pos.reshape(-1, block_rows))
    )
    return (outputs.reshape(-1, head_dim), logsum.reshape(-1))


def attend_backward(query_rows, keyval, grad_rows, logsum, seq_length, query_pos, key_pos):
    head_dim = query_rows.shape[1]
    score_scale = head_dim ** (-0.5)
    key_part = keyval[:, :head_dim]
    value_part = keyval[:, head_dim:]
    key_live = key_pos < seq_length
    block_rows = math.gcd(512, query_rows.shape[0])

    def one_block(carry, pieces):
        query_blk, pos_blk, grad_blk, logsum_blk = pieces
        scores = inner_cols(query_blk, key_part) * score_scale
        allowed = (key_pos[None, :] <= pos_blk[:, None]) & key_live[None, :]
        scores = jnp.where(allowed, scores, MASKED)
        probs = jnp.exp(scores - logsum_blk[:, None])
        grad_prob = inner_cols(grad_blk, value_part)
        centre = jnp.sum(probs * grad_prob, -1, keepdims=True)
        grad_score = (probs * (grad_prob - centre)).astype(jnp.bfloat16)
        grad_query = jnp.dot(grad_score, key_part, preferred_element_type=jnp.float32) * score_scale
        grad_key = inner_rows(grad_score, query_blk) * score_scale
        grad_value = inner_rows(probs.astype(jnp.bfloat16), grad_blk)
        return (carry + jnp.concatenate([grad_key, grad_value], 1), grad_query)

    start_grad = jnp.zeros(keyval.shape, jnp.float32)
    grad_keyval, grad_query = lax.scan(
        one_block,
        start_grad,
        (
            query_rows.reshape(-1, block_rows, head_dim),
            query_pos.reshape(-1, block_rows),
            grad_rows.reshape(-1, block_rows, head_dim),
            logsum.reshape(-1, block_rows),
        ),
    )
    return (grad_query.reshape(-1, head_dim), grad_keyval)


def attention_forward(x_rows, weights, lengths, query_pos, key_pos, seq_count):
    (
        first_gain,
        first_shift,
        query_weight,
        query_bias,
        keyval_weight,
        value_bias,
        output_weight,
        output_bias,
    ) = weights
    head_dim = value_bias.shape[0]
    normed_low = layer_norm(
        x_rows, first_gain.astype(jnp.float32), first_shift.astype(jnp.float32)
    ).astype(jnp.bfloat16)
    query = (
        jnp.dot(normed_low, query_weight, preferred_element_type=jnp.float32)
        + query_bias.astype(jnp.float32)
    ).astype(jnp.bfloat16)
    keyval_bias = jnp.concatenate(
        [jnp.zeros((head_dim,), jnp.float32), value_bias.astype(jnp.float32)]
    )
    keyval = (
        jnp.dot(normed_low, keyval_weight, preferred_element_type=jnp.float32) + keyval_bias
    ).astype(jnp.bfloat16)
    keyval_all = lax.all_gather(
        keyval.reshape(seq_count, -1, 2 * head_dim), "ctx", axis=1, tiled=True
    )
    query_rows = query.reshape(seq_count, -1, head_dim)

    def one_sequence(pieces):
        return attend_forward(pieces[0], pieces[1], pieces[2], query_pos, key_pos)

    attended, logsum = lax.map(one_sequence, (query_rows, keyval_all, lengths))
    attended = attended.reshape(x_rows.shape[0], -1).astype(jnp.bfloat16)
    mixed = (
        x_rows
        + jnp.dot(attended, output_weight, preferred_element_type=jnp.float32)
        + output_bias.astype(jnp.float32)
    )
    return (normed_low, query_rows, keyval_all, attended, logsum, mixed)


def mlp_forward(mixed, weights):
    second_gain, second_shift, up_weight, up_bias, down_weight, down_bias = weights
    normed_low = layer_norm(
        mixed, second_gain.astype(jnp.float32), second_shift.astype(jnp.float32)
    ).astype(jnp.bfloat16)
    upward = jnp.dot(normed_low, up_weight, preferred_element_type=jnp.float32) + up_bias.astype(
        jnp.float32
    )
    middle = gelu_tanh(upward).astype(jnp.bfloat16)
    result = (
        mixed
        + jnp.dot(middle, down_weight, preferred_element_type=jnp.float32)
        + down_bias.astype(jnp.float32)
    )
    return (normed_low, upward, middle, result)


def shards(
    tokens,
    lengths,
    block_map,
    first_gain,
    first_shift,
    query_weight,
    query_bias,
    keyval_weight,
    value_bias,
    output_weight,
    output_bias,
    second_gain,
    second_shift,
    up_weight,
    up_bias,
    down_weight,
    down_bias,
    cotangent,
):
    seq_count, slot_count, block_len, width = tokens.shape
    row_count = seq_count * slot_count * block_len
    head_dim = keyval_weight.shape[1] // 2
    heads = query_weight.shape[1] // head_dim
    offsets = jnp.arange(block_len, dtype=jnp.int32)
    own_map = lax.dynamic_slice_in_dim(block_map, lax.axis_index("ctx") * slot_count, slot_count)
    own_pos = (own_map[:, None] * block_len + offsets[None, :]).reshape(-1)
    key_pos = (block_map[:, None] * block_len + offsets[None, :]).reshape(-1)
    query_pos = jnp.repeat(own_pos, heads)
    valid = (own_pos[None, :] < lengths[:, None]).astype(jnp.float32).reshape(row_count, 1)
    x_rows = tokens.reshape(row_count, width).astype(jnp.float32)
    attn_first = fetch_attention(
        first_gain,
        first_shift,
        query_weight,
        query_bias,
        keyval_weight,
        value_bias,
        output_weight,
        output_bias,
    )
    forward_first = attention_forward(x_rows, attn_first, lengths, query_pos, key_pos, seq_count)
    mlp_first = fetch_mlp(second_gain, second_shift, up_weight, up_bias, down_weight, down_bias)
    result_first = mlp_forward(forward_first[5], mlp_first)[3]
    layer_out = (valid * result_first).astype(jnp.bfloat16).reshape(tokens.shape)
    attn_weights = fetch_attention(
        first_gain,
        first_shift,
        query_weight,
        query_bias,
        keyval_weight,
        value_bias,
        output_weight,
        output_bias,
    )
    normed_one, query_rows, keyval_all, attended, logsum, mixed = attention_forward(
        x_rows, attn_weights, lengths, query_pos, key_pos, seq_count
    )
    mlp_weights = fetch_mlp(second_gain, second_shift, up_weight, up_bias, down_weight, down_bias)
    normed_two, upward, middle, result = mlp_forward(mixed, mlp_weights)
    second_gain_all, second_shift_all, up_all, up_bias_all, down_all, down_bias_all = mlp_weights
    grad_out = valid * cotangent.reshape(row_count, width)
    grad_out_low = grad_out.astype(jnp.bfloat16)
    grad_downbias = jnp.sum(grad_out_low.astype(jnp.float32), 0)
    grad_down = inner_rows(middle, grad_out_low)
    grad_middle = inner_cols(grad_out_low, down_all)
    gelu_pull = jax.vjp(gelu_tanh, upward)[1]
    grad_upward = gelu_pull(grad_middle)[0].astype(jnp.bfloat16)
    grad_upbias = jnp.sum(grad_upward.astype(jnp.float32), 0)
    grad_up = inner_rows(normed_two, grad_upward)
    grad_second = inner_cols(grad_upward, up_all)
    second_pull = jax.vjp(
        layer_norm, mixed, second_gain_all.astype(jnp.float32), second_shift_all.astype(jnp.float32)
    )[1]
    grad_mixed_norm, grad_second_gain, grad_second_shift = second_pull(grad_second)
    grad_mixed = grad_out + grad_mixed_norm
    mlp_shares = (
        lax.psum_scatter(
            grad_second_gain.astype(jnp.bfloat16), "fsdp", scatter_dimension=0, tiled=True
        ).astype(jnp.float32),
        lax.psum_scatter(
            grad_second_shift.astype(jnp.bfloat16), "fsdp", scatter_dimension=0, tiled=True
        ).astype(jnp.float32),
        lax.psum_scatter(
            grad_up.astype(jnp.bfloat16), "fsdp", scatter_dimension=0, tiled=True
        ).astype(jnp.float32),
        lax.psum_scatter(
            grad_upbias.astype(jnp.bfloat16), "fsdp", scatter_dimension=0, tiled=True
        ).astype(jnp.float32),
        lax.psum_scatter(
            grad_down.astype(jnp.bfloat16), "fsdp", scatter_dimension=0, tiled=True
        ).astype(jnp.float32),
        lax.psum_scatter(
            grad_downbias.astype(jnp.bfloat16), "fsdp", scatter_dimension=0, tiled=True
        ).astype(jnp.float32),
    )
    (
        first_gain_all,
        first_shift_all,
        query_all,
        query_bias_all,
        keyval_wall,
        value_bias_all,
        output_all,
        output_bias_all,
    ) = attn_weights
    grad_mixed_low = grad_mixed.astype(jnp.bfloat16)
    grad_outbias = jnp.sum(grad_mixed_low.astype(jnp.float32), 0)
    grad_output = inner_rows(attended, grad_mixed_low)
    grad_attended = (
        inner_cols(grad_mixed_low, output_all).astype(jnp.bfloat16).reshape(seq_count, -1, head_dim)
    )

    def sequence_back(pieces):
        return attend_backward(
            pieces[0], pieces[1], pieces[2], pieces[3], pieces[4], query_pos, key_pos
        )

    grad_query_rows, grad_keyval_part = lax.map(
        sequence_back, (query_rows, keyval_all, grad_attended, logsum, lengths)
    )
    grad_keyval = (
        lax.psum_scatter(
            grad_keyval_part.astype(jnp.bfloat16), "ctx", scatter_dimension=1, tiled=True
        )
        .astype(jnp.float32)
        .reshape(row_count, 2 * head_dim)
        .astype(jnp.bfloat16)
    )
    grad_query = grad_query_rows.reshape(row_count, -1).astype(jnp.bfloat16)
    grad_querybias = jnp.sum(grad_query.astype(jnp.float32), 0)
    grad_queryw = inner_rows(normed_one, grad_query)
    grad_valuebias = jnp.sum(grad_keyval[:, head_dim:].astype(jnp.float32), 0)
    grad_keyvalw = inner_rows(normed_one, grad_keyval)
    grad_first = inner_cols(grad_query, query_all) + inner_cols(grad_keyval, keyval_wall)
    first_pull = jax.vjp(
        layer_norm, x_rows, first_gain_all.astype(jnp.float32), first_shift_all.astype(jnp.float32)
    )[1]
    grad_x_norm, grad_first_gain, grad_first_shift = first_pull(grad_first)
    input_grad = (grad_mixed + grad_x_norm).reshape(tokens.shape)
    attn_shares = (
        lax.psum_scatter(
            grad_first_gain.astype(jnp.bfloat16), "fsdp", scatter_dimension=0, tiled=True
        ).astype(jnp.float32),
        lax.psum_scatter(
            grad_first_shift.astype(jnp.bfloat16), "fsdp", scatter_dimension=0, tiled=True
        ).astype(jnp.float32),
        lax.psum_scatter(
            grad_queryw.astype(jnp.bfloat16), "fsdp", scatter_dimension=0, tiled=True
        ).astype(jnp.float32),
        lax.psum_scatter(
            grad_querybias.astype(jnp.bfloat16), "fsdp", scatter_dimension=0, tiled=True
        ).astype(jnp.float32),
        lax.psum_scatter(
            grad_keyvalw.astype(jnp.bfloat16), "fsdp", scatter_dimension=0, tiled=True
        ).astype(jnp.float32),
        lax.psum_scatter(
            grad_valuebias.astype(jnp.bfloat16), "fsdp", scatter_dimension=0, tiled=True
        ).astype(jnp.float32),
        lax.psum_scatter(
            grad_output.astype(jnp.bfloat16), "fsdp", scatter_dimension=0, tiled=True
        ).astype(jnp.float32),
        lax.psum_scatter(
            grad_outbias.astype(jnp.bfloat16), "fsdp", scatter_dimension=0, tiled=True
        ).astype(jnp.float32),
    )
    totals = (
        lax.psum(attn_shares[0].astype(jnp.bfloat16), "ctx").astype(jnp.float32),
        lax.psum(attn_shares[1].astype(jnp.bfloat16), "ctx").astype(jnp.float32),
        lax.psum(attn_shares[2].astype(jnp.bfloat16), "ctx").astype(jnp.float32),
        lax.psum(attn_shares[3].astype(jnp.bfloat16), "ctx").astype(jnp.float32),
        lax.psum(attn_shares[4].astype(jnp.bfloat16), "ctx").astype(jnp.float32),
        lax.psum(attn_shares[5].astype(jnp.bfloat16), "ctx").astype(jnp.float32),
        lax.psum(attn_shares[6].astype(jnp.bfloat16), "ctx").astype(jnp.float32),
        lax.psum(attn_shares[7].astype(jnp.bfloat16), "ctx").astype(jnp.float32),
        lax.psum(mlp_shares[0].astype(jnp.bfloat16), "ctx").astype(jnp.float32),
        lax.psum(mlp_shares[1].astype(jnp.bfloat16), "ctx").astype(jnp.float32),
        lax.psum(mlp_shares[2].astype(jnp.bfloat16), "ctx").astype(jnp.float32),
        lax.psum(mlp_shares[3].astype(jnp.bfloat16), "ctx").astype(jnp.float32),
        lax.psum(mlp_shares[4].astype(jnp.bfloat16), "ctx").astype(jnp.float32),
        lax.psum(mlp_shares[5].astype(jnp.bfloat16), "ctx").astype(jnp.float32),
    )
    return (
        layer_out,
        input_grad,
        totals[0],
        totals[1],
        totals[2],
        totals[3],
        totals[4],
        totals[5],
        totals[6],
        totals[7],
        totals[8],
        totals[9],
        totals[10],
        totals[11],
        totals[12],
        totals[13],
    )


def solution(mesh):
    placed = (
        P("fsdp", "ctx", None, None),
        P("fsdp"),
        P(),
        P("fsdp"),
        P("fsdp"),
        P("fsdp", None),
        P("fsdp"),
        P("fsdp", None),
        P("fsdp"),
        P("fsdp", None),
        P("fsdp"),
        P("fsdp"),
        P("fsdp"),
        P("fsdp", None),
        P("fsdp"),
        P("fsdp", None),
        P("fsdp"),
        P("fsdp", "ctx", None, None),
    )
    return jax.shard_map(
        shards,
        mesh=mesh,
        in_specs=placed,
        out_specs=(
            P("fsdp", "ctx", None, None),
            P("fsdp", "ctx", None, None),
            P("fsdp"),
            P("fsdp"),
            P("fsdp", None),
            P("fsdp"),
            P("fsdp", None),
            P("fsdp"),
            P("fsdp", None),
            P("fsdp"),
            P("fsdp"),
            P("fsdp"),
            P("fsdp", None),
            P("fsdp"),
            P("fsdp", None),
            P("fsdp"),
        ),
        check_vma=False,
    )
```

profile of v0, /device:TPU:0, one launch (start us, length us, event | category | flops | bytes accessed | tf_op | source)
XLA Modules:
  0.0 824.4 jit_solution(10735596926647286596)
XLA Ops:
  20.1 56.7 %all-reduce.20 = (bf16[768]{0:T(1024)(128)(2,1)S(1)}, bf16[768]{0:T(1024)(128)(2,1)S(1)}, bf16[768]{0:T(1024)(128)(2,1)S(1)}, bf16[64]{0:T(256)(128)(2,1)S(1)}, ...) all-reduce(bf16[768]{0:T(1024)(128)(2,1)S(1)} %dynamic-update-slice, ...), channel_id=1, replica_groups=mesh['ctx'=8,'fsdp'=16] {'fsdp'}, use_global_device_ids=true, to_apply=%add.2 | all-reduce | flops 7744 | bytes 30976
  79.8 16.9 %all_gather.63 = bf16[768,128]{1,0:T(8,128)(2,1)S(1)} all-gather(bf16[48,128]{1,0:T(8,128)(2,1)} %param.31), channel_id=1, replica_groups=mesh['ctx'=8,'fsdp'=16] {'fsdp'}, dimensions={0}, use_global_device_ids=true | all-gather | bytes 208896 | tf_op jit(solution)/shard_map/all_gather | solution.py:49
  98.3 36.6 %all-gather = bf16[2048,128]{1,0:T(8,128)(2,1)S(1)} all-gather(bf16[256,128]{1,0:T(8,128)(2,1)S(1)} %fusion.77), channel_id=2, replica_groups=mesh['ctx'=8,'fsdp'=16] {'ctx'}, dimensions={0}, use_global_device_ids=true | all-gather | bytes 589824 | tf_op jit(solution)/shard_map/all_gather | solution.py:156
  141.2 67.8 %while.67 = (s32[]{:T(128)}, bf16[6,512,64]{1,2,0:T(8,128)(2,1)S(1)}, f32[6,512]{1,0:T(8,128)}, s32[6,512]{1,0:T(8,128)}, bf16[6,512,64]{2,1,0:T(8,128)(2,1)}, /...) while((s32[]{:T(128)}, ...), condition=%wide.region_11.12_spmd.clone.clone, body=%wide.region_8.11_spmd.clone.clone.sunk | while | flops 278926848 | bytes 30456600 | solution.py:89
  142.8 2.3 fusion.190
  149.3 3.3 fusion.192
  154.2 2.3 fusion.190
  160.7 3.3 fusion.192
  165.5 2.3 fusion.190
  171.9 3.3 fusion.192
  176.7 2.3 fusion.190
  183.2 3.3 fusion.192
  188.0 2.3 fusion.190
  194.5 3.3 fusion.192
  199.3 2.3 fusion.190
  205.8 3.3 fusion.192
  212.2 5.4 fusion.115
  217.6 8.6 %fusion.106 = (bf16[3072]{0:T(1024)(128)(2,1)}, bf16[256,3072]{1,0:T(8,128)(2,1)S(1)}, f32[256,3072]{1,0:T(8,128)}) fusion(f32[256,3072]{1,0:T(8,128)} %fusion.115, f32[3072]{0:T(1024)S(1)} %convert_element_type.273, bf16[768,3072]{1,0:T(8,128)(2,1)} %all-gather.10.cloned.1.call-done, f32[256,768]{1,0:T(8,128)S(1)} %get-tuple-element.562, ...), kind=kOutput, calls=%fused_computation.174 | convolution fusion | flops 1226241024 | bytes 13395968 | tf_op jit(solution)/shard_map/dot_general | solution.py:179
  233.1 89.4 %while.68 = (s32[]{:T(128)}, f32[2048,128]{0,1:T(8,128)}, bf16[6,512,64]{1,2,0:T(8,128)(2,1)}, s32[6,512]{1,0:T(8,128)}, bf16[6,512,64]{2,1,0:T(8,128)(2,1)}, /*...) while((s32[]{:T(128)}, f32[2048,128]{0,1:T(8,128)}, ...), condition=%wide.region_18.19_spmd.clone.clone.clone, body=%wide.region_16.18_spmd.clone.clone.clone.sunk | while | flops 683578880 | bytes 37919504 | solution.py:118
  237.1 3.0 multiply_reduce_fusion.9
  244.5 2.4 fusion.206
  251.0 3.0 multiply_reduce_fusion.9
  259.6 2.4 fusion.206
  266.1 3.0 multiply_reduce_fusion.9
  274.7 2.4 fusion.206
  281.2 3.0 multiply_reduce_fusion.9
  289.8 2.4 fusion.206
  296.3 3.0 multiply_reduce_fusion.9
  304.9 2.4 fusion.206
  311.4 3.0 multiply_reduce_fusion.9
  320.0 2.4 fusion.206
  324.6 2.9 convolution_convert_fusion.2
  331.5 5.3 convolution_convert_fusion.1
  339.9 6.2 convolution_convert_fusion
  346.3 40.5 %while.66 = (s32[]{:T(128)}, bf16[6,512,64]{1,2,0:T(8,128)(2,1)S(1)}, s32[6,512]{1,0:T(8,128)}, bf16[6,512,64]{2,1,0:T(8,128)(2,1)}, bf16[2048,64]{1,0:T(8,128)(...) while((s32[]{:T(128)}, ...), condition=%wide.region_5.6_spmd.clone.clone, body=%wide.region_2.5_spmd.clone.clone.sunk | while | flops 278926336 | bytes 13669097 | solution.py:89
  354.9 2.3 fusion.183
  361.6 2.3 fusion.183
  368.3 2.3 fusion.183
  390.4 2.7 fusion.116
  399.1 53.4 %all-reduce.19 = (bf16[768]{0:T(1024)(128)(2,1)S(1)}, bf16[768]{0:T(1024)(128)(2,1)S(1)}, bf16[768]{0:T(1024)(128)(2,1)S(1)}, bf16[768]{0:T(1024)(128)(2,1)S(1)}...) all-reduce(bf16[768]{0:T(1024)(128)(2,1)S(1)} %copy-done.39, ...), channel_id=1, replica_groups=mesh['ctx'=8,'fsdp'=16] {'fsdp'}, use_global_device_ids=true, to_apply=%add.9 | all-reduce | flops 9280 | bytes 37120
  454.3 3.4 reduce-scatter.13.cloned.1.call-done
  457.7 63.2 %reduce-scatter.9.cloned.1.call-done = bf16[48,768]{1,0:T(8,128)(2,1)} async-done(((bf16[768,768]{1,0:T(8,128)(2,1)}), bf16[48,768]{1,0:T(8,128)(2,1)}) %reduce-scatter.9.cloned.1.call-update) | async-done | bytes 73744 | tf_op jit(solution)/shard_map/reduce_scatter | solution.py:338
  520.9 69.7 %reduce-scatter.15.cloned.1.call-done = bf16[48,3072]{1,0:T(8,128)(2,1)} async-done(((bf16[768,3072]{1,0:T(8,128)(2,1)}), bf16[48,3072]{1,0:T(8,128)(2,1)}) %reduce-scatter.15.cloned.1.call-update) | async-done | bytes 294928 | tf_op jit(solution)/shard_map/reduce_scatter | solution.py:274
  590.6 69.9 %reduce-scatter.17.cloned.1.call-done = bf16[192,768]{1,0:T(8,128)(2,1)} async-done(((bf16[3072,768]{1,0:T(8,128)(2,1)}), bf16[192,768]{1,0:T(8,128)(2,1)}) %reduce-scatter.17.cloned.1.call-update) | async-done | bytes 294928 | tf_op jit(solution)/shard_map/reduce_scatter | solution.py:280
  660.6 7.6 fusion.76
  668.2 54.8 %reduce-scatter.11.cloned.1.call-done = bf16[48,128]{1,0:T(8,128)(2,1)} async-done(((bf16[768,128]{1,0:T(8,128)(2,1)}), bf16[48,128]{1,0:T(8,128)(2,1)}) %reduce-scatter.11.cloned.1.call-update) | async-done | bytes 12304 | tf_op jit(solution)/shard_map/reduce_scatter | solution.py:344
  723.0 41.5 %all-reduce.21 = (bf16[48]{0:T(256)(128)(2,1)S(1)}, bf16[48]{0:T(256)(128)(2,1)S(1)}, bf16[48]{0:T(256)(128)(2,1)S(1)}, bf16[48,128]{1,0:T(8,128)(2,1)S(1)}, bf1...) all-reduce(bf16[48]{0:T(256)(128)(2,1)S(1)} %dynamic-slice.10, ...), channel_id=1, replica_groups=mesh['ctx'=8,'fsdp'=16] {'ctx'}, use_global_device_ids=true, to_apply=%region_24.25 | all-reduce | flops 6676 | bytes 26704 | tf_op jit(solution)/shard_map/psum | solution.py:358
  769.8 41.4 %all-reduce.25.cloned.1.call-done = (bf16[48,768]{1,0:T(8,128)(2,1)}, bf16[48,768]{1,0:T(8,128)(2,1)}, bf16[48,3072]{1,0:T(8,128)(2,1)}, bf16[192,768]{1,0:T(8,128)(2,1)}) async-done(((bf16[48,768]{1,0:T(8,128)(2,1)}, bf16[48,768]{1,0:T(8,128)(2,1)}, bf16[48,3072]{1,0:T(8,128)(2,1)}, bf16[192,768]{1,0:T(8,128)(2,1)}), (bf16[48,768]{1,0:T(8,128)(2,1)}, bf16[48,768]{1,0:T(8,128)(2,1)}, ...) | async-done | bytes 737296 | tf_op jit(solution)/shard_map/psum | solution.py:360
  (369 shorter events, 185.0 us)
Async XLA Ops:
  7.2 128.9 %copy-start.49 = (s32[16]{0:T(128)S(1)}, s32[16]{0:T(128)}, u32[]{:S(2)}) copy-start(s32[16]{0:T(128)} %param.26) | copy-start | bytes 196
  7.2 130.8 %all-gather.6.cloned.1.call-start = ((), (), s32[]{:S(2)}) async-start(), calls=%async_computation.6 | async-start | bytes 1253376 | tf_op jit(solution)/shard_map/all_gather | solution.py:47
  7.9 129.9 %copy-start.8 = (f32[1,2,128,768]{3,2,1,0:T(8,128)S(1)}, f32[1,2,128,768]{3,2,1,0:T(8,128)}, u32[]{:S(2)}) copy-start(f32[1,2,128,768]{3,2,1,0:T(8,128)} %param.41) | copy-start | bytes 2359300
  7.9 202.0 %all-gather.8.cloned.1.call-start = ((), (), s32[]{:S(2)}) async-start(), calls=%async_computation.7 | async-start | bytes 1253376 | tf_op jit(solution)/shard_map/all_gather | solution.py:51
  8.7 203.5 %all-gather.12.cloned.1.call-start = ((), (), s32[]{:S(2)}) async-start(), calls=%async_computation.9 | async-start | bytes 5013504 | tf_op jit(solution)/shard_map/all_gather | solution.py:62
  9.4 208.2 %all-gather.10.cloned.1.call-start = ((), (), s32[]{:S(2)}) async-start(), calls=%async_computation.8 | async-start | bytes 5013504 | tf_op jit(solution)/shard_map/all_gather | solution.py:60
  10.0 384.3 %reduce-scatter.7.cloned.1.call-start = ((), (), s32[]{:S(2)}) async-start(), calls=%async_computation.10 | async-start | bytes 589824 | tf_op jit(solution)/shard_map/reduce_scatter | solution.py:313
  76.8 59.4 %copy-start.17 = (f32[768]{0:T(1024)}, f32[768]{0:T(1024)S(1)}, u32[]{:S(2)}) copy-start(f32[768]{0:T(1024)S(1)} %convert_element_type.262) | copy-start | bytes 9220
  77.9 58.2 %copy-start.19 = (f32[256]{0:T(256)}, f32[256]{0:T(256)S(1)}, u32[]{:S(2)}) copy-start(f32[256]{0:T(256)S(1)} %get-tuple-element.557) | copy-start | bytes 3076
  79.7 56.4 %copy-start.25 = (f32[2,128]{1,0:T(2,128)}, f32[2,128]{1,0:T(2,128)S(1)}, u32[]{:S(2)}) copy-start(f32[2,128]{1,0:T(2,128)S(1)} %multiply_reduce_fusion.7) | copy-start | bytes 3076
  79.8 56.4 %copy-start.23 = (f32[256]{0:T(256)}, f32[256]{0:T(256)S(1)}, u32[]{:S(2)}) copy-start(f32[256]{0:T(256)S(1)} %bitcast_rsqrt_fusion) | copy-start | bytes 3076
  136.2 5.1 copy-start.45
  137.1 72.9 %copy-start.16 = (f32[768]{0:T(1024)}, f32[768]{0:T(1024)S(1)}, u32[]{:S(2)}) copy-start(f32[768]{0:T(1024)S(1)} %convert_element_type.269) | copy-start | bytes 9220
  137.1 80.5 %copy-start.29 = (f32[3072]{0:T(1024)}, f32[3072]{0:T(1024)S(1)}, u32[]{:S(2)}) copy-start(f32[3072]{0:T(1024)S(1)} %convert_element_type.273) | copy-start | bytes 36868
  137.8 91.0 %copy-start.33 = (f32[256]{0:T(256)}, f32[256]{0:T(256)S(1)}, u32[]{:S(2)}) copy-start(f32[256]{0:T(256)S(1)} %compare_convert_fusion.1) | copy-start | bytes 3076
  138.0 74.2 %copy-start.12 = (bf16[256,768]{1,0:T(8,128)(2,1)}, bf16[256,768]{1,0:T(8,128)(2,1)S(1)}, u32[]{:S(2)}) copy-start(bf16[256,768]{1,0:T(8,128)(2,1)S(1)} %fusion.78) | copy-start | bytes 1179652
  141.2 68.7 %copy-start.1 = (bf16[1,2,128,768]{3,2,1,0:T(8,128)(2,1)S(1)}, bf16[1,2,128,768]{3,2,1,0:T(8,128)(2,1)}, u32[]{:S(2)}) copy-start(bf16[1,2,128,768]{3,2,1,0:T(8,128)(2,1)} %param.24) | copy-start | bytes 1179652
  209.9 7.7 copy-start.10
  211.9 16.5 %copy-start.2 = (f32[256,768]{1,0:T(8,128)}, f32[256,768]{1,0:T(8,128)S(1)}, u32[]{:S(2)}) copy-start(f32[256,768]{1,0:T(8,128)S(1)} %get-tuple-element.562) | copy-start | bytes 2359300
  211.9 16.5 %copy-start.21 = (f32[256]{0:T(256)}, f32[256]{0:T(256)S(1)}, u32[]{:S(2)}) copy-start(f32[256]{0:T(256)S(1)} %broadcast_multiply_fusion) | copy-start | bytes 3076
  212.2 16.3 %copy-start.27 = (f32[256]{0:T(256)}, f32[256]{0:T(256)S(1)}, u32[]{:S(2)}) copy-start(f32[256]{0:T(256)S(1)} %fusion.89) | copy-start | bytes 3076
  217.6 8.6 %copy-start.48 = (bf16[768,3072]{1,0:T(8,128)(2,1)S(1)}, bf16[768,3072]{1,0:T(8,128)(2,1)}, u32[]{:S(2)}) copy-start(bf16[768,3072]{1,0:T(8,128)(2,1)} %all-gather.10.cloned.1.call-done) | copy-start | bytes 14155780
  322.4 5.2 copy-start.26
  322.4 5.2 copy-start.18
  322.4 5.2 copy-start.32
  324.6 133.1 %reduce-scatter.13.cloned.1.call-start = ((), (), s32[]{:S(2)}) async-start(), calls=%async_computation.13 | async-start | bytes 1253376 | tf_op jit(solution)/shard_map/reduce_scatter | solution.py:350
  327.6 193.3 %reduce-scatter.9.cloned.1.call-start = ((), (), s32[]{:S(2)}) async-start(), calls=%async_computation.11 | async-start | bytes 1253376 | tf_op jit(solution)/shard_map/reduce_scatter | solution.py:338
  327.6 3.8 copy-start.3
  331.4 259.2 %reduce-scatter.15.cloned.1.call-start = ((), (), s32[]{:S(2)}) async-start(), calls=%async_computation.14 | async-start | bytes 5013504 | tf_op jit(solution)/shard_map/reduce_scatter | solution.py:274
  336.8 323.8 %reduce-scatter.17.cloned.1.call-start = ((), (), s32[]{:S(2)}) async-start(), calls=%async_computation.15 | async-start | bytes 5013504 | tf_op jit(solution)/shard_map/reduce_scatter | solution.py:280
  339.1 7.0 copy-start.38
  346.2 376.8 %reduce-scatter.11.cloned.1.call-start = ((), (), s32[]{:S(2)}) async-start(), calls=%async_computation.12 | async-start | bytes 208896 | tf_op jit(solution)/shard_map/reduce_scatter | solution.py:344
  346.3 41.4 %copy-start.7 = (bf16[768,768]{1,0:T(8,128)(2,1)S(1)}, bf16[768,768]{1,0:T(8,128)(2,1)}, u32[]{:S(2)}) copy-start(bf16[768,768]{1,0:T(8,128)(2,1)} %all-gather.8.cloned.1.call-done) | copy-start | bytes 3538948
  387.7 6.6 copy-start.20
  390.4 62.7 %copy-start.5 = (f32[256,768]{1,0:T(8,128)S(1)}, f32[256,768]{1,0:T(8,128)}, u32[]{:S(2)}) copy-start(f32[256,768]{1,0:T(8,128)} %copy-done.4) | copy-start | bytes 2359300
  393.2 5.8 copy-start.35
  393.2 5.9 copy-start.36
  393.2 5.9 copy-start.37
  393.2 5.9 copy-start.39
  393.2 5.9 copy-start.40
  393.2 5.9 copy-start.43
  393.2 5.9 copy-start.44
  393.2 59.9 %copy-start.24 = (f32[256]{0:T(256)S(1)}, f32[256]{0:T(256)}, u32[]{:S(2)}) copy-start(f32[256]{0:T(256)} %copy-done.23) | copy-start | bytes 3076
  396.1 264.5 %copy-start.30 = (f32[3072]{0:T(1024)S(1)}, f32[3072]{0:T(1024)}, u32[]{:S(2)}) copy-start(f32[3072]{0:T(1024)} %copy-done.29) | copy-start | bytes 36868
  396.1 264.5 %copy-start.34 = (f32[256]{0:T(256)S(1)}, f32[256]{0:T(256)}, u32[]{:S(2)}) copy-start(f32[256]{0:T(256)} %copy-done.33) | copy-start | bytes 3076
  396.1 264.5 %copy-start.42 = (f32[256]{0:T(256)S(1)}, f32[256]{0:T(256)}, u32[]{:S(2)}) copy-start(f32[256]{0:T(256)} %copy-done.41) | copy-start | bytes 3076
  396.1 264.5 %copy-start.47 = (f32[256]{0:T(256)S(1)}, f32[256]{0:T(256)}, u32[]{:S(2)}) copy-start(f32[256]{0:T(256)} %add_rsqrt_fusion) | copy-start | bytes 3076
  398.9 412.3 %all-reduce.25.cloned.1.call-start = ((), (), s32[]{:S(2)}) async-start(), calls=%async_computation.16 | async-start | bytes 1474560 | tf_op jit(solution)/shard_map/psum | solution.py:360
  (19 other events, 41.5 us)
Sparse Core Ops, SparseCore 0:
  9.7 35.2 all-gather.5
  46.7 32.7 all-gather.7
  81.3 38.9 all-gather.11
  121.9 38.4 all-gather.9
  324.7 69.5 reduce-scatter.6
  396.7 60.9 reduce-scatter.12
  460.2 60.6 reduce-scatter.8
  523.5 67.1 reduce-scatter.14
  593.2 67.3 reduce-scatter.16
  663.5 59.5 reduce-scatter.10
  725.8 85.3 all-reduce.24
where the time goes:
time: 829 us; the launch traced here: 824 us
  waiting for transfers between devices  306 us (37%)
  blocking collectives  205 us (25%)
  matrix products  172 us (21%)
  other arithmetic  63.1 us (8%)
  local copies, waits for them, and re-layouts  57.6 us (7%)
  between operations  19.3 us (2%)
    unnamed x2, blocking collectives  110 us
    reduce_scatter x1, waiting for transfers between devices, shards(): lax.psum_scatter(grad_down.astype(jnp.bfloat16), 'fsdp', scatter_dimensio...  69.9 us
    reduce_scatter x1, waiting for transfers between devices, shards(): lax.psum_scatter(grad_up.astype(jnp.bfloat16), 'fsdp', scatter_dimension=...  69.7 us
    dot_general x29, matrix products, inner_cols(): lax.dot_general(left, right, (((1,), (1,)), ((), ())), preferred_element_...  69.2 us
    reduce_scatter x1, waiting for transfers between devices, shards(): lax.psum_scatter(grad_queryw.astype(jnp.bfloat16), 'fsdp', scatter_dimens...  63.2 us
    reduce_scatter x1, waiting for transfers between devices, shards(): lax.psum_scatter(grad_keyvalw.astype(jnp.bfloat16), 'fsdp', scatter_dimen...  54.8 us
    psum x1, blocking collectives, shards(): lax.psum(attn_shares[0].astype(jnp.bfloat16), 'ctx').astype(jnp.float32)  41.5 us
    psum x1, waiting for transfers between devices, shards(): lax.psum(attn_shares[2].astype(jnp.bfloat16), 'ctx').astype(jnp.float32)  41.4 us
  transfers between devices with their start and end apart: 11, of which 7 were waited for; matrix products, arithmetic and copies ran while one was open for 20% of the time, Pallas kernels for 0%

commit v1 on v0

v1 whole, which is shorter than its diff:
```python
import functools

import jax
import jax.numpy as jnp
from jax import lax
from jax.experimental import pallas as pl
from jax.experimental.pallas import tpu as pltpu
from jax.sharding import PartitionSpec as P

EPS = 1e-05
NEG = -1e30
MESH = pl.DeviceIdType.MESH
F32 = jnp.float32
BF16 = jnp.bfloat16

WIDTH = 768
HEADS = 12
HD = 64
FF = 3072
HALF = FF // 2
BLK = 128
ROWS = 2 * BLK
GROUPS = HEADS // 2
PEERS = 8
N_A, N_B = 8, 7
ITEMS = N_A + N_B + 2
KEYS = ITEMS * BLK
SEMS = 224


def dot(left, right):
    return jnp.dot(left, right, preferred_element_type=F32)


def dot_nt(left, right):
    return lax.dot_general(left, right, (((1,), (1,)), ((), ())), preferred_element_type=F32)


def normalize(values):
    centre = values - jnp.mean(values, -1, keepdims=True)
    spread = jnp.mean(centre * centre, -1, keepdims=True)
    rate = lax.rsqrt(spread + EPS)
    return centre * rate, rate


def norm_back(normed, rate, grad, gain):
    scaled = grad * gain
    first = jnp.mean(scaled, -1, keepdims=True)
    second = jnp.mean(scaled * normed, -1, keepdims=True)
    return rate * (scaled - first - normed * second)


def layer_kernel(
    lengths,
    block_map,
    tokens,
    cotangent,
    vecs,
    wq,
    wkv,
    wo,
    wup,
    wdn,
    out_ref,
    ing_ref,
    gq_ref,
    go_ref,
    gt_ref,
    gup_ref,
    gdn_ref,
    f_vec,
    f_q,
    f_kv,
    f_o,
    f_up,
    r_up,
    f_dn,
    g_q,
    g_o,
    g_t,
    g_up,
    g_dn,
    rc_q,
    rc_o,
    rz_q,
    rz_o,
    rz_up,
    rz_dn,
    s_up,
    s_dn,
    ry_q,
    ry_o,
    ry_up,
    ry_dn,
    rx_up,
    rx_dn,
    rh_up,
    rh_dn,
    f2_up,
    f2_dn,
    r_t,
    c_q,
    c_o,
    c_t,
    kv_all,
    dkv_out,
    dkv_in,
    k_both,
    v_both,
    kt_both,
    vt_both,
    q_both,
    q_rows,
    probs,
    score,
    acc,
    o_norm,
    l_inv,
    att_t,
    do_both,
    do_rows,
    x_low,
    xn,
    xn_t,
    mixed_s,
    n2s,
    gos,
    mid,
    dup,
    part_out,
    part_in,
    dsec_own,
    dsec_out,
    dsec_in,
    send_sem,
    recv_sem,
    local_sem,
):
    ctx = lax.axis_index("ctx")
    fs = lax.axis_index("fsdp")
    zh, xx = ctx // 4, ctx % 4
    yy, zl, co = fs // 4, (fs // 2) % 2, fs % 2
    oz, oc = 1 - zl, 1 - co

    def peer(j):
        return ((zh + j // 4) % 2) * 4 + (xx + j % 4) % 4

    def from_peer(j):
        return ((zh + j // 4) % 2) * 4 + (xx + 4 - j % 4) % 4

    def shard_peer(k):
        return ((yy + k // 4) % 4) * 4 + ((zl + (k // 2) % 2) % 2) * 2 + (co + k % 2) % 2

    sib = (ctx, fs + 1 - 2 * co)
    z_near = (ctx, fs + 2 - 4 * zl)
    z_far = (ctx + 4 - 8 * zh, fs + 2 - 4 * zl)
    z_of = (z_near, z_far)

    def y_peer(k):
        return (ctx, ((yy + k) % 4) * 4 + zl * 2 + co)

    def x_peer(k):
        return (zh * 4 + (xx + k) % 4, fs)

    h_peer = (ctx + 4 - 8 * zh, fs)

    count = [0]
    started = []

    def send(src, dst, to):
        i = count[0]
        count[0] += 1
        copy = pltpu.make_async_remote_copy(
            src_ref=src,
            dst_ref=dst,
            send_sem=send_sem.at[i],
            recv_sem=recv_sem.at[i],
            device_id=to,
            device_id_type=MESH,
        )
        copy.start()
        started.append(copy)
        return copy

    def arrived(copies):
        for copy in copies:
            copy.wait_recv()

    locals_ = []

    def keep(src, dst):
        i = len(locals_)
        copy = pltpu.make_async_copy(src, dst, local_sem.at[i])
        copy.start()
        locals_.append(copy)
        return copy

    barrier = pltpu.get_barrier_semaphore()
    greeted = [(peer(j), fs) for j in range(1, PEERS)]
    greeted += [(ctx, shard_peer(k)) for k in range(1, 16)]
    greeted += [z_far]
    for device in greeted:
        pl.semaphore_signal(barrier, inc=1, device_id=device, device_id_type=MESH)
    pl.semaphore_wait(barrier, len(greeted))

    def gather_y(src, full):
        out = [send(src, full.at[yy, zl, co], y_peer(k)) for k in (1, 2, 3)]
        return out, keep(src, full.at[yy, zl, co])

    def gather_z(full):
        return [
            send(
                full.at[pl.ds(2 * e, 2), zl, co], full.at[pl.ds(2 * e, 2), zl, co], z_of[e]
            )
            for e in (0, 1)
        ]

    attn = ((vecs, f_vec), (wkv, f_kv), (wq, f_q), (wo, f_o))
    step_y = [gather_y(src, full) for src, full in attn]

    slot0, slot1 = block_map[2 * ctx], block_map[2 * ctx + 1]
    low = jnp.minimum(slot0, slot1)
    swap = slot0 > slot1
    length = lengths[0]

    t0, t1 = tokens[0], tokens[1]
    x_low[0:BLK] = jnp.where(swap, t1, t0)
    x_low[BLK:ROWS] = jnp.where(swap, t0, t1)

    row = lax.broadcasted_iota(jnp.int32, (ROWS, 1), 0)
    pos = jnp.where(row < BLK, low * BLK, (14 - low) * BLK) + row
    valid = (pos < length).astype(F32)

    def grad_out():
        c0, c1 = cotangent[0], cotangent[1]
        both = jnp.concatenate([jnp.where(swap, c1, c0), jnp.where(swap, c0, c1)], 0)
        return valid * both

    gos[0] = grad_out().astype(BF16)
    go_copy = send(gos.at[0], gos.at[1], sib)

    def gather_c(full, z):
        return send(full.at[:, z, co], full.at[:, z, co], sib)

    step_z, step_c = [], []
    for (_, full), (copies, own) in zip(attn, step_y):
        arrived(copies)
        own.wait()
        step_z.append(gather_z(full))
        step_c.append(gather_c(full, zl))

    def mine(c):
        return pl.ds(pl.multiple_of(c * HALF, HALF), HALF)

    def up_y():
        out = [send(wup.at[:, mine(co)], f_up.at[yy, zl, co], y_peer(k)) for k in (1, 2, 3)]
        out += [send(wup.at[:, mine(oc)], r_up.at[yy, zl], y_peer(k)) for k in (1, 2, 3)]
        return out, [keep(wup.at[:, mine(co)], f_up.at[yy, zl, co]), keep(wup.at[:, mine(oc)], r_up.at[yy, zl])]

    def up_z():
        out = []
        for e in (0, 1):
            part_y = pl.ds(2 * e, 2)
            out.append(send(f_up.at[part_y, zl, co], f_up.at[part_y, zl, co], z_of[e]))
            out.append(send(r_up.at[part_y, zl], r_up.at[part_y, zl], z_of[e]))
        return out

    def dn_slot(y, z):
        other = y // 2 + co - 2 * (y // 2) * co
        return (1 - other) * ((y % 2) * 4 + z * 2 + co) + other * (8 + (y % 2) * 2 + z)

    def dn_y():
        dst = f_dn.at[dn_slot(yy, zl)]
        return [send(wdn, dst, y_peer(k)) for k in (1, 2, 3)], [keep(wdn, dst)]

    def dn_z():
        return [
            send(f_dn.at[dn_slot(y, zl)], f_dn.at[dn_slot(y, zl)], z_of[y // 2]) for y in range(4)
        ]

    y_up, own_up = up_y()
    y_dn, own_dn = dn_y()

    for i, (_, full) in enumerate(attn):
        arrived(step_z[i])
        step_c.append(gather_c(full, oz))

    def up_c(z):
        return [send(r_up.at[:, z], f_up.at[:, z, co], sib)]

    def dn_c(z):
        return [send(f_dn.at[8 + y * 2 + z], f_dn.at[y * 4 + z * 2 + co], sib) for y in (0, 1)]

    arrived([step_c[0], step_c[4]])
    vec = f_vec[...].astype(F32).reshape(16, 16, WIDTH)
    vec = jnp.sum(vec, 0)
    gain1, shift1, qbias, obias = vec[0:1], vec[1:2], vec[2:3], vec[3:4]
    gain2, shift2, dbias, kvbias = vec[4:5], vec[5:6], vec[6:7], vec[7:8, 0 : 2 * HD]

    n1, _ = normalize(x_low[...].astype(F32))
    xn_v = n1 * gain1 + shift1
    xn[...] = xn_v.astype(BF16)
    xn_t[...] = xn_v.T.astype(BF16)

    arrived([step_c[1], step_c[5]])
    kv = dot(xn[...], f_kv[...].reshape(WIDTH, 2 * HD)) + kvbias
    kv_all[0] = kv.astype(BF16)
    kv_copies = [send(kv_all.at[0], kv_all.at[j], (peer(j), fs)) for j in range(1, PEERS)]

    arrived(y_up)
    for copy in own_up:
        copy.wait()
    z_up = up_z()
    c_up = up_c(zl)
    arrived(y_dn)
    for copy in own_dn:
        copy.wait()
    z_dn = dn_z()
    c_dn = dn_c(zl)

    arrived([step_c[2], step_c[6]])
    q = dot(xn[...], f_q[...].reshape(WIDTH, WIDTH)) + qbias
    q = (q.astype(BF16).astype(F32) * (HD**-0.5)).T
    for g in range(GROUPS):
        h0, h1 = q[g * BLK : g * BLK + HD], q[g * BLK + HD : (g + 1) * BLK]
        both = jnp.concatenate(
            [
                jnp.concatenate([h0[:, BLK:], h1[:, BLK:]], 1),
                jnp.concatenate([h0[:, :BLK], h1[:, :BLK]], 1),
            ],
            0,
        )
        q_both[g] = both.astype(BF16)
        q_rows[g] = both.T.astype(BF16)

    arrived(kv_copies)
    lane = lax.broadcasted_iota(jnp.int32, (BLK, BLK), 1)
    sub = lax.broadcasted_iota(jnp.int32, (BLK, BLK), 0)
    extra = lax.broadcasted_iota(jnp.int32, (16, BLK), 0)

    picks, limits = [], []
    for j in range(1, PEERS):
        c = from_peer(j)
        other = jnp.minimum(block_map[2 * c], block_map[2 * c + 1])
        high = other > low
        picks.append(jnp.where(high, 1.0, 0.0).astype(F32))
        limits.append(length - jnp.where(high, 15 - other, other) * BLK)

    def place(item, block, to_high):
        rows = pl.ds(item * BLK, BLK)
        left = jnp.where(lane < HD, to_high, 1.0 - to_high)
        kk = jnp.concatenate([block[:, :HD], block[:, :HD]], 1) * left
        vv = jnp.concatenate([block[:, HD:], block[:, HD:]], 1) * left
        k_both[rows] = kk.astype(BF16)
        v_both[rows] = vv.astype(BF16)
        kt_both[:, rows] = kk.T.astype(BF16)
        vt_both[0:BLK, rows] = vv.T.astype(BF16)
        vt_both[BLK : BLK + 16, rows] = jnp.where(extra < 8, to_high, 1.0 - to_high).astype(BF16)

    one, zero = jnp.float32(1.0), jnp.float32(0.0)
    for j in range(PEERS):
        block = kv_all[j].astype(F32)
        place(j, block[:BLK], one)
        if j:
            pick = picks[j - 1]
            place(N_A + j - 1, jnp.where(pick > 0.5, block[BLK:], block[:BLK]), pick)
        else:
            place(N_A + N_B, block[BLK:], one)
            place(N_A + N_B + 1, block[:BLK], zero)

    sub2 = lax.broadcasted_iota(jnp.int32, (BLK, ROWS), 0)
    lane2 = lax.broadcasted_iota(jnp.int32, (BLK, ROWS), 1) % BLK

    def fold(values, op):
        return op(values.reshape(BLK // 8, 8, ROWS), 0)

    def forward_group(g, carry):
        score[...] = dot(k_both[...], q_both[g])
        top_h = jnp.full((8, ROWS), NEG, F32)
        top_l = jnp.full((8, ROWS), NEG, F32)
        for item in range(ITEMS):
            rows = slice(item * BLK, (item + 1) * BLK)
            s = score[rows]
            if item < N_A:
                top_h = jnp.maximum(top_h, fold(s, jnp.max))
            elif item < N_A + N_B:
                j = item - N_A
                s = jnp.where(sub2 < limits[j], s, NEG)
                score[rows] = s
                best = fold(s, jnp.max)
                top_h = jnp.maximum(top_h, jnp.where(picks[j] > 0.5, best, NEG))
                top_l = jnp.maximum(top_l, jnp.where(picks[j] > 0.5, NEG, best))
            elif item == N_A + N_B:
                limit = length - (15 - low) * BLK
                s = jnp.where((sub2 <= lane2) & (sub2 < limit), s, NEG)
                score[rows] = s
                top_h = jnp.maximum(top_h, fold(s, jnp.max))
            else:
                s = jnp.where(sub2 <= lane2, s, NEG)
                score[rows] = s
                top_l = jnp.maximum(top_l, fold(s, jnp.max))
        top_h = jnp.max(top_h, 0, keepdims=True)
        top_l = jnp.max(top_l, 0, keepdims=True)
        for item in range(ITEMS):
            rows = slice(item * BLK, (item + 1) * BLK)
            if item < N_A or item == N_A + N_B:
                top = top_h
            elif item < N_A + N_B:
                top = jnp.where(picks[item - N_A] > 0.5, top_h, top_l)
            else:
                top = top_l
            probs[g, rows] = jnp.exp(score[rows] - top).astype(BF16)
        o = dot(vt_both[...], probs[g])
        inv_h = 1.0 / o[BLK : BLK + 1]
        inv_l = 1.0 / o[BLK + 8 : BLK + 9]
        high, lower = o[0:HD] * inv_h, o[HD:BLK] * inv_l
        o_norm[g, 0:HD] = high
        o_norm[g, HD:BLK] = lower
        l_inv[g, 0:8] = jnp.broadcast_to(inv_h, (8, ROWS))
        l_inv[g, 8:16] = jnp.broadcast_to(inv_l, (8, ROWS))
        att_t[g, 0:HD, 0:BLK] = lower[:, :BLK].astype(BF16)
        att_t[g, 0:HD, BLK:ROWS] = high[:, :BLK].astype(BF16)
        att_t[g, HD:BLK, 0:BLK] = lower[:, BLK:].astype(BF16)
        att_t[g, HD:BLK, BLK:ROWS] = high[:, BLK:].astype(BF16)
        return carry

    lax.fori_loop(0, GROUPS // 2, forward_group, 0)
    arrived(z_up)
    c_up += up_c(oz)
    arrived(z_dn)
    c_dn += dn_c(oz)
    lax.fori_loop(GROUPS // 2, GROUPS, forward_group, 0)

    arrived([step_c[3], step_c[7]])
    attended = att_t[...].reshape(WIDTH, ROWS).astype(F32).T.astype(BF16)
    mixed = x_low[...].astype(F32) + dot(attended, f_o[...].reshape(WIDTH, WIDTH)) + obias
    mixed_s[...] = mixed
    n2, _ = normalize(mixed)
    n2s[0] = (n2 * gain2 + shift2).astype(BF16)
    n2_copy = send(n2s.at[0], n2s.at[1], sib)

    arrived([go_copy] + c_up + c_dn + [n2_copy])
    sub_cols = 256
    n_sub = HALF // sub_cols
    coef = 0.7978845608028654

    up_sums = []
    for s in range(n_sub):
        cols = slice(s * sub_cols, (s + 1) * sub_cols)
        per = WIDTH // sub_cols
        bias_row = jnp.where(co == 0, vec[8 + s // per : 9 + s // per], vec[10 + s // per : 11 + s // per])
        bias = bias_row[:, (s % per) * sub_cols : (s % per + 1) * sub_cols]
        n2b = n2s[...].reshape(2 * ROWS, WIDTH)
        gob = gos[...].reshape(2 * ROWS, WIDTH)
        up = dot(n2b, f_up[:, :, :, :, cols].reshape(WIDTH, sub_cols)) + bias
        w_rows = f_dn[4 * (s // per) : 4 * (s // per) + 4].reshape(WIDTH, WIDTH)
        w_rows = w_rows[(s % per) * sub_cols : (s % per + 1) * sub_cols]
        dmid = dot_nt(gob, w_rows)
        square = up * up
        th = jnp.tanh(coef * up * (1.0 + 0.044715 * square))
        half_sum = 0.5 + 0.5 * th
        mid[:, cols] = (up * half_sum).astype(BF16)
        slope = half_sum + 0.5 * up * (1.0 - th * th) * coef * (1.0 + 3 * 0.044715 * square)
        du = (dmid * slope).astype(BF16)
        dup[:, cols] = du
        up_sums.append(jnp.sum(du.astype(F32), 0, keepdims=True))

    thirds = [slice(256 * n, 256 * (n + 1)) for n in range(3)]
    for n in thirds:
        w = f_up[...].reshape(WIDTH, HALF)[n]
        piece = dot_nt(dup[...], w)
        dsec_own[:, n] = piece[:ROWS]
        dsec_out[:, n] = piece[ROWS:].astype(BF16)
    dsec_copy = send(dsec_out, dsec_in, sib)

    z_dn = []
    for j in (0, 1):
        m_t = mid[:, j * WIDTH : (j + 1) * WIDTH].astype(F32).T.astype(BF16)
        for n in thirds:
            piece = dot(m_t, gos[:, :, n].reshape(2 * ROWS, 256))
            g_dn[j, :, :, :, n] = piece.astype(BF16).reshape(2, 2, 192, 256)
        z_dn.append(send(g_dn.at[j, oz], rz_dn.at[j], z_of[j]))
    n2_t = n2s[...].reshape(2 * ROWS, WIDTH).astype(F32).T.astype(BF16)
    for s in range(n_sub):
        cols = slice(s * sub_cols, (s + 1) * sub_cols)
        piece = dot(n2_t, dup[:, cols])
        g_up[:, :, :, :, cols] = piece.astype(BF16).reshape(4, 2, 2, 48, sub_cols)
    z_up = [send(g_up.at[pl.ds(2 * e, 2), oz], rz_up.at[pl.ds(2 * e, 2)], z_of[e]) for e in (0, 1)]

    arrived([dsec_copy])
    dsec = dsec_own[...] + dsec_in[...].astype(F32)
    n2, rate2 = normalize(mixed_s[...])
    sum_gain2 = jnp.sum(dsec * n2, 0, keepdims=True)
    sum_shift2 = jnp.sum(dsec, 0, keepdims=True)
    dmix = grad_out() + norm_back(n2, rate2, dsec, gain2)
    ing_ref[0] = dmix[:BLK]
    ing_ref[1] = dmix[BLK:]
    dmix_low = dmix.astype(BF16)
    dmix_r = dmix_low.astype(F32)
    sum_obias = jnp.sum(dmix_r, 0, keepdims=True)
    sum_dbias = jnp.sum(gos[0].astype(F32), 0, keepdims=True)

    g_o[...] = (
        dot(att_t[...].reshape(WIDTH, ROWS), dmix_low).astype(BF16).reshape(4, 2, 2, 48, WIDTH)
    )
    c_go = send(g_o.at[:, :, oc], rc_o, sib)

    for n in thirds:
        piece = dot(mid[...], f_dn[0:8, :, n].reshape(HALF, 256))
        dsec_own[:, n] = piece[:ROWS]
        part_out[:, n] = piece[ROWS:].astype(BF16)
    part_copy = send(part_out, part_in, sib)

    datt = dot(f_o[...].reshape(WIDTH, WIDTH), dmix_r.T.astype(BF16)).astype(BF16).astype(F32)
    deltas = []
    for g in range(GROUPS):
        h0, h1 = datt[g * BLK : g * BLK + HD], datt[g * BLK + HD : (g + 1) * BLK]
        high = jnp.concatenate([h0[:, BLK:], h1[:, BLK:]], 1) * l_inv[g, 0:1]
        lower = jnp.concatenate([h0[:, :BLK], h1[:, :BLK]], 1) * l_inv[g, 8:9]
        both = jnp.concatenate([high, lower], 0)
        do_both[g] = both.astype(BF16)
        do_rows[g] = both.T.astype(BF16)
        both = both.astype(BF16).astype(F32) * o_norm[g]
        l_inv[g, 0:8] = jnp.broadcast_to(jnp.sum(both[:HD], 0, keepdims=True), (8, ROWS))
        l_inv[g, 8:16] = jnp.broadcast_to(jnp.sum(both[HD:], 0, keepdims=True), (8, ROWS))

    def dn_after_z():
        for j in (0, 1):
            arrived([z_dn[j]])
            total = g_dn[j, zl].astype(F32) + rz_dn[j].astype(F32)
            g_dn[j, zl] = total.astype(BF16)
        copies = []
        for j in (0, 1):
            copies.append(send(g_dn.at[j, zl, oc], s_dn.at[2 * co + j], sib))
            s_dn[2 * co + j] = g_dn[j, zl, co]
        return copies

    def up_after_z():
        copies = []
        for e in (0, 1):
            arrived([z_up[e]])
            part_y = pl.ds(2 * e, 2)
            total = g_up[part_y, zl].astype(F32) + rz_up[part_y].astype(F32)
            g_up[part_y, zl] = total.astype(BF16)
            copies.append(send(g_up.at[part_y, zl, oc], s_up.at[part_y, :, mine(co)], sib))
            s_up[part_y, :, mine(co)] = g_up[part_y, zl, co]
        return copies

    def y_sends(src, dst):
        return [send(src.at[(yy + k) % 4], dst.at[k - 1], y_peer(k)) for k in (1, 2, 3)]

    acc[...] = jnp.zeros_like(acc)

    def backward_group(g, carry):
        acc[:, BLK:ROWS] += dot(probs[g], do_rows[g])
        delta_h, delta_l = l_inv[g, 0:1], l_inv[g, 8:9]
        score[...] = dot(v_both[...], do_both[g])
        for item in range(ITEMS):
            rows = slice(item * BLK, (item + 1) * BLK)
            if item < N_A or item == N_A + N_B:
                delta = delta_h
            elif item < N_A + N_B:
                delta = jnp.where(picks[item - N_A] > 0.5, delta_h, delta_l)
            else:
                delta = delta_l
            probs[g, rows] = (probs[g, rows].astype(F32) * (score[rows] - delta)).astype(BF16)
        dq = dot(kt_both[...], probs[g]) * (HD**-0.5)
        do_both[g, 0:HD, 0:BLK] = dq[HD:, :BLK].astype(BF16)
        do_both[g, 0:HD, BLK:ROWS] = dq[:HD, :BLK].astype(BF16)
        do_both[g, HD:BLK, 0:BLK] = dq[HD:, BLK:].astype(BF16)
        do_both[g, HD:BLK, BLK:ROWS] = dq[:HD, BLK:].astype(BF16)
        acc[:, 0:BLK] += dot(probs[g], q_rows[g])
        return carry

    lax.fori_loop(0, 2, backward_group, 0)

    c_dn = dn_after_z()
    c_up = up_after_z()
    arrived([c_go])
    g_o[:, :, co] = (g_o[:, :, co].astype(F32) + rc_o[...].astype(F32)).astype(BF16)

    def z_sends(grad, dst):
        return [
            send(grad.at[pl.ds(2 * e, 2), oz, co], dst.at[pl.ds(2 * e, 2)], z_of[e]) for e in (0, 1)
        ]

    z_o = z_sends(g_o, rz_o)
    lax.fori_loop(2, 4, backward_group, 0)

    arrived(c_dn)
    y_dn = y_sends(s_dn, ry_dn)
    arrived(c_up)
    y_up = y_sends(s_up, ry_up)

    def after_z(copies, grad, got):
        arrived(copies)
        grad[:, zl, co] = (grad[:, zl, co].astype(F32) + got[...].astype(F32)).astype(BF16)
        return [
            send(grad.at[(yy + k) % 4, zl, co], ry.at[k - 1], y_peer(k))
            for ry in [{id(rz_o): ry_o, id(rz_q): ry_q}[id(got)]]
            for k in (1, 2, 3)
        ]

    y_o = after_z(z_o, g_o, rz_o)
    lax.fori_loop(4, 6, backward_group, 0)

    def halves(item, second):
        rows = slice(item * BLK, (item + 1) * BLK)
        at = HD if second else 0
        return jnp.concatenate(
            [acc[rows, at : at + HD], acc[rows, BLK + at : BLK + at + HD]], 1
        )

    dkv_copies = []
    for j in range(1, PEERS):
        item = N_A + j - 1
        pick = picks[j - 1]
        other = jnp.where(pick > 0.5, halves(item, False), halves(item, True))
        dkv_out[j, 0:BLK] = (halves(j, False) + (1.0 - pick) * other).astype(BF16)
        dkv_out[j, BLK:ROWS] = (pick * other).astype(BF16)
        dkv_copies.append(send(dkv_out.at[j], dkv_in.at[j], (from_peer(j), fs)))

    dq = do_both[...].reshape(WIDTH, ROWS).astype(F32).T
    sum_qbias = jnp.sum(dq, 0, keepdims=True)
    dq = dq.astype(BF16)
    g_q[...] = dot(xn_t[...], dq).astype(BF16).reshape(4, 2, 2, 48, WIDTH)
    c_gq = send(g_q.at[:, :, oc], rc_q, sib)
    dfirst = dot_nt(dq, f_q[...].reshape(WIDTH, WIDTH))

    def y_sum(own, got):
        total = own.astype(F32)
        for k in range(3):
            total = total + got[k].astype(F32)
        return total

    arrived(y_dn)
    s_dn[yy] = y_sum(s_dn[yy], ry_dn).astype(BF16)
    arrived(y_up)
    s_up[yy] = y_sum(s_up[yy], ry_up).astype(BF16)

    def quarter_dn(k):
        return pl.ds(pl.multiple_of(k * 48, 16), 48)

    def quarter_up(k):
        return pl.ds(pl.multiple_of(k * WIDTH, WIDTH), WIDTH)

    x_dn, x_up = [], []
    for k in (1, 2, 3):
        q4 = (xx + k) % 4
        x_dn.append(send(s_dn.at[yy, quarter_dn(q4)], rx_dn.at[k - 1], x_peer(k)))
        x_up.append(send(s_up.at[yy, :, quarter_up(q4)], rx_up.at[k - 1], x_peer(k)))

    arrived(y_o)
    g_o[yy, zl, co] = y_sum(g_o[yy, zl, co], ry_o).astype(BF16)

    def ctx_sends(src, dst):
        return [send(src, dst.at[j], (peer(j), fs)) for j in range(1, PEERS)]

    ctx_o = ctx_sends(g_o.at[yy, zl, co], c_o)

    arrived([c_gq])
    g_q[:, :, co] = (g_q[:, :, co].astype(F32) + rc_q[...].astype(F32)).astype(BF16)
    z_q = z_sends(g_q, rz_q)

    top = halves(0, False) + halves(N_A + N_B + 1, True)
    dkv = jnp.concatenate([top, halves(N_A + N_B, False)], 0)
    arrived(dkv_copies)
    for j in range(1, PEERS):
        dkv = dkv + dkv_in[j].astype(F32)
    dkv = dkv.astype(BF16)
    sum_kv = jnp.sum(dkv.astype(F32), 0, keepdims=True)
    g_kv = dot(xn_t[...], dkv)
    dfirst = dfirst + dot_nt(dkv, f_kv[...].reshape(WIDTH, 2 * HD))

    n1, rate1 = normalize(x_low[...].astype(F32))
    sum_gain1 = jnp.sum(dfirst * n1, 0, keepdims=True)
    sum_shift1 = jnp.sum(dfirst, 0, keepdims=True)

    zeros = jnp.zeros((1, WIDTH), F32)
    columns = jnp.concatenate(
        [zeros] * 4
        + [sum_dbias, sum_gain2, sum_shift2, sum_obias, sum_gain1, sum_shift1, sum_qbias]
        + [jnp.zeros((BLK - 11, WIDTH), F32)],
        0,
    ).T
    lanes = lax.broadcasted_iota(jnp.int32, (WIDTH, BLK), 1)
    columns = jnp.where(lanes < HD, columns, sum_kv)
    g_t[:, :, :, :, 0:BLK] = g_kv.astype(BF16).reshape(4, 2, 2, 48, BLK)
    g_t[:, :, :, :, BLK:ROWS] = columns.astype(BF16).reshape(4, 2, 2, 48, BLK)
    lanes = lax.broadcasted_iota(jnp.int32, (48, BLK), 1)
    for j in (0, 1):
        sums = jnp.concatenate(up_sums[3 * j : 3 * j + 3], 1)
        sums = jnp.broadcast_to(sums, (BLK, WIDTH)).T
        for k in range(4):
            block = g_t[2 * co + j, k // 2, k % 2, :, BLK:ROWS].astype(F32)
            for r in range(4):
                at = k * 192 + r * 48
                block = jnp.where(lanes == r, sums[at : at + 48], block)
            g_t[2 * co + j, k // 2, k % 2, :, BLK:ROWS] = block.astype(BF16)

    t_copies = []
    for k in range(1, 16):
        dst = shard_peer(k)
        t_copies.append(
            send(g_t.at[dst // 4, (dst // 2) % 2, dst % 2], r_t.at[k], (ctx, dst))
        )

    y_q = after_z(z_q, g_q, rz_q)

    ing = ing_ref[...].reshape(ROWS, WIDTH) + norm_back(n1, rate1, dfirst, gain1)
    ing_ref[0] = jnp.where(swap, ing[BLK:], ing[:BLK])
    ing_ref[1] = jnp.where(swap, ing[:BLK], ing[BLK:])
    arrived([part_copy])
    res = valid * (mixed_s[...] + dsec_own[...] + part_in[...].astype(F32) + dbias)
    out_ref[0] = jnp.where(swap, res[BLK:], res[:BLK]).astype(BF16)
    out_ref[1] = jnp.where(swap, res[:BLK], res[BLK:]).astype(BF16)

    h_out = []
    arrived(x_dn)
    rh_dn[1] = y_sum(s_dn[yy, quarter_dn(xx)], rx_dn).astype(BF16)
    h_out.append(send(rh_dn.at[1], rh_dn.at[0], h_peer))
    arrived(x_up)
    rh_up[1] = y_sum(s_up[yy, :, quarter_up(xx)], rx_up).astype(BF16)
    h_out.append(send(rh_up.at[1], rh_up.at[0], h_peer))

    arrived(t_copies)
    total = g_t[yy, zl, co].astype(F32)
    for k in range(1, 16):
        total = total + r_t[k].astype(F32)
    c_t[0] = total.astype(BF16)
    ctx_t = ctx_sends(c_t.at[0], c_t)

    arrived(y_q)
    g_q[yy, zl, co] = y_sum(g_q[yy, zl, co], ry_q).astype(BF16)
    ctx_q = ctx_sends(g_q.at[yy, zl, co], c_q)

    arrived([h_out[0]])
    f2_dn[xx] = (rh_dn[0].astype(F32) + rh_dn[1].astype(F32)).astype(BF16)
    a_dn = [send(f2_dn.at[xx], f2_dn.at[xx], x_peer(k)) for k in (1, 2, 3)]
    arrived([h_out[1]])
    f2_up[xx] = (rh_up[0].astype(F32) + rh_up[1].astype(F32)).astype(BF16)
    a_up = [send(f2_up.at[xx], f2_up.at[xx], x_peer(k)) for k in (1, 2, 3)]

    def ctx_sum(copies, own, got):
        arrived(copies)
        total = own.astype(F32)
        for j in range(1, PEERS):
            total = total + got[j].astype(F32)
        return total

    go_ref[...] = ctx_sum(ctx_o, g_o[yy, zl, co], c_o)
    gt_ref[...] = ctx_sum(ctx_t, c_t[0], c_t)
    gq_ref[...] = ctx_sum(ctx_q, g_q[yy, zl, co], c_q)
    arrived(a_dn)
    gdn_ref[...] = f2_dn[...].astype(F32).reshape(192, WIDTH)
    arrived(a_up)
    for k in range(4):
        gup_ref[:, k * WIDTH : (k + 1) * WIDTH] = f2_up[k].astype(F32)

    for copy in started:
        copy.wait_send()


def expand(values, at, fs):
    first = jnp.zeros((16, WIDTH), BF16)
    for row, value in enumerate(values):
        first = lax.dynamic_update_slice(first, value[None], (row, fs * 48))
    value_bias, up_bias = at
    first = lax.dynamic_update_slice(first, value_bias[None], (7, HD + fs * 4))
    return lax.dynamic_update_slice(first, up_bias[None], (8 + fs // 4, (fs % 4) * 192))


def shards(
    tokens,
    lengths,
    block_map,
    first_gain,
    first_shift,
    query_weight,
    query_bias,
    keyval_weight,
    value_bias,
    output_weight,
    output_bias,
    second_gain,
    second_shift,
    up_weight,
    up_bias,
    down_weight,
    down_bias,
    cotangent,
):
    fs = lax.axis_index("fsdp")
    vecs = expand(
        (first_gain, first_shift, query_bias, output_bias, second_gain, second_shift, down_bias),
        (value_bias, up_bias),
        fs,
    )
    vmem = pl.BlockSpec(memory_space=pltpu.VMEM)
    smem = pl.BlockSpec(memory_space=pltpu.SMEM)
    hbm = pl.BlockSpec(memory_space=pl.ANY)

    def v(*shape, dtype=BF16):
        return pltpu.VMEM(shape, dtype)

    scratch = [
        v(4, 2, 2, 16, WIDTH),
        v(4, 2, 2, 48, WIDTH),
        v(4, 2, 2, 48, 2 * HD),
        v(4, 2, 2, 48, WIDTH),
        v(4, 2, 2, 48, HALF),
        v(4, 2, 48, HALF),
        v(12, 192, WIDTH),
        v(4, 2, 2, 48, WIDTH),
        v(4, 2, 2, 48, WIDTH),
        v(4, 2, 2, 48, 2 * BLK),
        v(4, 2, 2, 48, HALF),
        v(2, 2, 2, 192, WIDTH),
        v(4, 2, 48, WIDTH),
        v(4, 2, 48, WIDTH),
        v(4, 48, WIDTH),
        v(4, 48, WIDTH),
        v(4, 2, 48, HALF),
        v(2, 2, 192, WIDTH),
        v(4, 48, FF),
        v(4, 192, WIDTH),
        v(3, 48, WIDTH),
        v(3, 48, WIDTH),
        v(3, 48, FF),
        v(3, 192, WIDTH),
        v(3, 48, WIDTH),
        v(3, 48, WIDTH),
        v(2, 48, WIDTH),
        v(2, 48, WIDTH),
        v(4, 48, WIDTH),
        v(4, 48, WIDTH),
        v(16, 48, 2 * BLK),
        v(PEERS, 48, WIDTH),
        v(PEERS, 48, WIDTH),
        v(PEERS, 48, 2 * BLK),
        v(PEERS, ROWS, 2 * HD),
        v(PEERS, ROWS, 2 * HD),
        v(PEERS, ROWS, 2 * HD),
        v(KEYS, BLK),
        v(KEYS, BLK),
        v(BLK, KEYS),
        v(BLK + 16, KEYS),
        v(GROUPS, BLK, ROWS),
        v(GROUPS, ROWS, BLK),
        v(GROUPS, KEYS, ROWS),
        v(KEYS, ROWS, dtype=F32),
        v(KEYS, ROWS, dtype=F32),
        v(GROUPS, BLK, ROWS, dtype=F32),
        v(GROUPS, 16, ROWS, dtype=F32),
        v(GROUPS, BLK, ROWS),
        v(GROUPS, BLK, ROWS),
        v(GROUPS, ROWS, BLK),
        v(ROWS, WIDTH),
        v(ROWS, WIDTH),
        v(WIDTH, ROWS),
        v(ROWS, WIDTH, dtype=F32),
        v(2, ROWS, WIDTH),
        v(2, ROWS, WIDTH),
        v(2 * ROWS, HALF),
        v(2 * ROWS, HALF),
        v(ROWS, WIDTH),
        v(ROWS, WIDTH),
        v(ROWS, WIDTH, dtype=F32),
        v(ROWS, WIDTH),
        v(ROWS, WIDTH),
        pltpu.SemaphoreType.DMA((SEMS,)),
        pltpu.SemaphoreType.DMA((SEMS,)),
        pltpu.SemaphoreType.DMA((16,)),
    ]
    outs = pl.pallas_call(
        layer_kernel,
        out_shape=(
            jax.ShapeDtypeStruct((2, BLK, WIDTH), BF16),
            jax.ShapeDtypeStruct((2, BLK, WIDTH), F32),
            jax.ShapeDtypeStruct((48, WIDTH), F32),
            jax.ShapeDtypeStruct((48, WIDTH), F32),
            jax.ShapeDtypeStruct((48, 2 * BLK), F32),
            jax.ShapeDtypeStruct((48, FF), F32),
            jax.ShapeDtypeStruct((192, WIDTH), F32),
        ),
        in_specs=[smem, smem, vmem, vmem] + [hbm] * 6,
        out_specs=(vmem,) * 7,
        scratch_shapes=scratch,
        compiler_params=pltpu.CompilerParams(
            collective_id=0, has_side_effects=True, vmem_limit_bytes=62 * 2**20
        ),
    )(
        lengths,
        block_map,
        tokens[0],
        cotangent[0],
        vecs,
        query_weight,
        keyval_weight,
        output_weight,
        up_weight,
        down_weight,
    )
    layer_out, input_grad, g_query, g_output, g_tail, g_up, g_down = outs
    g_keyval = g_tail[:, : 2 * HD]

    def column(k):
        return g_tail[:, BLK + k]

    g_value_bias = lax.dynamic_slice(g_tail[0], (BLK + HD + fs * 4,), (4,))
    g_up_bias = g_tail[:, BLK : BLK + 4].T.reshape(192)
    return (
        layer_out[None],
        input_grad[None],
        column(8),
        column(9),
        g_query,
        column(10),
        g_keyval,
        g_value_bias,
        g_output,
        column(7),
        column(5),
        column(6),
        g_up,
        g_up_bias,
        g_down,
        column(4),
    )


def solution(mesh):
    rows, matrix, batch = P("fsdp"), P("fsdp", None), P("fsdp", "ctx", None, None)
    return jax.shard_map(
        shards,
        mesh=mesh,
        in_specs=(
            batch,
            rows,
            P(),
            rows,
            rows,
            matrix,
            rows,
            matrix,
            rows,
            matrix,
            rows,
            rows,
            rows,
            matrix,
            rows,
            matrix,
            rows,
            batch,
        ),
        out_specs=(
            batch,
            batch,
            rows,
            rows,
            matrix,
            rows,
            matrix,
            rows,
            matrix,
            rows,
            rows,
            rows,
            matrix,
            rows,
            matrix,
            rows,
        ),
        check_vma=False,
    )
```

time: 829 us -> 194 us (0.23)
  waiting for transfers between devices: 306 us -> 0 us
  blocking collectives: 205 us -> 0 us
  Pallas kernels: 0 us -> 175 us
  matrix products: 172 us -> 0 us
  other arithmetic: 63.1 us -> 0 us
  local copies, waits for them, and re-layouts: 57.6 us -> 17.7 us
  between operations: 19.3 us -> 1.45 us
    reduce_scatter x6 -> x0, waiting for transfers between devices: 262 us -> none  [the longest x1 69.9 us: shards(): lax.psum_scatter(grad_down.astype(jnp.bfloat16), 'fsdp', scatter_dimensio...]
    pallas_call x0 -> x1, Pallas kernels: none -> 175 us  [shards(): pl.pallas_call(layer_kernel, out_shape=(jax.ShapeDtypeStruct((2, BLK, WID...]
    dot_general x70 -> x0, matrix products: 172 us -> none  [the longest x29 69.2 us: inner_cols(): lax.dot_general(left, right, (((1,), (1,)), ((), ())), preferred_element_...]
    unnamed x2 -> x0, blocking collectives: 110 us -> none
    all_gather x2 -> x0, blocking collectives: 53.5 us -> none  [the longest x1 36.6 us: attention_forward(): lax.all_gather(keyval.reshape(seq_count, -1, 2 * head_dim), 'ctx', axis=1...]
    psum x1 -> x0, blocking collectives: 41.5 us -> none  [shards(): lax.psum(attn_shares[0].astype(jnp.bfloat16), 'ctx').astype(jnp.float32)]
    psum x1 -> x0, waiting for transfers between devices: 41.4 us -> none  [shards(): lax.psum(attn_shares[2].astype(jnp.bfloat16), 'ctx').astype(jnp.float32)]
    convert_element_type x34 -> x0, other arithmetic: 18.5 us -> none  [the longest x6 2.59 us: one_block(): grad_score = (probs * (grad_prob - centre)).astype(jnp.bfloat16)]
  transfers between devices with their start and end apart: 11 -> 0, of which waited for: 7 -> 0; matrix products, arithmetic and copies ran while one was open for 20% -> 0% of each run, Pallas kernels for 0% -> 0%
where the time goes in v1:
time: 194 us
  Pallas kernels  175 us (90%)
  local copies, waits for them, and re-layouts  17.7 us (9%)
    pallas_call x1, Pallas kernels, shards(): pl.pallas_call(layer_kernel, out_shape=(jax.ShapeDtypeStruct((2, BLK, WID...  175 us
    unnamed x38, local copies, waits for them, and re-layouts  12.1 us

profile of v1, /device:TPU:0, one launch (start us, length us, event | category | flops | bytes accessed | tf_op | source)
XLA Modules:
  0.0 193.9 jit_solution(12971972042122208191)
XLA Ops:
  1.3 0.0 copy-start.15
  1.3 0.6 copy-done.15
  2.0 0.0 copy-start.7
  2.0 0.6 copy-done.7
  2.6 0.0 copy-start.8
  2.6 0.1 dynamic_update_slice.27
  2.7 0.6 copy-done.8
  3.3 0.0 copy-start.9
  3.3 0.1 dynamic_update_slice.28
  3.4 0.6 copy-done.9
  4.0 0.0 copy-start.10
  4.0 0.1 dynamic_update_slice.29
  4.0 0.6 copy-done.10
  4.6 0.0 copy-start.11
  4.6 0.1 dynamic_update_slice.30
  4.7 0.6 copy-done.11
  5.3 0.0 copy-start.12
  5.3 0.1 dynamic_update_slice.31
  5.4 0.6 copy-done.12
  5.9 0.0 copy-start.13
  5.9 0.1 dynamic_update_slice.32
  6.0 0.6 copy-done.13
  6.6 0.0 copy-start.14
  6.6 0.1 dynamic_update_slice.33
  6.7 0.6 copy-done.14
  7.2 0.2 dynamic_update_slice.34
  7.5 0.2 dynamic_update_slice.35.vecs
  7.7 0.0 copy-start.6
  7.7 0.6 copy-done.6
  8.3 174.7 %shard_map.297 = (bf16[2,128,768]{2,1,0:T(8,128)(2,1)}, f32[2,128,768]{2,1,0:T(8,128)}, f32[48,768]{1,0:T(8,128)}, f32[48,768]{1,0:T(8,128)}, f32[48,256]{1,0:T(...) custom-call(s32[1]{0:T(128)S(6)} %copy.50.lengths, s32[16]{0:T(128)} %block_map.1, bf16[2,128,768]{2,1,0:T(8,128)(2,1)} %bitcast.18, ...), custom_call_target="tpu_custom_call" | custom-call | tf_op jit(solution)/shard_map/pallas_call | solution.py:875
  183.0 0.7 slice.34
  183.7 0.6 dynamic-slice_bitcast_fusion
  184.3 2.0 %slice_reduce_fusion = (f32[48]{0:T(128)}, f32[48]{0:T(128)}, f32[48]{0:T(128)}, f32[48]{0:T(128)}, f32[48]{0:T(128)}, /*index=5*/f32[48]{0:T(128)}, f32[48]{0:T(128)}) fusion(f32[48,256]{1,0:T(8,128)} %get-tuple-element.25), kind=kLoop, calls=%fused_computation | loop fusion | bytes 2688 | tf_op jit(solution)/shard_map/slice | solution.py:908
  186.3 0.0 copy-done
  186.3 0.6 slice.33
  186.9 0.1 copy.34
  187.0 0.7 reshape.36
  187.7 1.8 copy.51
  189.4 0.0 copy-done.1
  189.4 0.9 copy.52
  190.3 0.1 copy-done.5
  190.5 0.7 copy.53
  191.1 0.0 copy-done.4
  191.1 0.7 copy.54
  191.8 0.0 copy-done.3
  191.8 0.8 copy.55
  192.6 0.5 copy-done.2
  193.1 0.8 copy.56
  (9 shorter events, 0.0 us)
Async XLA Ops:
  1.3 0.7 copy-start.15
  2.0 0.7 copy-start.7
  2.6 0.7 copy-start.8
  3.3 0.7 copy-start.9
  4.0 0.7 copy-start.10
  4.6 0.7 copy-start.11
  5.3 0.7 copy-start.12
  5.9 0.7 copy-start.13
  6.6 0.7 copy-start.14
  7.7 0.6 copy-start.6
  184.3 2.0 %copy-start = (f32[48,256]{1,0:T(8,128)S(1)}, f32[48,256]{1,0:T(8,128)}, u32[]{:S(2)}) copy-start(f32[48,256]{1,0:T(8,128)} %get-tuple-element.25) | copy-start | bytes 147460
  184.3 5.1 %copy-start.1 = (f32[2,128,768]{2,1,0:T(8,128)S(1)}, f32[2,128,768]{2,1,0:T(8,128)}, u32[]{:S(2)}) copy-start(f32[2,128,768]{2,1,0:T(8,128)} %get-tuple-element.24) | copy-start | bytes 2359300
  189.4 1.0 copy-start.5
  189.4 1.7 copy-start.4
  190.5 1.3 copy-start.3
  191.8 1.3 copy-start.2

commit v2 on v1

--- a/solution.py
+++ b/solution.py
@@ -25,7 +25,17 @@
 N_A, N_B = 8, 7
 ITEMS = N_A + N_B + 2
 KEYS = ITEMS * BLK
-SEMS = 224
+SEMS = 300
+
+
+class Chain:
+    def __init__(self, *steps):
+        self.steps = list(steps)
+        self.flying = []
+
+    def go(self, arrived):
+        arrived(self.flying)
+        self.flying = self.steps.pop(0)() if self.steps else []
 
 
 def dot(left, right):
@@ -53,16 +63,32 @@
 def layer_kernel(
     lengths,
     block_map,
-    tokens,
-    cotangent,
-    vecs,
+    tokens_in,
+    cotangent_in,
+    own_gain1,
+    own_shift1,
+    own_qbias,
+    own_vbias,
+    own_obias,
+    own_gain2,
+    own_shift2,
+    own_ubias,
+    own_dbias,
     wq,
     wkv,
     wo,
     wup,
     wdn,
-    out_ref,
-    ing_ref,
+    out_hbm,
+    ing_hbm,
+    gq_hbm,
+    go_hbm,
+    gt_hbm,
+    gup_hbm,
+    gdn_hbm,
+    tokens,
+    cotangent,
+    vecs,
     gq_ref,
     go_ref,
     gt_ref,
@@ -99,8 +125,10 @@
     f2_up,
     f2_dn,
     r_t,
-    c_q,
-    c_o,
+    cx_q,
+    cx_o,
+    ch_q,
+    ch_o,
     c_t,
     kv_all,
     dkv_out,
@@ -163,6 +191,8 @@
         return (zh * 4 + (xx + k) % 4, fs)
 
     h_peer = (ctx + 4 - 8 * zh, fs)
+    odd = xx % 2
+    x_of = ((ctx + 1 - 2 * odd, fs), (zh * 4 + 3 - xx, fs))
 
     count = [0]
     started = []
@@ -195,34 +225,38 @@
         locals_.append(copy)
         return copy
 
+    got_tokens = keep(tokens_in, tokens)
+    got_cotangent = keep(cotangent_in, cotangent)
     barrier = pltpu.get_barrier_semaphore()
     greeted = [(peer(j), fs) for j in range(1, PEERS)]
     greeted += [(ctx, shard_peer(k)) for k in range(1, 16)]
     greeted += [z_far]
     for device in greeted:
         pl.semaphore_signal(barrier, inc=1, device_id=device, device_id_type=MESH)
-    pl.semaphore_wait(barrier, len(greeted))
-
-    def gather_y(src, full):
-        out = [send(src, full.at[yy, zl, co], y_peer(k)) for k in (1, 2, 3)]
-        return out, keep(src, full.at[yy, zl, co])
-
-    def gather_z(full):
-        return [
-            send(
-                full.at[pl.ds(2 * e, 2), zl, co], full.at[pl.ds(2 * e, 2), zl, co], z_of[e]
-            )
-            for e in (0, 1)
-        ]
-
-    attn = ((vecs, f_vec), (wkv, f_kv), (wq, f_q), (wo, f_o))
-    step_y = [gather_y(src, full) for src, full in attn]
+
+    def spread(values, at):
+        size = values.shape[1]
+        i = lax.broadcasted_iota(jnp.int32, (size, WIDTH), 0)
+        lane = lax.broadcasted_iota(jnp.int32, (size, WIDTH), 1)
+        return dot(values, jnp.where(lane == at + i, 1.0, 0.0).astype(BF16))
+
+    plain = (own_gain1, own_shift1, own_qbias, own_obias, own_gain2, own_shift2, own_dbias)
+    plain = [ref[...].reshape(1, 48) for ref in plain]
+    up_row = spread(own_ubias[...].reshape(1, 192), (fs % 4) * 192)
+    vecs[...] = jnp.concatenate(
+        [spread(value, fs * 48) for value in plain]
+        + [spread(own_vbias[...].reshape(1, 4), HD + fs * 4)]
+        + [jnp.where(fs // 4 == r, up_row, 0.0) for r in range(4)]
+        + [jnp.zeros((4, WIDTH), F32)],
+        0,
+    ).astype(BF16)
 
     slot0, slot1 = block_map[2 * ctx], block_map[2 * ctx + 1]
     low = jnp.minimum(slot0, slot1)
     swap = slot0 > slot1
     length = lengths[0]
 
+    got_tokens.wait()
     t0, t1 = tokens[0], tokens[1]
     x_low[0:BLK] = jnp.where(swap, t1, t0)
     x_low[BLK:ROWS] = jnp.where(swap, t0, t1)
@@ -236,62 +270,132 @@
         both = jnp.concatenate([jnp.where(swap, c1, c0), jnp.where(swap, c0, c1)], 0)
         return valid * both
 
+    got_cotangent.wait()
     gos[0] = grad_out().astype(BF16)
-    go_copy = send(gos.at[0], gos.at[1], sib)
-
-    def gather_c(full, z):
-        return send(full.at[:, z, co], full.at[:, z, co], sib)
-
-    step_z, step_c = [], []
-    for (_, full), (copies, own) in zip(attn, step_y):
-        arrived(copies)
-        own.wait()
-        step_z.append(gather_z(full))
-        step_c.append(gather_c(full, zl))
-
-    def mine(c):
-        return pl.ds(pl.multiple_of(c * HALF, HALF), HALF)
-
-    def up_y():
-        out = [send(wup.at[:, mine(co)], f_up.at[yy, zl, co], y_peer(k)) for k in (1, 2, 3)]
-        out += [send(wup.at[:, mine(oc)], r_up.at[yy, zl], y_peer(k)) for k in (1, 2, 3)]
-        return out, [keep(wup.at[:, mine(co)], f_up.at[yy, zl, co]), keep(wup.at[:, mine(oc)], r_up.at[yy, zl])]
-
-    def up_z():
-        out = []
-        for e in (0, 1):
-            part_y = pl.ds(2 * e, 2)
-            out.append(send(f_up.at[part_y, zl, co], f_up.at[part_y, zl, co], z_of[e]))
-            out.append(send(r_up.at[part_y, zl], r_up.at[part_y, zl], z_of[e]))
-        return out
-
-    def dn_slot(y, z):
-        other = y // 2 + co - 2 * (y // 2) * co
-        return (1 - other) * ((y % 2) * 4 + z * 2 + co) + other * (8 + (y % 2) * 2 + z)
-
-    def dn_y():
-        dst = f_dn.at[dn_slot(yy, zl)]
-        return [send(wdn, dst, y_peer(k)) for k in (1, 2, 3)], [keep(wdn, dst)]
-
-    def dn_z():
-        return [
-            send(f_dn.at[dn_slot(y, zl)], f_dn.at[dn_slot(y, zl)], z_of[y // 2]) for y in range(4)
-        ]
-
-    y_up, own_up = up_y()
-    y_dn, own_dn = dn_y()
-
-    for i, (_, full) in enumerate(attn):
-        arrived(step_z[i])
-        step_c.append(gather_c(full, oz))
-
-    def up_c(z):
-        return [send(r_up.at[:, z], f_up.at[:, z, co], sib)]
-
-    def dn_c(z):
-        return [send(f_dn.at[8 + y * 2 + z], f_dn.at[y * 4 + z * 2 + co], sib) for y in (0, 1)]
-
-    arrived([step_c[0], step_c[4]])
+
+    pl.semaphore_wait(barrier, len(greeted))
+
+    def thirds_of(start, width):
+        return (
+            pl.ds(pl.multiple_of(start + odd * width, BLK), 2 * width),
+            pl.ds(pl.multiple_of(start + odd * 2 * width, BLK), width),
+            pl.ds(pl.multiple_of(start + (1 - odd) * 2 * width, BLK), width),
+        )
+
+    every = slice(None)
+
+    class Whole:
+        def __init__(self, src, full, cols=None, rows=every, dst=None, src_at=0):
+            self.src, self.full, self.rows = src, full, rows
+            self.dst = full if dst is None else dst
+            self.fetch, self.own, self.other = (every,) * 3 if cols is None else thirds_of(*cols)
+            self.src_cols = self.fetch
+            if cols is not None:
+                self.src_cols = pl.ds(
+                    pl.multiple_of(src_at + cols[0] + odd * cols[1], BLK), 2 * cols[1]
+                )
+
+        def at(self, y, z, cols):
+            return self.full.at[y, z, co, self.rows, cols]
+
+        def y(self):
+            src, dst = self.src.at[self.rows, self.src_cols], self.at(yy, zl, self.fetch)
+            self.kept = keep(src, dst)
+            return [send(src, dst, y_peer(k)) for k in (1, 2, 3)]
+
+        def z(self):
+            self.kept.wait()
+            refs = [self.at(pl.ds(2 * e, 2), zl, self.fetch) for e in (0, 1)]
+            return [send(ref, ref, z_of[e]) for e, ref in enumerate(refs)]
+
+        def x(self):
+            refs = [self.at(pl.ds(2 * e, 2), every, self.own) for e in (0, 1)]
+            return [send(ref, ref, x_of[e]) for e, ref in enumerate(refs)]
+
+        def c(self, cols, z=every):
+            ref = self.at(every, z, cols)
+            return [send(ref, self.dst.at[every, z, co, self.rows, cols], sib)]
+
+    class Part(Whole):
+        def at(self, y, z, cols):
+            return self.full.at[y, z, self.rows, cols]
+
+    class Mine(Whole):
+        def c(self, cols, z=every):
+            return []
+
+    class Units(Whole):
+        def at(self, y, z, cols):
+            e = yy // 2 if y is yy else y
+            other = e + co - 2 * e * co
+            lead = (1 - other) * co + 2 * other
+            return self.full.at[lead, yy % 2 if y is yy else every, z, self.rows, cols]
+
+        def z(self):
+            self.kept.wait()
+            refs = [self.at(e, zl, self.fetch) for e in (0, 1)]
+            return [send(ref, ref, z_of[e]) for e, ref in enumerate(refs)]
+
+        def x(self):
+            refs = [self.at(e, every, self.own) for e in (0, 1)]
+            return [send(ref, ref, x_of[e]) for e, ref in enumerate(refs)]
+
+        def c(self, cols, z=every):
+            ref = self.full.at[2, every, z, self.rows, cols]
+            return [send(ref, self.full.at[co, every, z, self.rows, cols], sib)]
+
+    def each(arrays, action):
+        return [copy for array in arrays for copy in action(array)]
+
+    def narrow(*arrays):
+        first = []
+
+        def after_y():
+            out = each(arrays, lambda a: a.z())
+            first.extend(each(arrays, lambda a: a.c(every, zl)))
+            return out
+
+        return Chain(
+            lambda: each(arrays, lambda a: a.y()),
+            after_y,
+            lambda: each(arrays, lambda a: a.c(every, oz)) + first,
+        )
+
+    def wide(*arrays):
+        first = []
+
+        def after_z():
+            out = each(arrays, lambda a: a.x())
+            first.extend(each(arrays, lambda a: a.c(a.fetch)))
+            return out
+
+        return Chain(
+            lambda: each(arrays, lambda a: a.y()),
+            lambda: each(arrays, lambda a: a.z()),
+            after_z,
+            lambda: each(arrays, lambda a: a.c(a.other)) + first,
+        )
+
+    def step(*chains):
+        for chain in chains:
+            chain.go(arrived)
+
+    def up_chunk(j):
+        cols = (j * WIDTH, WIDTH // 3)
+        return wide(
+            Mine(wup, f_up, cols, src_at=co * HALF),
+            Part(wup, r_up, cols, dst=f_up, src_at=oc * HALF),
+        )
+
+    kvv = narrow(Whole(vecs, f_vec), Whole(wkv, f_kv))
+    wq_in, wo_in = wide(Whole(wq, f_q, (0, 256))), wide(Whole(wo, f_o, (0, 256)))
+    dn_a, dn_b = (wide(Units(wdn, f_dn, (0, 256), pl.ds(96 * i, 96))) for i in (0, 1))
+    up_a, up_b = up_chunk(0), up_chunk(1)
+
+    step(kvv, wq_in, wo_in)
+    step(kvv, dn_a)
+    step(wq_in, kvv, dn_b)
+    step(wo_in, kvv)
     vec = f_vec[...].astype(F32).reshape(16, 16, WIDTH)
     vec = jnp.sum(vec, 0)
     gain1, shift1, qbias, obias = vec[0:1], vec[1:2], vec[2:3], vec[3:4]
@@ -302,23 +406,17 @@
     xn[...] = xn_v.astype(BF16)
     xn_t[...] = xn_v.T.astype(BF16)
 
-    arrived([step_c[1], step_c[5]])
     kv = dot(xn[...], f_kv[...].reshape(WIDTH, 2 * HD)) + kvbias
     kv_all[0] = kv.astype(BF16)
-    kv_copies = [send(kv_all.at[0], kv_all.at[j], (peer(j), fs)) for j in range(1, PEERS)]
-
-    arrived(y_up)
-    for copy in own_up:
-        copy.wait()
-    z_up = up_z()
-    c_up = up_c(zl)
-    arrived(y_dn)
-    for copy in own_dn:
-        copy.wait()
-    z_dn = dn_z()
-    c_dn = dn_c(zl)
-
-    arrived([step_c[2], step_c[6]])
+    kv_copies = [send(kv_all.at[0], kv_all.at[j], (peer(j), fs)) for j in (1, 2, 3)]
+    kv_far = send(kv_all.at[0], kv_all.at[4], h_peer)
+    step(wq_in, dn_a, up_a, wo_in)
+    arrived([kv_far])
+    kv_copies += [send(kv_all.at[4], kv_all.at[4 + j], (peer(j), fs)) for j in (1, 2, 3)]
+    step(wq_in, dn_b, up_b, wq_in)
+    go_copy = send(gos.at[0], gos.at[1], sib)
+    step(dn_a, wo_in)
+
     q = dot(xn[...], f_q[...].reshape(WIDTH, WIDTH)) + qbias
     q = (q.astype(BF16).astype(F32) * (HD**-0.5)).T
     for g in range(GROUPS):
@@ -334,6 +432,7 @@
         q_rows[g] = both.T.astype(BF16)
 
     arrived(kv_copies)
+    step(up_a)
     lane = lax.broadcasted_iota(jnp.int32, (BLK, BLK), 1)
     sub = lax.broadcasted_iota(jnp.int32, (BLK, BLK), 0)
     extra = lax.broadcasted_iota(jnp.int32, (16, BLK), 0)
@@ -424,14 +523,14 @@
         att_t[g, HD:BLK, BLK:ROWS] = high[:, BLK:].astype(BF16)
         return carry
 
-    lax.fori_loop(0, GROUPS // 2, forward_group, 0)
-    arrived(z_up)
-    c_up += up_c(oz)
-    arrived(z_dn)
-    c_dn += dn_c(oz)
-    lax.fori_loop(GROUPS // 2, GROUPS, forward_group, 0)
-
-    arrived([step_c[3], step_c[7]])
+    lax.fori_loop(0, 2, forward_group, 0)
+    step(dn_a, dn_b)
+    lax.fori_loop(2, 4, forward_group, 0)
+    step(up_b, up_a)
+    lax.fori_loop(4, 6, forward_group, 0)
+    step(dn_b, up_a, up_b)
+
+    step(wo_in)
     attended = att_t[...].reshape(WIDTH, ROWS).astype(F32).T.astype(BF16)
     mixed = x_low[...].astype(F32) + dot(attended, f_o[...].reshape(WIDTH, WIDTH)) + obias
     mixed_s[...] = mixed
@@ -439,7 +538,20 @@
     n2s[0] = (n2 * gain2 + shift2).astype(BF16)
     n2_copy = send(n2s.at[0], n2s.at[1], sib)
 
-    arrived([go_copy] + c_up + c_dn + [n2_copy])
+    step(up_b)
+    arrived([go_copy])
+    step(dn_a, dn_b, up_a)
+    arrived([n2_copy])
+
+    def unit_rows(j, start, size):
+        blocks = []
+        while size:
+            k, r = start // 192, start % 192
+            n = min(size, 192 - r)
+            blocks.append(f_dn[k % 2, j, k // 2, r : r + n])
+            start, size = start + n, size - n
+        return jnp.concatenate(blocks, 0)
+
     sub_cols = 256
     n_sub = HALF // sub_cols
     coef = 0.7978845608028654
@@ -448,13 +560,14 @@
     for s in range(n_sub):
         cols = slice(s * sub_cols, (s + 1) * sub_cols)
         per = WIDTH // sub_cols
+        if s == per:
+            step(up_b)
         bias_row = jnp.where(co == 0, vec[8 + s // per : 9 + s // per], vec[10 + s // per : 11 + s // per])
         bias = bias_row[:, (s % per) * sub_cols : (s % per + 1) * sub_cols]
         n2b = n2s[...].reshape(2 * ROWS, WIDTH)
         gob = gos[...].reshape(2 * ROWS, WIDTH)
         up = dot(n2b, f_up[:, :, :, :, cols].reshape(WIDTH, sub_cols)) + bias
-        w_rows = f_dn[4 * (s // per) : 4 * (s // per) + 4].reshape(WIDTH, WIDTH)
-        w_rows = w_rows[(s % per) * sub_cols : (s % per + 1) * sub_cols]
+        w_rows = unit_rows(s // per, (s % per) * sub_cols, sub_cols)
         dmid = dot_nt(gob, w_rows)
         square = up * up
         th = jnp.tanh(coef * up * (1.0 + 0.044715 * square))
@@ -466,6 +579,148 @@
         up_sums.append(jnp.sum(du.astype(F32), 0, keepdims=True))
 
     thirds = [slice(256 * n, 256 * (n + 1)) for n in range(3)]
+    for j in (0, 1):
+        m_t = mid[:, j * WIDTH : (j + 1) * WIDTH].astype(F32).T.astype(BF16)
+        for n in thirds:
+            piece = dot(m_t, gos[:, :, n].reshape(2 * ROWS, 256))
+            g_dn[j, :, :, :, n] = piece.astype(BF16).reshape(2, 2, 192, 256)
+
+    def low_sum(own, *others):
+        total = own.astype(F32)
+        for other in others:
+            total = total + other.astype(F32)
+        return total.astype(BF16)
+
+    class Down:
+        def __init__(self, rows):
+            self.rows = rows
+
+        def z(self):
+            rows = self.rows
+            return [send(g_dn.at[j, oz, :, rows], rz_dn.at[j, :, rows], z_of[j]) for j in (0, 1)]
+
+        def c(self):
+            rows = self.rows
+            for j in (0, 1):
+                g_dn[j, zl, :, rows] = low_sum(g_dn[j, zl, :, rows], rz_dn[j, :, rows])
+                s_dn[2 * co + j, rows] = g_dn[j, zl, co, rows]
+            return [send(g_dn.at[:, zl, oc, rows], s_dn.at[pl.ds(2 * co, 2), rows], sib)]
+
+        def y(self):
+            rows = self.rows
+            return [
+                send(s_dn.at[(yy + k) % 4, rows], ry_dn.at[k - 1, rows], y_peer(k)) for k in (1, 2, 3)
+            ]
+
+        def y_sum(self):
+            rows = self.rows
+            s_dn[yy, rows] = low_sum(s_dn[yy, rows], *[ry_dn[k, rows] for k in range(3)])
+            return []
+
+        def x(self):
+            self.y_sum()
+            return [
+                send(s_dn.at[yy, quarter_dn((xx + k) % 4)], rx_dn.at[k - 1], x_peer(k))
+                for k in (1, 2, 3)
+            ]
+
+        def h(self):
+            rh_dn[1] = low_sum(s_dn[yy, quarter_dn(xx)], *[rx_dn[k] for k in range(3)])
+            return [send(rh_dn.at[1], rh_dn.at[0], h_peer)]
+
+        def a(self):
+            f2_dn[xx] = low_sum(rh_dn[0], rh_dn[1])
+            return [send(f2_dn.at[xx], f2_dn.at[xx], x_peer(k)) for k in (1, 2, 3)]
+
+    def quarter_dn(k):
+        return pl.ds(pl.multiple_of(k * 48, 16), 48)
+
+    class Up:
+        def __init__(self, i):
+            self.i, self.cols = i, slice(512 * i, 512 * (i + 1))
+
+        def quarter(self, k):
+            return pl.ds(pl.multiple_of(512 * self.i + k * BLK, BLK), BLK)
+
+        def z(self):
+            return [
+                send(
+                    g_up.at[pl.ds(2 * e, 2), oz, :, :, self.cols],
+                    rz_up.at[pl.ds(2 * e, 2), :, :, self.cols],
+                    z_of[e],
+                )
+                for e in (0, 1)
+            ]
+
+        def c(self):
+            cols = self.cols
+            g_up[:, zl, :, :, cols] = low_sum(g_up[:, zl, :, :, cols], rz_up[:, :, :, cols])
+            s_up[:, co, :, cols] = g_up[:, zl, co, :, cols]
+            return [send(g_up.at[:, zl, oc, :, cols], s_up.at[:, co, :, cols], sib)]
+
+        def y(self):
+            cols = self.cols
+            return [
+                send(s_up.at[(yy + k) % 4, :, :, cols], ry_up.at[k - 1, :, :, cols], y_peer(k))
+                for k in (1, 2, 3)
+            ]
+
+        def x(self):
+            cols = self.cols
+            s_up[yy, :, :, cols] = low_sum(
+                s_up[yy, :, :, cols], *[ry_up[k, :, :, cols] for k in range(3)]
+            )
+            return [
+                send(s_up.at[yy, :, :, self.quarter((xx + k) % 4)], rx_up.at[self.i, k - 1], x_peer(k))
+                for k in (1, 2, 3)
+            ]
+
+        def h(self):
+            got = [rx_up[self.i, k] for k in range(3)]
+            rh_up[self.i, 1] = low_sum(s_up[yy, :, :, self.quarter(xx)], *got)
+            return [send(rh_up.at[self.i, 1], rh_up.at[self.i, 0], h_peer)]
+
+        def a(self):
+            f2_up[self.i, xx] = low_sum(rh_up[self.i, 0], rh_up[self.i, 1])
+            ref = f2_up.at[self.i, xx]
+            return [send(ref, ref, x_peer(k)) for k in (1, 2, 3)]
+
+    down = [Down(slice(96 * i, 96 * (i + 1))) for i in (0, 1)]
+    down_a = Chain(down[0].z, down[0].c, down[0].y, down[0].y_sum)
+    down_b = Chain(down[1].z, down[1].c, down[1].y, down[1].x, down[1].h, down[1].a)
+    ups = [Chain(u.z, u.c, u.y, u.x, u.h, u.a) for u in map(Up, range(3))]
+
+    def square(grad, rc, rz, ry, cx, ch):
+        def c():
+            return [send(grad.at[:, :, oc], rc, sib)]
+
+        def z():
+            grad[:, :, co] = low_sum(grad[:, :, co], rc[...])
+            return [
+                send(grad.at[pl.ds(2 * e, 2), oz, co], rz.at[pl.ds(2 * e, 2)], z_of[e])
+                for e in (0, 1)
+            ]
+
+        def y():
+            grad[:, zl, co] = low_sum(grad[:, zl, co], rz[...])
+            return [
+                send(grad.at[(yy + k) % 4, zl, co], ry.at[k - 1], y_peer(k)) for k in (1, 2, 3)
+            ]
+
+        def x():
+            cx[0] = low_sum(grad[yy, zl, co], *[ry[k] for k in range(3)])
+            return [send(cx.at[0], cx.at[k], x_peer(k)) for k in (1, 2, 3)]
+
+        def h():
+            ch[0] = low_sum(cx[0], *[cx[k] for k in (1, 2, 3)])
+            return [send(ch.at[0], ch.at[1], h_peer)]
+
+        return Chain(c, z, y, x, h)
+
+    out_w = square(g_o, rc_o, rz_o, ry_o, cx_o, ch_o)
+    query_w = square(g_q, rc_q, rz_q, ry_q, cx_q, ch_q)
+
+    step(down_a)
     for n in thirds:
         w = f_up[...].reshape(WIDTH, HALF)[n]
         piece = dot_nt(dup[...], w)
@@ -473,19 +728,12 @@
         dsec_out[:, n] = piece[ROWS:].astype(BF16)
     dsec_copy = send(dsec_out, dsec_in, sib)
 
-    z_dn = []
-    for j in (0, 1):
-        m_t = mid[:, j * WIDTH : (j + 1) * WIDTH].astype(F32).T.astype(BF16)
-        for n in thirds:
-            piece = dot(m_t, gos[:, :, n].reshape(2 * ROWS, 256))
-            g_dn[j, :, :, :, n] = piece.astype(BF16).reshape(2, 2, 192, 256)
-        z_dn.append(send(g_dn.at[j, oz], rz_dn.at[j], z_of[j]))
     n2_t = n2s[...].reshape(2 * ROWS, WIDTH).astype(F32).T.astype(BF16)
     for s in range(n_sub):
         cols = slice(s * sub_cols, (s + 1) * sub_cols)
         piece = dot(n2_t, dup[:, cols])
         g_up[:, :, :, :, cols] = piece.astype(BF16).reshape(4, 2, 2, 48, sub_cols)
-    z_up = [send(g_up.at[pl.ds(2 * e, 2), oz], rz_up.at[pl.ds(2 * e, 2)], z_of[e]) for e in (0, 1)]
+    step(down_b)
 
     arrived([dsec_copy])
     dsec = dsec_own[...] + dsec_in[...].astype(F32)
@@ -493,8 +741,8 @@
     sum_gain2 = jnp.sum(dsec * n2, 0, keepdims=True)
     sum_shift2 = jnp.sum(dsec, 0, keepdims=True)
     dmix = grad_out() + norm_back(n2, rate2, dsec, gain2)
-    ing_ref[0] = dmix[:BLK]
-    ing_ref[1] = dmix[BLK:]
+    cotangent[0] = dmix[:BLK]
+    cotangent[1] = dmix[BLK:]
     dmix_low = dmix.astype(BF16)
     dmix_r = dmix_low.astype(F32)
     sum_obias = jnp.sum(dmix_r, 0, keepdims=True)
@@ -503,10 +751,11 @@
     g_o[...] = (
         dot(att_t[...].reshape(WIDTH, ROWS), dmix_low).astype(BF16).reshape(4, 2, 2, 48, WIDTH)
     )
-    c_go = send(g_o.at[:, :, oc], rc_o, sib)
+    step(out_w)
 
     for n in thirds:
-        piece = dot(mid[...], f_dn[0:8, :, n].reshape(HALF, 256))
+        blocks = [f_dn[c, j, z, :, n] for j in (0, 1) for z in (0, 1) for c in (0, 1)]
+        piece = dot(mid[...], jnp.concatenate(blocks, 0))
         dsec_own[:, n] = piece[:ROWS]
         part_out[:, n] = piece[ROWS:].astype(BF16)
     part_copy = send(part_out, part_in, sib)
@@ -523,31 +772,6 @@
         both = both.astype(BF16).astype(F32) * o_norm[g]
         l_inv[g, 0:8] = jnp.broadcast_to(jnp.sum(both[:HD], 0, keepdims=True), (8, ROWS))
         l_inv[g, 8:16] = jnp.broadcast_to(jnp.sum(both[HD:], 0, keepdims=True), (8, ROWS))
-
-    def dn_after_z():
-        for j in (0, 1):
-            arrived([z_dn[j]])
-            total = g_dn[j, zl].astype(F32) + rz_dn[j].astype(F32)
-            g_dn[j, zl] = total.astype(BF16)
-        copies = []
-        for j in (0, 1):
-            copies.append(send(g_dn.at[j, zl, oc], s_dn.at[2 * co + j], sib))
-            s_dn[2 * co + j] = g_dn[j, zl, co]
-        return copies
-
-    def up_after_z():
-        copies = []
-        for e in (0, 1):
-            arrived([z_up[e]])
-            part_y = pl.ds(2 * e, 2)
-            total = g_up[part_y, zl].astype(F32) + rz_up[part_y].astype(F32)
-            g_up[part_y, zl] = total.astype(BF16)
-            copies.append(send(g_up.at[part_y, zl, oc], s_up.at[part_y, :, mine(co)], sib))
-            s_up[part_y, :, mine(co)] = g_up[part_y, zl, co]
-        return copies
-
-    def y_sends(src, dst):
-        return [send(src.at[(yy + k) % 4], dst.at[k - 1], y_peer(k)) for k in (1, 2, 3)]
 
     acc[...] = jnp.zeros_like(acc)
 
@@ -573,36 +797,11 @@
         return carry
 
     lax.fori_loop(0, 2, backward_group, 0)
-
-    c_dn = dn_after_z()
-    c_up = up_after_z()
-    arrived([c_go])
-    g_o[:, :, co] = (g_o[:, :, co].astype(F32) + rc_o[...].astype(F32)).astype(BF16)
-
-    def z_sends(grad, dst):
-        return [
-            send(grad.at[pl.ds(2 * e, 2), oz, co], dst.at[pl.ds(2 * e, 2)], z_of[e]) for e in (0, 1)
-        ]
-
-    z_o = z_sends(g_o, rz_o)
+    step(out_w)
     lax.fori_loop(2, 4, backward_group, 0)
-
-    arrived(c_dn)
-    y_dn = y_sends(s_dn, ry_dn)
-    arrived(c_up)
-    y_up = y_sends(s_up, ry_up)
-
-    def after_z(copies, grad, got):
-        arrived(copies)
-        grad[:, zl, co] = (grad[:, zl, co].astype(F32) + got[...].astype(F32)).astype(BF16)
-        return [
-            send(grad.at[(yy + k) % 4, zl, co], ry.at[k - 1], y_peer(k))
-            for ry in [{id(rz_o): ry_o, id(rz_q): ry_q}[id(got)]]
-            for k in (1, 2, 3)
-        ]
-
-    y_o = after_z(z_o, g_o, rz_o)
+    step(down_a, ups[0])
     lax.fori_loop(4, 6, backward_group, 0)
+    step(down_a)
 
     def halves(item, second):
         rows = slice(item * BLK, (item + 1) * BLK)
@@ -624,43 +823,10 @@
     sum_qbias = jnp.sum(dq, 0, keepdims=True)
     dq = dq.astype(BF16)
     g_q[...] = dot(xn_t[...], dq).astype(BF16).reshape(4, 2, 2, 48, WIDTH)
-    c_gq = send(g_q.at[:, :, oc], rc_q, sib)
+    step(query_w, down_b, ups[1])
     dfirst = dot_nt(dq, f_q[...].reshape(WIDTH, WIDTH))
 
-    def y_sum(own, got):
-        total = own.astype(F32)
-        for k in range(3):
-            total = total + got[k].astype(F32)
-        return total
-
-    arrived(y_dn)
-    s_dn[yy] = y_sum(s_dn[yy], ry_dn).astype(BF16)
-    arrived(y_up)
-    s_up[yy] = y_sum(s_up[yy], ry_up).astype(BF16)
-
-    def quarter_dn(k):
-        return pl.ds(pl.multiple_of(k * 48, 16), 48)
-
-    def quarter_up(k):
-        return pl.ds(pl.multiple_of(k * WIDTH, WIDTH), WIDTH)
-
-    x_dn, x_up = [], []
-    for k in (1, 2, 3):
-        q4 = (xx + k) % 4
-        x_dn.append(send(s_dn.at[yy, quarter_dn(q4)], rx_dn.at[k - 1], x_peer(k)))
-        x_up.append(send(s_up.at[yy, :, quarter_up(q4)], rx_up.at[k - 1], x_peer(k)))
-
-    arrived(y_o)
-    g_o[yy, zl, co] = y_sum(g_o[yy, zl, co], ry_o).astype(BF16)
-
-    def ctx_sends(src, dst):
-        return [send(src, dst.at[j], (peer(j), fs)) for j in range(1, PEERS)]
-
-    ctx_o = ctx_sends(g_o.at[yy, zl, co], c_o)
-
-    arrived([c_gq])
-    g_q[:, :, co] = (g_q[:, :, co].astype(F32) + rc_q[...].astype(F32)).astype(BF16)
-    z_q = z_sends(g_q, rz_q)
+    step(query_w, down_b, out_w, down_a, ups[0], ups[2])
 
     top = halves(0, False) + halves(N_A + N_B + 1, True)
     dkv = jnp.concatenate([top, halves(N_A + N_B, False)], 0)
@@ -705,69 +871,117 @@
             send(g_t.at[dst // 4, (dst // 2) % 2, dst % 2], r_t.at[k], (ctx, dst))
         )
 
-    y_q = after_z(z_q, g_q, rz_q)
-
-    ing = ing_ref[...].reshape(ROWS, WIDTH) + norm_back(n1, rate1, dfirst, gain1)
-    ing_ref[0] = jnp.where(swap, ing[BLK:], ing[:BLK])
-    ing_ref[1] = jnp.where(swap, ing[:BLK], ing[BLK:])
+    step(ups[0], down_b, query_w, out_w)
+
+    ing = cotangent[...].reshape(ROWS, WIDTH) + norm_back(n1, rate1, dfirst, gain1)
+    cotangent[0] = jnp.where(swap, ing[BLK:], ing[:BLK])
+    cotangent[1] = jnp.where(swap, ing[:BLK], ing[BLK:])
+    done = [keep(cotangent, ing_hbm)]
     arrived([part_copy])
     res = valid * (mixed_s[...] + dsec_own[...] + part_in[...].astype(F32) + dbias)
-    out_ref[0] = jnp.where(swap, res[BLK:], res[:BLK]).astype(BF16)
-    out_ref[1] = jnp.where(swap, res[:BLK], res[BLK:]).astype(BF16)
-
-    h_out = []
-    arrived(x_dn)
-    rh_dn[1] = y_sum(s_dn[yy, quarter_dn(xx)], rx_dn).astype(BF16)
-    h_out.append(send(rh_dn.at[1], rh_dn.at[0], h_peer))
-    arrived(x_up)
-    rh_up[1] = y_sum(s_up[yy, :, quarter_up(xx)], rx_up).astype(BF16)
-    h_out.append(send(rh_up.at[1], rh_up.at[0], h_peer))
+    tokens[0] = jnp.where(swap, res[BLK:], res[:BLK]).astype(BF16)
+    tokens[1] = jnp.where(swap, res[:BLK], res[BLK:]).astype(BF16)
+    done.append(keep(tokens, out_hbm))
+
+    step(ups[1], ups[0], ups[1], down_b, out_w)
 
     arrived(t_copies)
     total = g_t[yy, zl, co].astype(F32)
     for k in range(1, 16):
         total = total + r_t[k].astype(F32)
     c_t[0] = total.astype(BF16)
-    ctx_t = ctx_sends(c_t.at[0], c_t)
-
-    arrived(y_q)
-    g_q[yy, zl, co] = y_sum(g_q[yy, zl, co], ry_q).astype(BF16)
-    ctx_q = ctx_sends(g_q.at[yy, zl, co], c_q)
-
-    arrived([h_out[0]])
-    f2_dn[xx] = (rh_dn[0].astype(F32) + rh_dn[1].astype(F32)).astype(BF16)
-    a_dn = [send(f2_dn.at[xx], f2_dn.at[xx], x_peer(k)) for k in (1, 2, 3)]
-    arrived([h_out[1]])
-    f2_up[xx] = (rh_up[0].astype(F32) + rh_up[1].astype(F32)).astype(BF16)
-    a_up = [send(f2_up.at[xx], f2_up.at[xx], x_peer(k)) for k in (1, 2, 3)]
-
-    def ctx_sum(copies, own, got):
-        arrived(copies)
-        total = own.astype(F32)
-        for j in range(1, PEERS):
-            total = total + got[j].astype(F32)
-        return total
-
-    go_ref[...] = ctx_sum(ctx_o, g_o[yy, zl, co], c_o)
-    gt_ref[...] = ctx_sum(ctx_t, c_t[0], c_t)
-    gq_ref[...] = ctx_sum(ctx_q, g_q[yy, zl, co], c_q)
-    arrived(a_dn)
+    ctx_t = [send(c_t.at[0], c_t.at[j], (peer(j), fs)) for j in range(1, PEERS)]
+
+    step(ups[2], ups[2], query_w, ups[0], ups[1], down_b, query_w, ups[0], ups[2])
+    step(out_w, ups[1], ups[2], query_w, ups[1], ups[2], ups[2])
+
+    go_ref[...] = ch_o[0].astype(F32) + ch_o[1].astype(F32)
+    done.append(keep(go_ref, go_hbm))
+    step(down_b)
     gdn_ref[...] = f2_dn[...].astype(F32).reshape(192, WIDTH)
-    arrived(a_up)
-    for k in range(4):
-        gup_ref[:, k * WIDTH : (k + 1) * WIDTH] = f2_up[k].astype(F32)
+    done.append(keep(gdn_ref, gdn_hbm))
+    step(*ups)
+    for i in range(3):
+        for k in range(4):
+            for half in (0, 1):
+                at = half * HALF + 512 * i + k * BLK
+                gup_ref[:, at : at + BLK] = f2_up[i, k, half].astype(F32)
+    done.append(keep(gup_ref, gup_hbm))
+    arrived(ctx_t)
+    total = c_t[0].astype(F32)
+    for j in range(1, PEERS):
+        total = total + c_t[j].astype(F32)
+    gt_ref[...] = total
+    done.append(keep(gt_ref, gt_hbm))
+    step(query_w)
+    gq_ref[...] = ch_q[0].astype(F32) + ch_q[1].astype(F32)
+    done.append(keep(gq_ref, gq_hbm))
+    for chain in (kvv, wq_in, wo_in, dn_a, dn_b, up_a, up_b, down_a, down_b, out_w, query_w, *ups):
+        assert not chain.steps and not chain.flying
+    for copy in done:
+        copy.wait()
 
     for copy in started:
         copy.wait_send()
 
 
-def expand(values, at, fs):
-    first = jnp.zeros((16, WIDTH), BF16)
-    for row, value in enumerate(values):
-        first = lax.dynamic_update_slice(first, value[None], (row, fs * 48))
-    value_bias, up_bias = at
-    first = lax.dynamic_update_slice(first, value_bias[None], (7, HD + fs * 4))
-    return lax.dynamic_update_slice(first, up_bias[None], (8 + fs // 4, (fs % 4) * 192))
+def finish_kernel(
+    out_in,
+    ing_in,
+    gq_in,
+    go_in,
+    gt_in,
+    gup_in,
+    gdn_in,
+    out,
+    ing,
+    gain1,
+    shift1,
+    gq,
+    qbias,
+    gkv,
+    vbias,
+    go,
+    obias,
+    gain2,
+    shift2,
+    gup,
+    ubias,
+    gdn,
+    dbias,
+    stage0,
+    stage1,
+    stage2,
+    stage3,
+    stage4,
+    stage5,
+    sems,
+):
+    stages = (stage0, stage1, stage2, stage3, stage4, stage5)
+    pairs = ((ing_in, ing), (gup_in, gup), (gdn_in, gdn), (out_in, out), (gq_in, gq), (go_in, go))
+    loads, stores = [], []
+    for i, ((src, dst), stage) in enumerate(zip(pairs, stages)):
+        loads.append(pltpu.make_async_copy(src, stage, sems.at[i]))
+        stores.append(pltpu.make_async_copy(stage, dst, sems.at[6 + i]))
+        loads[i].start()
+    fs = lax.axis_index("fsdp")
+    gkv[...] = gt_in[:, 0:BLK]
+    columns = gt_in[:, BLK : 2 * BLK]
+    rows = jnp.concatenate([columns, jnp.zeros((BLK - 48, BLK), F32)], 0).T
+    for k, ref in ((4, dbias), (5, gain2), (6, shift2), (7, obias), (8, gain1), (9, shift1), (10, qbias)):
+        ref[...] = rows[k, 0:48]
+    ubias[...] = jnp.concatenate([rows[r : r + 1, 0:48] for r in range(4)], 1)[0]
+    lane = lax.broadcasted_iota(jnp.int32, (8, BLK), 1)
+    pick = jnp.zeros((8, BLK), F32)
+    for i in range(4):
+        value = jnp.sum(jnp.where(lane == HD + fs * 4 + i, columns[0:8], 0.0), 1, keepdims=True)
+        pick = jnp.where(lane == i, value, pick)
+    vbias[...] = pick[0, 0:4]
+    for load, store in zip(loads, stores):
+        load.wait()
+        store.start()
+    for store in stores:
+        store.wait()
 
 
 def shards(
@@ -790,12 +1004,6 @@
     down_bias,
     cotangent,
 ):
-    fs = lax.axis_index("fsdp")
-    vecs = expand(
-        (first_gain, first_shift, query_bias, output_bias, second_gain, second_shift, down_bias),
-        (value_bias, up_bias),
-        fs,
-    )
     vmem = pl.BlockSpec(memory_space=pltpu.VMEM)
     smem = pl.BlockSpec(memory_space=pltpu.SMEM)
     hbm = pl.BlockSpec(memory_space=pl.ANY)
@@ -803,14 +1011,29 @@
     def v(*shape, dtype=BF16):
         return pltpu.VMEM(shape, dtype)
 
+    shapes = (
+        jax.ShapeDtypeStruct((2, BLK, WIDTH), BF16),
+        jax.ShapeDtypeStruct((2, BLK, WIDTH), F32),
+        jax.ShapeDtypeStruct((48, WIDTH), F32),
+        jax.ShapeDtypeStruct((48, WIDTH), F32),
+        jax.ShapeDtypeStruct((48, 2 * BLK), F32),
+        jax.ShapeDtypeStruct((48, FF), F32),
+        jax.ShapeDtypeStruct((192, WIDTH), F32),
+    )
     scratch = [
+        v(2, BLK, WIDTH),
+        v(2, BLK, WIDTH, dtype=F32),
+        v(16, WIDTH),
+    ]
+    scratch += [v(*shape.shape, dtype=shape.dtype) for shape in shapes[2:]]
+    scratch += [
         v(4, 2, 2, 16, WIDTH),
         v(4, 2, 2, 48, WIDTH),
         v(4, 2, 2, 48, 2 * HD),
         v(4, 2, 2, 48, WIDTH),
         v(4, 2, 2, 48, HALF),
         v(4, 2, 48, HALF),
-        v(12, 192, WIDTH),
+        v(3, 2, 2, 192, WIDTH),
         v(4, 2, 2, 48, WIDTH),
         v(4, 2, 2, 48, WIDTH),
         v(4, 2, 2, 48, 2 * BLK),
@@ -822,21 +1045,23 @@
         v(4, 48, WIDTH),
         v(4, 2, 48, HALF),
         v(2, 2, 192, WIDTH),
-        v(4, 48, FF),
+        v(4, 2, 48, HALF),
         v(4, 192, WIDTH),
         v(3, 48, WIDTH),
         v(3, 48, WIDTH),
-        v(3, 48, FF),
+        v(3, 2, 48, HALF),
         v(3, 192, WIDTH),
+        v(3, 3, 2, 48, BLK),
         v(3, 48, WIDTH),
-        v(3, 48, WIDTH),
+        v(3, 2, 2, 48, BLK),
+        v(2, 48, WIDTH),
+        v(3, 4, 2, 48, BLK),
+        v(4, 48, WIDTH),
+        v(16, 48, 2 * BLK),
+        v(4, 48, WIDTH),
+        v(4, 48, WIDTH),
         v(2, 48, WIDTH),
         v(2, 48, WIDTH),
-        v(4, 48, WIDTH),
-        v(4, 48, WIDTH),
-        v(16, 48, 2 * BLK),
-        v(PEERS, 48, WIDTH),
-        v(PEERS, 48, WIDTH),
         v(PEERS, 48, 2 * BLK),
         v(PEERS, ROWS, 2 * HD),
         v(PEERS, ROWS, 2 * HD),
@@ -870,21 +1095,13 @@
         v(ROWS, WIDTH),
         pltpu.SemaphoreType.DMA((SEMS,)),
         pltpu.SemaphoreType.DMA((SEMS,)),
-        pltpu.SemaphoreType.DMA((16,)),
+        pltpu.SemaphoreType.DMA((32,)),
     ]
     outs = pl.pallas_call(
         layer_kernel,
-        out_shape=(
-            jax.ShapeDtypeStruct((2, BLK, WIDTH), BF16),
-            jax.ShapeDtypeStruct((2, BLK, WIDTH), F32),
-            jax.ShapeDtypeStruct((48, WIDTH), F32),
-            jax.ShapeDtypeStruct((48, WIDTH), F32),
-            jax.ShapeDtypeStruct((48, 2 * BLK), F32),
-            jax.ShapeDtypeStruct((48, FF), F32),
-            jax.ShapeDtypeStruct((192, WIDTH), F32),
-        ),
-        in_specs=[smem, smem, vmem, vmem] + [hbm] * 6,
-        out_specs=(vmem,) * 7,
+        out_shape=shapes,
+        in_specs=[smem, smem, hbm, hbm] + [vmem] * 9 + [hbm] * 5,
+        out_specs=(hbm,) * 7,
         scratch_shapes=scratch,
         compiler_params=pltpu.CompilerParams(
             collective_id=0, has_side_effects=True, vmem_limit_bytes=62 * 2**20
@@ -894,39 +1111,55 @@
         block_map,
         tokens[0],
         cotangent[0],
-        vecs,
+        first_gain,
+        first_shift,
+        query_bias,
+        value_bias,
+        output_bias,
+        second_gain,
+        second_shift,
+        up_bias,
+        down_bias,
         query_weight,
         keyval_weight,
         output_weight,
         up_weight,
         down_weight,
     )
-    layer_out, input_grad, g_query, g_output, g_tail, g_up, g_down = outs
-    g_keyval = g_tail[:, : 2 * HD]
-
-    def column(k):
-        return g_tail[:, BLK + k]
-
-    g_value_bias = lax.dynamic_slice(g_tail[0], (BLK + HD + fs * 4,), (4,))
-    g_up_bias = g_tail[:, BLK : BLK + 4].T.reshape(192)
-    return (
-        layer_out[None],
-        input_grad[None],
-        column(8),
-        column(9),
-        g_query,
-        column(10),
-        g_keyval,
-        g_value_bias,
-        g_output,
-        column(7),
-        column(5),
-        column(6),
-        g_up,
-        g_up_bias,
-        g_down,
-        column(4),
-    )
+
+    def f(*shape):
+        return jax.ShapeDtypeStruct(shape, F32)
+
+    results = pl.pallas_call(
+        finish_kernel,
+        out_shape=(
+            shapes[0],
+            shapes[1],
+            f(48),
+            f(48),
+            f(48, WIDTH),
+            f(48),
+            f(48, 2 * HD),
+            f(4),
+            f(48, WIDTH),
+            f(48),
+            f(48),
+            f(48),
+            f(48, FF),
+            f(192),
+            f(192, WIDTH),
+            f(48),
+        ),
+        in_specs=[hbm] * 4 + [vmem] + [hbm] * 2,
+        out_specs=tuple(
+            hbm if i in (0, 1, 4, 8, 12, 14) else vmem for i in range(16)
+        ),
+        scratch_shapes=[
+            pltpu.VMEM(shapes[i].shape, shapes[i].dtype) for i in (1, 5, 6, 0, 2, 3)
+        ]
+        + [pltpu.SemaphoreType.DMA((12,))],
+    )(*outs)
+    return (results[0][None], results[1][None]) + tuple(results[2:])
 
 
 def solution(mesh):

time: 194 us -> 137 us (0.71)
  Pallas kernels: 175 us -> 136 us
  local copies, waits for them, and re-layouts: 17.7 us -> 0 us
    pallas_call x1 -> x2, Pallas kernels: 175 us -> 136 us  [the longest x1 132 us: shards(): pl.pallas_call(layer_kernel, out_shape=shapes, in_specs=[smem, smem, hbm,...]
    unnamed x38 -> x0, local copies, waits for them, and re-layouts: 12.1 us -> none
    slice x3 -> x0, local copies, waits for them, and re-layouts: 3.3 us -> none  [the longest x1 1.99 us: column(): return g_tail[:, BLK + k]]
where the time goes in v2:
time: 137 us
  Pallas kernels  136 us (99%)
  between operations  1.49 us (1%)
    pallas_call x1, Pallas kernels, shards(): pl.pallas_call(layer_kernel, out_shape=shapes, in_specs=[smem, smem, hbm,...  132 us
    pallas_call x1, Pallas kernels, shards(): pl.pallas_call(finish_kernel, out_shape=(shapes[0], shapes[1], f(48), f(4...  4.16 us

profile of v2, /device:TPU:0, one launch (start us, length us, event | category | flops | bytes accessed | tf_op | source)
XLA Modules:
  0.0 137.2 jit_solution(15500873875081114685)
XLA Ops:
  1.3 131.6 %shard_map.297 = (bf16[2,128,768]{2,1,0:T(8,128)(2,1)}, f32[2,128,768]{2,1,0:T(8,128)}, f32[48,768]{1,0:T(8,128)}, f32[48,768]{1,0:T(8,128)}, f32[48,256]{1,0:T(...) custom-call(s32[1]{0:T(128)S(6)} %copy.34.lengths, s32[16]{0:T(128)} %block_map.1, bf16[2,128,768]{2,1,0:T(8,128)(2,1)} %bitcast.5, ...), custom_call_target="tpu_custom_call" | custom-call | tf_op jit(solution)/shard_map/pallas_call | solution.py:1100
  132.9 4.2 %shard_map.298 = (bf16[2,128,768]{2,1,0:T(8,128)(2,1)}, f32[2,128,768]{2,1,0:T(8,128)}, f32[48]{0:T(128)}, f32[48]{0:T(128)}, f32[48,768]{1,0:T(8,128)}, /*index...) custom-call(bf16[2,128,768]{2,1,0:T(8,128)(2,1)} %get-tuple-element., ...), custom_call_target="tpu_custom_call" | custom-call | tf_op jit(solution)/shard_map/pallas_call | solution.py:1133

commit v3 on v2

--- a/solution.py
+++ b/solution.py
@@ -124,6 +124,20 @@
     rh_dn,
     f2_up,
     f2_dn,
+    fx,
+    fg,
+    fz,
+    fs_up,
+    fy,
+    fh,
+    fa,
+    g_r,
+    rc_r,
+    rz_r,
+    ry_r,
+    cx_r,
+    ch_r,
+    rc_t,
     r_t,
     cx_q,
     cx_o,
@@ -152,6 +166,7 @@
     xn_t,
     mixed_s,
     n2s,
+    n2_t,
     gos,
     mid,
     dup,
@@ -228,9 +243,8 @@
     got_tokens = keep(tokens_in, tokens)
     got_cotangent = keep(cotangent_in, cotangent)
     barrier = pltpu.get_barrier_semaphore()
-    greeted = [(peer(j), fs) for j in range(1, PEERS)]
-    greeted += [(ctx, shard_peer(k)) for k in range(1, 16)]
-    greeted += [z_far]
+    greeted = [(peer(j), fs) for j in (1, 2, 3, 4)]
+    greeted += [(ctx, shard_peer(k)) for k in (1, 2, 4, 8, 12)] + [z_far]
     for device in greeted:
         pl.semaphore_signal(barrier, inc=1, device_id=device, device_id_type=MESH)
 
@@ -325,11 +339,15 @@
             return []
 
     class Units(Whole):
-        def at(self, y, z, cols):
-            e = yy // 2 if y is yy else y
+        def at(self, e, z, cols, y=every):
             other = e + co - 2 * e * co
             lead = (1 - other) * co + 2 * other
-            return self.full.at[lead, yy % 2 if y is yy else every, z, self.rows, cols]
+            return self.full.at[lead, y, z, self.rows, cols]
+
+        def y(self):
+            src, dst = self.src.at[self.rows, self.src_cols], self.at(yy // 2, zl, self.fetch, yy % 2)
+            self.kept = keep(src, dst)
+            return [send(src, dst, y_peer(k)) for k in (1, 2, 3)]
 
         def z(self):
             self.kept.wait()
@@ -388,14 +406,14 @@
         )
 
     kvv = narrow(Whole(vecs, f_vec), Whole(wkv, f_kv))
-    wq_in, wo_in = wide(Whole(wq, f_q, (0, 256))), wide(Whole(wo, f_o, (0, 256)))
+    wq_in, wo_in = narrow(Whole(wq, f_q)), wide(Whole(wo, f_o, (0, 256)))
     dn_a, dn_b = (wide(Units(wdn, f_dn, (0, 256), pl.ds(96 * i, 96))) for i in (0, 1))
     up_a, up_b = up_chunk(0), up_chunk(1)
 
-    step(kvv, wq_in, wo_in)
-    step(kvv, dn_a)
-    step(wq_in, kvv, dn_b)
-    step(wo_in, kvv)
+    step(kvv, wq_in, wo_in, dn_a, dn_b, up_a, up_b)
+    step(kvv)
+    step(wq_in, kvv)
+    step(kvv)
     vec = f_vec[...].astype(F32).reshape(16, 16, WIDTH)
     vec = jnp.sum(vec, 0)
     gain1, shift1, qbias, obias = vec[0:1], vec[1:2], vec[2:3], vec[3:4]
@@ -410,12 +428,11 @@
     kv_all[0] = kv.astype(BF16)
     kv_copies = [send(kv_all.at[0], kv_all.at[j], (peer(j), fs)) for j in (1, 2, 3)]
     kv_far = send(kv_all.at[0], kv_all.at[4], h_peer)
-    step(wq_in, dn_a, up_a, wo_in)
+    step(wo_in, wq_in)
     arrived([kv_far])
     kv_copies += [send(kv_all.at[4], kv_all.at[4 + j], (peer(j), fs)) for j in (1, 2, 3)]
-    step(wq_in, dn_b, up_b, wq_in)
+    step(dn_a, wo_in, wq_in)
     go_copy = send(gos.at[0], gos.at[1], sib)
-    step(dn_a, wo_in)
 
     q = dot(xn[...], f_q[...].reshape(WIDTH, WIDTH)) + qbias
     q = (q.astype(BF16).astype(F32) * (HD**-0.5)).T
@@ -432,7 +449,7 @@
         q_rows[g] = both.T.astype(BF16)
 
     arrived(kv_copies)
-    step(up_a)
+    step(dn_b)
     lane = lax.broadcasted_iota(jnp.int32, (BLK, BLK), 1)
     sub = lax.broadcasted_iota(jnp.int32, (BLK, BLK), 0)
     extra = lax.broadcasted_iota(jnp.int32, (16, BLK), 0)
@@ -524,13 +541,11 @@
         return carry
 
     lax.fori_loop(0, 2, forward_group, 0)
-    step(dn_a, dn_b)
+    step(up_a, dn_a)
     lax.fori_loop(2, 4, forward_group, 0)
-    step(up_b, up_a)
+    step(dn_b, wo_in)
     lax.fori_loop(4, 6, forward_group, 0)
-    step(dn_b, up_a, up_b)
-
-    step(wo_in)
+    step(up_b, up_a, dn_a, wo_in)
     attended = att_t[...].reshape(WIDTH, ROWS).astype(F32).T.astype(BF16)
     mixed = x_low[...].astype(F32) + dot(attended, f_o[...].reshape(WIDTH, WIDTH)) + obias
     mixed_s[...] = mixed
@@ -538,10 +553,8 @@
     n2s[0] = (n2 * gain2 + shift2).astype(BF16)
     n2_copy = send(n2s.at[0], n2s.at[1], sib)
 
-    step(up_b)
-    arrived([go_copy])
-    step(dn_a, dn_b, up_a)
-    arrived([n2_copy])
+    step(dn_b, up_a, up_b)
+    arrived([go_copy, n2_copy])
 
     def unit_rows(j, start, size):
         blocks = []
@@ -552,38 +565,7 @@
             start, size = start + n, size - n
         return jnp.concatenate(blocks, 0)
 
-    sub_cols = 256
-    n_sub = HALF // sub_cols
     coef = 0.7978845608028654
-
-    up_sums = []
-    for s in range(n_sub):
-        cols = slice(s * sub_cols, (s + 1) * sub_cols)
-        per = WIDTH // sub_cols
-        if s == per:
-            step(up_b)
-        bias_row = jnp.where(co == 0, vec[8 + s // per : 9 + s // per], vec[10 + s // per : 11 + s // per])
-        bias = bias_row[:, (s % per) * sub_cols : (s % per + 1) * sub_cols]
-        n2b = n2s[...].reshape(2 * ROWS, WIDTH)
-        gob = gos[...].reshape(2 * ROWS, WIDTH)
-        up = dot(n2b, f_up[:, :, :, :, cols].reshape(WIDTH, sub_cols)) + bias
-        w_rows = unit_rows(s // per, (s % per) * sub_cols, sub_cols)
-        dmid = dot_nt(gob, w_rows)
-        square = up * up
-        th = jnp.tanh(coef * up * (1.0 + 0.044715 * square))
-        half_sum = 0.5 + 0.5 * th
-        mid[:, cols] = (up * half_sum).astype(BF16)
-        slope = half_sum + 0.5 * up * (1.0 - th * th) * coef * (1.0 + 3 * 0.044715 * square)
-        du = (dmid * slope).astype(BF16)
-        dup[:, cols] = du
-        up_sums.append(jnp.sum(du.astype(F32), 0, keepdims=True))
-
-    thirds = [slice(256 * n, 256 * (n + 1)) for n in range(3)]
-    for j in (0, 1):
-        m_t = mid[:, j * WIDTH : (j + 1) * WIDTH].astype(F32).T.astype(BF16)
-        for n in thirds:
-            piece = dot(m_t, gos[:, :, n].reshape(2 * ROWS, 256))
-            g_dn[j, :, :, :, n] = piece.astype(BF16).reshape(2, 2, 192, 256)
 
     def low_sum(own, *others):
         total = own.astype(F32)
@@ -592,33 +574,27 @@
         return total.astype(BF16)
 
     class Down:
-        def __init__(self, rows):
-            self.rows = rows
+        def __init__(self, j):
+            self.j = j
 
         def z(self):
-            rows = self.rows
-            return [send(g_dn.at[j, oz, :, rows], rz_dn.at[j, :, rows], z_of[j]) for j in (0, 1)]
+            halves_ = [(j, slice(96 * j, 96 * (j + 1))) for j in (0, 1)]
+            return [
+                send(g_dn.at[self.j, oz, :, rows], rz_dn.at[self.j, :, rows], z_of[e])
+                for e, rows in halves_
+            ]
 
         def c(self):
-            rows = self.rows
-            for j in (0, 1):
-                g_dn[j, zl, :, rows] = low_sum(g_dn[j, zl, :, rows], rz_dn[j, :, rows])
-                s_dn[2 * co + j, rows] = g_dn[j, zl, co, rows]
-            return [send(g_dn.at[:, zl, oc, rows], s_dn.at[pl.ds(2 * co, 2), rows], sib)]
+            j = self.j
+            g_dn[j, zl] = low_sum(g_dn[j, zl], rz_dn[j])
+            s_dn[2 * co + j] = g_dn[j, zl, co]
+            return [send(g_dn.at[j, zl, oc], s_dn.at[2 * co + j], sib)]
 
         def y(self):
-            rows = self.rows
-            return [
-                send(s_dn.at[(yy + k) % 4, rows], ry_dn.at[k - 1, rows], y_peer(k)) for k in (1, 2, 3)
-            ]
-
-        def y_sum(self):
-            rows = self.rows
-            s_dn[yy, rows] = low_sum(s_dn[yy, rows], *[ry_dn[k, rows] for k in range(3)])
-            return []
+            return [send(s_dn.at[(yy + k) % 4], ry_dn.at[k - 1], y_peer(k)) for k in (1, 2, 3)]
 
         def x(self):
-            self.y_sum()
+            s_dn[yy] = low_sum(s_dn[yy], *[ry_dn[k] for k in range(3)])
             return [
                 send(s_dn.at[yy, quarter_dn((xx + k) % 4)], rx_dn.at[k - 1], x_peer(k))
                 for k in (1, 2, 3)
@@ -635,60 +611,103 @@
     def quarter_dn(k):
         return pl.ds(pl.multiple_of(k * 48, 16), 48)
 
-    class Up:
-        def __init__(self, i):
-            self.i, self.cols = i, slice(512 * i, 512 * (i + 1))
+    class Near:
+        def __init__(self, j):
+            self.j, self.cols = j, slice(j * WIDTH + 512, (j + 1) * WIDTH)
 
         def quarter(self, k):
-            return pl.ds(pl.multiple_of(512 * self.i + k * BLK, BLK), BLK)
+            return k // 2, slice(None), pl.ds(pl.multiple_of((k % 2) * BLK, BLK), BLK)
 
         def z(self):
             return [
                 send(
                     g_up.at[pl.ds(2 * e, 2), oz, :, :, self.cols],
-                    rz_up.at[pl.ds(2 * e, 2), :, :, self.cols],
+                    rz_up.at[self.j, pl.ds(2 * e, 2)],
                     z_of[e],
                 )
                 for e in (0, 1)
             ]
 
         def c(self):
-            cols = self.cols
-            g_up[:, zl, :, :, cols] = low_sum(g_up[:, zl, :, :, cols], rz_up[:, :, :, cols])
-            s_up[:, co, :, cols] = g_up[:, zl, co, :, cols]
-            return [send(g_up.at[:, zl, oc, :, cols], s_up.at[:, co, :, cols], sib)]
+            cols, j = self.cols, self.j
+            g_up[:, zl, :, :, cols] = low_sum(g_up[:, zl, :, :, cols], rz_up[j])
+            s_up[j, :, co] = g_up[:, zl, co, :, cols]
+            return [send(g_up.at[:, zl, oc, :, cols], s_up.at[j, :, co], sib)]
 
         def y(self):
-            cols = self.cols
+            j = self.j
             return [
-                send(s_up.at[(yy + k) % 4, :, :, cols], ry_up.at[k - 1, :, :, cols], y_peer(k))
+                send(s_up.at[j, (yy + k) % 4], ry_up.at[j, k - 1], y_peer(k)) for k in (1, 2, 3)
+            ]
+
+        def x(self):
+            j = self.j
+            s_up[j, yy] = low_sum(s_up[j, yy], *[ry_up[j, k] for k in range(3)])
+            return [
+                send(s_up.at[(j, yy) + self.quarter((xx + k) % 4)], rx_up.at[j, k - 1], x_peer(k))
                 for k in (1, 2, 3)
             ]
 
+        def h(self):
+            j = self.j
+            rh_up[j, 1] = low_sum(s_up[(j, yy) + self.quarter(xx)], *[rx_up[j, k] for k in range(3)])
+            return [send(rh_up.at[j, 1], rh_up.at[j, 0], h_peer)]
+
+        def a(self):
+            ref = f2_up.at[self.j, xx]
+            f2_up[self.j, xx] = low_sum(rh_up[self.j, 0], rh_up[self.j, 1])
+            return [send(ref, ref, x_peer(k)) for k in (1, 2, 3)]
+
+    class Far:
+        def __init__(self, j):
+            self.j = j
+
+        def quarter(self, k):
+            return pl.ds(pl.multiple_of(self.j * WIDTH + k * BLK, BLK), BLK)
+
         def x(self):
-            cols = self.cols
-            s_up[yy, :, :, cols] = low_sum(
-                s_up[yy, :, :, cols], *[ry_up[k, :, :, cols] for k in range(3)]
-            )
             return [
-                send(s_up.at[yy, :, :, self.quarter((xx + k) % 4)], rx_up.at[self.i, k - 1], x_peer(k))
+                send(g_up.at[:, :, :, :, self.quarter((xx + k) % 4)], fx.at[self.j, k - 1], x_peer(k))
                 for k in (1, 2, 3)
             ]
 
+        def z(self):
+            j = self.j
+            fg[j] = low_sum(g_up[:, :, :, :, self.quarter(xx)], *[fx[j, k] for k in range(3)])
+            return [
+                send(fg.at[j, pl.ds(2 * e, 2), oz], fz.at[j, pl.ds(2 * e, 2)], z_of[e])
+                for e in (0, 1)
+            ]
+
+        def c(self):
+            j = self.j
+            fg[j, :, zl] = low_sum(fg[j, :, zl], fz[j])
+            fs_up[j, :, co] = fg[j, :, zl, co]
+            return [send(fg.at[j, :, zl, oc], fs_up.at[j, :, co], sib)]
+
+        def y(self):
+            j = self.j
+            return [
+                send(fs_up.at[j, (yy + k) % 4], fy.at[j, k - 1], y_peer(k)) for k in (1, 2, 3)
+            ]
+
         def h(self):
-            got = [rx_up[self.i, k] for k in range(3)]
-            rh_up[self.i, 1] = low_sum(s_up[yy, :, :, self.quarter(xx)], *got)
-            return [send(rh_up.at[self.i, 1], rh_up.at[self.i, 0], h_peer)]
+            j = self.j
+            fh[j, 1] = low_sum(fs_up[j, yy], *[fy[j, k] for k in range(3)])
+            return [send(fh.at[j, 1], fh.at[j, 0], h_peer)]
 
         def a(self):
-            f2_up[self.i, xx] = low_sum(rh_up[self.i, 0], rh_up[self.i, 1])
-            ref = f2_up.at[self.i, xx]
+            ref = fa.at[self.j, xx]
+            fa[self.j, xx] = low_sum(fh[self.j, 0], fh[self.j, 1])
             return [send(ref, ref, x_peer(k)) for k in (1, 2, 3)]
 
-    down = [Down(slice(96 * i, 96 * (i + 1))) for i in (0, 1)]
-    down_a = Chain(down[0].z, down[0].c, down[0].y, down[0].y_sum)
-    down_b = Chain(down[1].z, down[1].c, down[1].y, down[1].x, down[1].h, down[1].a)
-    ups = [Chain(u.z, u.c, u.y, u.x, u.h, u.a) for u in map(Up, range(3))]
+    down = [Down(j) for j in (0, 1)]
+    downs = [
+        Chain(down[0].z, down[0].c),
+        Chain(down[1].z, down[1].c, down[1].y, down[1].x, down[1].h, down[1].a),
+    ]
+    nears = [Chain(u.z, u.c, u.y, u.x, u.h, u.a) for u in map(Near, (0, 1))]
+    fars = [Chain(u.x, u.z, u.c, u.y, u.h, u.a) for u in map(Far, (0, 1))]
 
     def square(grad, rc, rz, ry, cx, ch):
         def c():
@@ -717,23 +736,83 @@
 
         return Chain(c, z, y, x, h)
 
+    def direct(grad, rc, got, shares):
+        def c():
+            return [send(grad.at[:, :, oc], rc, sib)]
+
+        def group():
+            grad[:, :, co] = low_sum(grad[:, :, co], rc[...])
+            out = []
+            for k in range(1, 8):
+                dst = shard_peer(2 * k)
+                out.append(send(grad.at[dst // 4, (dst // 2) % 2, co], got.at[k], (ctx, dst)))
+            return out
+
+        def peers():
+            shares[0] = low_sum(grad[yy, zl, co], *[got[k] for k in range(1, 8)])
+            return [send(shares.at[0], shares.at[j], (peer(j), fs)) for j in range(1, PEERS)]
+
+        return Chain(c, group, peers)
+
+    def total_of(shares, n):
+        total = shares[0].astype(F32)
+        for j in range(1, n):
+            total = total + shares[j].astype(F32)
+        return total
+
     out_w = square(g_o, rc_o, rz_o, ry_o, cx_o, ch_o)
-    query_w = square(g_q, rc_q, rz_q, ry_q, cx_q, ch_q)
-
-    step(down_a)
+    query_a = square(g_q, rc_q, rz_q, ry_q, cx_q, ch_q)
+    query_b = square(g_r, rc_r, rz_r, ry_r, cx_r, ch_r)
+    tail = direct(g_t, rc_t, r_t, c_t)
+
+    thirds = [slice(256 * n, 256 * (n + 1)) for n in range(3)]
+    n2_t[...] = n2s[...].reshape(2 * ROWS, WIDTH).astype(F32).T.astype(BF16)
+    up_sums = []
+
+    def middle(j):
+        for n in thirds:
+            cols = slice(j * WIDTH + n.start, j * WIDTH + n.stop)
+            bias = jnp.where(co == 0, vec[8 + j : 9 + j, n], vec[10 + j : 11 + j, n])
+            n2b = n2s[...].reshape(2 * ROWS, WIDTH)
+            gob = gos[...].reshape(2 * ROWS, WIDTH)
+            up = dot(n2b, f_up[:, :, :, :, cols].reshape(WIDTH, 256)) + bias
+            dmid = dot_nt(gob, unit_rows(j, n.start, 256))
+            square = up * up
+            th = jnp.tanh(coef * up * (1.0 + 0.044715 * square))
+            half_sum = 0.5 + 0.5 * th
+            mid[:, cols] = (up * half_sum).astype(BF16)
+            slope = half_sum + 0.5 * up * (1.0 - th * th) * coef * (1.0 + 3 * 0.044715 * square)
+            du = (dmid * slope).astype(BF16)
+            dup[:, cols] = du
+            up_sums.append(jnp.sum(du.astype(F32), 0, keepdims=True))
+
+    def weight_grads(j):
+        m_t = mid[:, j * WIDTH : (j + 1) * WIDTH].astype(F32).T.astype(BF16)
+        for n in thirds:
+            piece = dot(m_t, gos[:, :, n].reshape(2 * ROWS, 256))
+            g_dn[j, :, :, :, n] = piece.astype(BF16).reshape(2, 2, 192, 256)
+        step(downs[j])
+        for n in thirds:
+            cols = slice(j * WIDTH + n.start, j * WIDTH + n.stop)
+            piece = dot(n2_t[...], dup[:, cols])
+            g_up[:, :, :, :, cols] = piece.astype(BF16).reshape(4, 2, 2, 48, 256)
+            if n.stop == 512:
+                step(fars[j])
+        step(nears[j])
+
+    step(dn_a, dn_b, up_a)
+    middle(0)
+    step(up_b)
+    weight_grads(0)
+    step(up_b)
+    middle(1)
     for n in thirds:
         w = f_up[...].reshape(WIDTH, HALF)[n]
         piece = dot_nt(dup[...], w)
         dsec_own[:, n] = piece[:ROWS]
         dsec_out[:, n] = piece[ROWS:].astype(BF16)
     dsec_copy = send(dsec_out, dsec_in, sib)
-
-    n2_t = n2s[...].reshape(2 * ROWS, WIDTH).astype(F32).T.astype(BF16)
-    for s in range(n_sub):
-        cols = slice(s * sub_cols, (s + 1) * sub_cols)
-        piece = dot(n2_t, dup[:, cols])
-        g_up[:, :, :, :, cols] = piece.astype(BF16).reshape(4, 2, 2, 48, sub_cols)
-    step(down_b)
+    weight_grads(1)
 
     arrived([dsec_copy])
     dsec = dsec_own[...] + dsec_in[...].astype(F32)
@@ -775,7 +854,7 @@
 
     acc[...] = jnp.zeros_like(acc)
 
-    def backward_group(g, carry):
+    def backward_group(g, carry, query=True):
         acc[:, BLK:ROWS] += dot(probs[g], do_rows[g])
         delta_h, delta_l = l_inv[g, 0:1], l_inv[g, 8:9]
         score[...] = dot(v_both[...], do_both[g])
@@ -788,20 +867,28 @@
             else:
                 delta = delta_l
             probs[g, rows] = (probs[g, rows].astype(F32) * (score[rows] - delta)).astype(BF16)
+        acc[:, 0:BLK] += dot(probs[g], q_rows[g])
+        if query:
+            query_grad(g)
+        return carry
+
+    def query_grad(g):
         dq = dot(kt_both[...], probs[g]) * (HD**-0.5)
         do_both[g, 0:HD, 0:BLK] = dq[HD:, :BLK].astype(BF16)
         do_both[g, 0:HD, BLK:ROWS] = dq[:HD, :BLK].astype(BF16)
         do_both[g, HD:BLK, 0:BLK] = dq[HD:, BLK:].astype(BF16)
         do_both[g, HD:BLK, BLK:ROWS] = dq[:HD, BLK:].astype(BF16)
-        acc[:, 0:BLK] += dot(probs[g], q_rows[g])
-        return carry
-
+
+    step(downs[0])
     lax.fori_loop(0, 2, backward_group, 0)
-    step(out_w)
+    step(nears[0], fars[0], out_w)
     lax.fori_loop(2, 4, backward_group, 0)
-    step(down_a, ups[0])
-    lax.fori_loop(4, 6, backward_group, 0)
-    step(down_a)
+    dq_a = do_both[0:4].reshape(512, ROWS).astype(F32).T
+    sum_qa = jnp.sum(dq_a, 0, keepdims=True)
+    dq_a = dq_a.astype(BF16)
+    g_q[...] = dot(xn_t[...], dq_a).astype(BF16).reshape(4, 2, 2, 48, 512)
+    step(query_a, nears[0])
+    lax.fori_loop(4, 6, functools.partial(backward_group, query=False), 0)
 
     def halves(item, second):
         rows = slice(item * BLK, (item + 1) * BLK)
@@ -819,40 +906,28 @@
         dkv_out[j, BLK:ROWS] = (pick * other).astype(BF16)
         dkv_copies.append(send(dkv_out.at[j], dkv_in.at[j], (from_peer(j), fs)))
 
-    dq = do_both[...].reshape(WIDTH, ROWS).astype(F32).T
-    sum_qbias = jnp.sum(dq, 0, keepdims=True)
-    dq = dq.astype(BF16)
-    g_q[...] = dot(xn_t[...], dq).astype(BF16).reshape(4, 2, 2, 48, WIDTH)
-    step(query_w, down_b, ups[1])
-    dfirst = dot_nt(dq, f_q[...].reshape(WIDTH, WIDTH))
-
-    step(query_w, down_b, out_w, down_a, ups[0], ups[2])
-
-    top = halves(0, False) + halves(N_A + N_B + 1, True)
-    dkv = jnp.concatenate([top, halves(N_A + N_B, False)], 0)
-    arrived(dkv_copies)
-    for j in range(1, PEERS):
-        dkv = dkv + dkv_in[j].astype(F32)
-    dkv = dkv.astype(BF16)
-    sum_kv = jnp.sum(dkv.astype(F32), 0, keepdims=True)
-    g_kv = dot(xn_t[...], dkv)
-    dfirst = dfirst + dot_nt(dkv, f_kv[...].reshape(WIDTH, 2 * HD))
-
-    n1, rate1 = normalize(x_low[...].astype(F32))
-    sum_gain1 = jnp.sum(dfirst * n1, 0, keepdims=True)
-    sum_shift1 = jnp.sum(dfirst, 0, keepdims=True)
+    query_grad(4)
+    query_grad(5)
+    dq_b = do_both[4:6].reshape(256, ROWS).astype(F32).T
+    sum_qbias = jnp.concatenate([sum_qa, jnp.sum(dq_b, 0, keepdims=True)], 1)
+    dq_b = dq_b.astype(BF16)
+    g_r[...] = dot(xn_t[...], dq_b).astype(BF16).reshape(4, 2, 2, 48, 256)
+    step(query_b)
+    step(downs[1], downs[0], fars[1], query_a)
+    dfirst = dot_nt(dq_a, f_q[:, :, :, :, 0:512].reshape(WIDTH, 512))
+    dfirst = dfirst + dot_nt(dq_b, f_q[:, :, :, :, 512:WIDTH].reshape(WIDTH, 256))
 
     zeros = jnp.zeros((1, WIDTH), F32)
-    columns = jnp.concatenate(
-        [zeros] * 4
-        + [sum_dbias, sum_gain2, sum_shift2, sum_obias, sum_gain1, sum_shift1, sum_qbias]
-        + [jnp.zeros((BLK - 11, WIDTH), F32)],
-        0,
-    ).T
-    lanes = lax.broadcasted_iota(jnp.int32, (WIDTH, BLK), 1)
-    columns = jnp.where(lanes < HD, columns, sum_kv)
-    g_t[:, :, :, :, 0:BLK] = g_kv.astype(BF16).reshape(4, 2, 2, 48, BLK)
-    g_t[:, :, :, :, BLK:ROWS] = columns.astype(BF16).reshape(4, 2, 2, 48, BLK)
+    g_t[:, :, :, :, BLK:ROWS] = (
+        jnp.concatenate(
+            [zeros] * 4
+            + [sum_dbias, sum_gain2, sum_shift2, sum_obias, zeros, zeros, sum_qbias]
+            + [jnp.zeros((BLK - 11, WIDTH), F32)],
+            0,
+        )
+        .T.astype(BF16)
+        .reshape(4, 2, 2, 48, BLK)
+    )
     lanes = lax.broadcasted_iota(jnp.int32, (48, BLK), 1)
     for j in (0, 1):
         sums = jnp.concatenate(up_sums[3 * j : 3 * j + 3], 1)
@@ -864,14 +939,32 @@
                 block = jnp.where(lanes == r, sums[at : at + 48], block)
             g_t[2 * co + j, k // 2, k % 2, :, BLK:ROWS] = block.astype(BF16)
 
-    t_copies = []
-    for k in range(1, 16):
-        dst = shard_peer(k)
-        t_copies.append(
-            send(g_t.at[dst // 4, (dst // 2) % 2, dst % 2], r_t.at[k], (ctx, dst))
-        )
-
-    step(ups[0], down_b, query_w, out_w)
+    step(fars[0], nears[1], query_b, downs[1], nears[0], fars[0], nears[1], out_w, fars[1], query_a)
+
+    top = halves(0, False) + halves(N_A + N_B + 1, True)
+    dkv = jnp.concatenate([top, halves(N_A + N_B, False)], 0)
+    arrived(dkv_copies)
+    for j in range(1, PEERS):
+        dkv = dkv + dkv_in[j].astype(F32)
+    dkv = dkv.astype(BF16)
+    sum_kv = jnp.sum(dkv.astype(F32), 0, keepdims=True)
+    g_kv = dot(xn_t[...], dkv)
+    dfirst = dfirst + dot_nt(dkv, f_kv[...].reshape(WIDTH, 2 * HD))
+
+    n1, rate1 = normalize(x_low[...].astype(F32))
+    sum_gain1 = jnp.sum(dfirst * n1, 0, keepdims=True)
+    sum_shift1 = jnp.sum(dfirst, 0, keepdims=True)
+
+    columns = jnp.concatenate(
+        [zeros] * 8 + [sum_gain1, sum_shift1] + [jnp.zeros((BLK - 10, WIDTH), F32)], 0
+    ).T
+    lanes = lax.broadcasted_iota(jnp.int32, (WIDTH, BLK), 1)
+    known = g_t[:, :, :, :, BLK:ROWS].reshape(WIDTH, BLK).astype(F32)
+    columns = jnp.where((lanes == 8) | (lanes == 9), columns, known)
+    columns = jnp.where(lanes < HD, columns, sum_kv)
+    g_t[:, :, :, :, 0:BLK] = g_kv.astype(BF16).reshape(4, 2, 2, 48, BLK)
+    g_t[:, :, :, :, BLK:ROWS] = columns.astype(BF16).reshape(4, 2, 2, 48, BLK)
+    step(tail)
 
     ing = cotangent[...].reshape(ROWS, WIDTH) + norm_back(n1, rate1, dfirst, gain1)
     cotangent[0] = jnp.where(swap, ing[BLK:], ing[:BLK])
@@ -883,40 +976,35 @@
     tokens[1] = jnp.where(swap, res[:BLK], res[BLK:]).astype(BF16)
     done.append(keep(tokens, out_hbm))
 
-    step(ups[1], ups[0], ups[1], down_b, out_w)
-
-    arrived(t_copies)
-    total = g_t[yy, zl, co].astype(F32)
-    for k in range(1, 16):
-        total = total + r_t[k].astype(F32)
-    c_t[0] = total.astype(BF16)
-    ctx_t = [send(c_t.at[0], c_t.at[j], (peer(j), fs)) for j in range(1, PEERS)]
-
-    step(ups[2], ups[2], query_w, ups[0], ups[1], down_b, query_w, ups[0], ups[2])
-    step(out_w, ups[1], ups[2], query_w, ups[1], ups[2], ups[2])
-
-    go_ref[...] = ch_o[0].astype(F32) + ch_o[1].astype(F32)
+    step(tail, query_b, fars[1], out_w, downs[1], nears[0], fars[0], nears[1], query_a, query_b, out_w)
+    step(tail)
+    step(fars[1], downs[1], nears[0], nears[1], fars[0], query_a, query_b)
+    step(downs[1], nears[1], fars[1], query_b)
+    step(out_w)
+    go_ref[...] = total_of(ch_o, 2)
     done.append(keep(go_ref, go_hbm))
-    step(down_b)
+    step(downs[1], nears[1], fars[1], query_a)
+    step(query_b)
+    gq_ref[:, 0:512] = total_of(ch_q, 2)
+    gq_ref[:, 512:WIDTH] = total_of(ch_r, 2)
+    done.append(keep(gq_ref, gq_hbm))
+    step(fars[0], nears[0], downs[1])
     gdn_ref[...] = f2_dn[...].astype(F32).reshape(192, WIDTH)
     done.append(keep(gdn_ref, gdn_hbm))
-    step(*ups)
-    for i in range(3):
+    step(nears[1], fars[1])
+    for j in (0, 1):
         for k in range(4):
+            at = (k // 2) * HALF + j * WIDTH + 512 + (k % 2) * BLK
+            gup_ref[:, at : at + BLK] = f2_up[j, k].astype(F32)
             for half in (0, 1):
-                at = half * HALF + 512 * i + k * BLK
-                gup_ref[:, at : at + BLK] = f2_up[i, k, half].astype(F32)
+                at = half * HALF + j * WIDTH + k * BLK
+                gup_ref[:, at : at + BLK] = fa[j, k, half].astype(F32)
     done.append(keep(gup_ref, gup_hbm))
-    arrived(ctx_t)
-    total = c_t[0].astype(F32)
-    for j in range(1, PEERS):
-        total = total + c_t[j].astype(F32)
-    gt_ref[...] = total
+    step(tail)
+    gt_ref[...] = total_of(c_t, PEERS)
     done.append(keep(gt_ref, gt_hbm))
-    step(query_w)
-    gq_ref[...] = ch_q[0].astype(F32) + ch_q[1].astype(F32)
-    done.append(keep(gq_ref, gq_hbm))
-    for chain in (kvv, wq_in, wo_in, dn_a, dn_b, up_a, up_b, down_a, down_b, out_w, query_w, *ups):
+    gathers = (kvv, wq_in, wo_in, dn_a, dn_b, up_a, up_b)
+    for chain in gathers + (out_w, query_a, query_b, tail, *downs, *nears, *fars):
         assert not chain.steps and not chain.flying
     for copy in done:
         copy.wait()
@@ -1034,33 +1122,47 @@
         v(4, 2, 2, 48, HALF),
         v(4, 2, 48, HALF),
         v(3, 2, 2, 192, WIDTH),
-        v(4, 2, 2, 48, WIDTH),
+        v(4, 2, 2, 48, 512),
         v(4, 2, 2, 48, WIDTH),
         v(4, 2, 2, 48, 2 * BLK),
         v(4, 2, 2, 48, HALF),
         v(2, 2, 2, 192, WIDTH),
+        v(4, 2, 48, 512),
         v(4, 2, 48, WIDTH),
-        v(4, 2, 48, WIDTH),
+        v(4, 48, 512),
         v(4, 48, WIDTH),
+        v(2, 4, 2, 48, 256),
+        v(2, 2, 192, WIDTH),
+        v(2, 4, 2, 48, 256),
+        v(4, 192, WIDTH),
+        v(3, 48, 512),
+        v(3, 48, WIDTH),
+        v(2, 3, 2, 48, 256),
+        v(3, 192, WIDTH),
+        v(2, 3, 48, BLK),
+        v(3, 48, WIDTH),
+        v(2, 2, 48, BLK),
+        v(2, 48, WIDTH),
+        v(2, 4, 48, BLK),
         v(4, 48, WIDTH),
-        v(4, 2, 48, HALF),
-        v(2, 2, 192, WIDTH),
-        v(4, 2, 48, HALF),
-        v(4, 192, WIDTH),
-        v(3, 48, WIDTH),
-        v(3, 48, WIDTH),
-        v(3, 2, 48, HALF),
-        v(3, 192, WIDTH),
-        v(3, 3, 2, 48, BLK),
-        v(3, 48, WIDTH),
-        v(3, 2, 2, 48, BLK),
-        v(2, 48, WIDTH),
-        v(3, 4, 2, 48, BLK),
+        v(2, 3, 4, 2, 2, 48, BLK),
+        v(2, 4, 2, 2, 48, BLK),
+        v(2, 4, 2, 48, BLK),
+        v(2, 4, 2, 48, BLK),
+        v(2, 3, 2, 48, BLK),
+        v(2, 2, 2, 48, BLK),
+        v(2, 4, 2, 48, BLK),
+        v(4, 2, 2, 48, 256),
+        v(4, 2, 48, 256),
+        v(4, 48, 256),
+        v(3, 48, 256),
+        v(4, 48, 256),
+        v(2, 48, 256),
+        v(4, 2, 48, 256),
+        v(8, 48, 2 * BLK),
+        v(4, 48, 512),
         v(4, 48, WIDTH),
-        v(16, 48, 2 * BLK),
-        v(4, 48, WIDTH),
-        v(4, 48, WIDTH),
-        v(2, 48, WIDTH),
+        v(2, 48, 512),
         v(2, 48, WIDTH),
         v(PEERS, 48, 2 * BLK),
         v(PEERS, ROWS, 2 * HD),
@@ -1085,6 +1187,7 @@
         v(WIDTH, ROWS),
         v(ROWS, WIDTH, dtype=F32),
         v(2, ROWS, WIDTH),
+        v(WIDTH, 2 * ROWS),
         v(2, ROWS, WIDTH),
         v(2 * ROWS, HALF),
         v(2 * ROWS, HALF),

time: 137 us -> 134 us (0.978)
  Pallas kernels: 136 us -> 132 us
    pallas_call x1, Pallas kernels: 132 us -> 128 us  [shards(): pl.pallas_call(layer_kernel, out_shape=shapes, in_specs=[smem, smem, hbm,...]
where the time goes in v3:
time: 134 us; the launch traced here: 133 us
  Pallas kernels  132 us (99%)
  between operations  1.49 us (1%)
    pallas_call x1, Pallas kernels, shards(): pl.pallas_call(layer_kernel, out_shape=shapes, in_specs=[smem, smem, hbm,...  128 us
    pallas_call x1, Pallas kernels, shards(): pl.pallas_call(finish_kernel, out_shape=(shapes[0], shapes[1], f(48), f(4...  4.16 us

profile of v3, /device:TPU:0, one launch (start us, length us, event | category | flops | bytes accessed | tf_op | source)
XLA Modules:
  0.0 133.5 jit_solution(15772564169554283132)
XLA Ops:
  1.3 127.8 %shard_map.297 = (bf16[2,128,768]{2,1,0:T(8,128)(2,1)}, f32[2,128,768]{2,1,0:T(8,128)}, f32[48,768]{1,0:T(8,128)}, f32[48,768]{1,0:T(8,128)}, f32[48,256]{1,0:T(...) custom-call(s32[1]{0:T(128)S(6)} %copy.34.lengths, s32[16]{0:T(128)} %block_map.1, bf16[2,128,768]{2,1,0:T(8,128)(2,1)} %bitcast.5, ...), custom_call_target="tpu_custom_call" | custom-call | tf_op jit(solution)/shard_map/pallas_call | solution.py:1203
  129.1 4.2 %shard_map.298 = (bf16[2,128,768]{2,1,0:T(8,128)(2,1)}, f32[2,128,768]{2,1,0:T(8,128)}, f32[48]{0:T(128)}, f32[48]{0:T(128)}, f32[48,768]{1,0:T(8,128)}, /*index...) custom-call(bf16[2,128,768]{2,1,0:T(8,128)(2,1)} %get-tuple-element., ...), custom_call_target="tpu_custom_call" | custom-call | tf_op jit(solution)/shard_map/pallas_call | solution.py:1236

commit v4 on v3

--- a/solution.py
+++ b/solution.py
@@ -127,10 +127,8 @@
     fx,
     fg,
     fz,
-    fs_up,
+    fs_dn,
     fy,
-    fh,
-    fa,
     g_r,
     rc_r,
     rz_r,
@@ -287,6 +285,7 @@
     got_cotangent.wait()
     gos[0] = grad_out().astype(BF16)
 
+    n1, _ = normalize(x_low[...].astype(F32))
     pl.semaphore_wait(barrier, len(greeted))
 
     def thirds_of(start, width):
@@ -419,20 +418,18 @@
     gain1, shift1, qbias, obias = vec[0:1], vec[1:2], vec[2:3], vec[3:4]
     gain2, shift2, dbias, kvbias = vec[4:5], vec[5:6], vec[6:7], vec[7:8, 0 : 2 * HD]
 
-    n1, _ = normalize(x_low[...].astype(F32))
     xn_v = n1 * gain1 + shift1
     xn[...] = xn_v.astype(BF16)
-    xn_t[...] = xn_v.T.astype(BF16)
 
     kv = dot(xn[...], f_kv[...].reshape(WIDTH, 2 * HD)) + kvbias
     kv_all[0] = kv.astype(BF16)
     kv_copies = [send(kv_all.at[0], kv_all.at[j], (peer(j), fs)) for j in (1, 2, 3)]
     kv_far = send(kv_all.at[0], kv_all.at[4], h_peer)
+    xn_t[...] = xn[...].astype(F32).T.astype(BF16)
     step(wo_in, wq_in)
     arrived([kv_far])
     kv_copies += [send(kv_all.at[4], kv_all.at[4 + j], (peer(j), fs)) for j in (1, 2, 3)]
-    step(dn_a, wo_in, wq_in)
-    go_copy = send(gos.at[0], gos.at[1], sib)
+    step(wq_in)
 
     q = dot(xn[...], f_q[...].reshape(WIDTH, WIDTH)) + qbias
     q = (q.astype(BF16).astype(F32) * (HD**-0.5)).T
@@ -447,6 +444,9 @@
         )
         q_both[g] = both.astype(BF16)
         q_rows[g] = both.T.astype(BF16)
+
+    step(dn_a, wo_in)
+    go_copy = send(gos.at[0], gos.at[1], sib)
 
     arrived(kv_copies)
     step(dn_b)
@@ -540,8 +540,9 @@
         att_t[g, HD:BLK, BLK:ROWS] = high[:, BLK:].astype(BF16)
         return carry
 
+    step(dn_a)
     lax.fori_loop(0, 2, forward_group, 0)
-    step(up_a, dn_a)
+    step(up_a)
     lax.fori_loop(2, 4, forward_group, 0)
     step(dn_b, wo_in)
     lax.fori_loop(4, 6, forward_group, 0)
@@ -573,22 +574,22 @@
             total = total + other.astype(F32)
         return total.astype(BF16)
 
-    class Down:
-        def __init__(self, j):
-            self.j = j
-
-        def z(self):
-            halves_ = [(j, slice(96 * j, 96 * (j + 1))) for j in (0, 1)]
+    def corner(half, k):
+        rows = pl.ds(pl.multiple_of(96 * half + (k // 2) * 48, 16), 48)
+        return rows, pl.ds(pl.multiple_of((k % 2) * 384, BLK), 384)
+
+    class DownNear:
+        def z(self, j):
+            rows = [slice(48 * e, 48 * (e + 1)) for e in (0, 1)]
             return [
-                send(g_dn.at[self.j, oz, :, rows], rz_dn.at[self.j, :, rows], z_of[e])
-                for e, rows in halves_
+                send(g_dn.at[j, oz, :, r], rz_dn.at[j, :, r], z_of[e]) for e, r in enumerate(rows)
             ]
 
         def c(self):
-            j = self.j
-            g_dn[j, zl] = low_sum(g_dn[j, zl], rz_dn[j])
-            s_dn[2 * co + j] = g_dn[j, zl, co]
-            return [send(g_dn.at[j, zl, oc], s_dn.at[2 * co + j], sib)]
+            for j in (0, 1):
+                g_dn[j, zl, :, 0:96] = low_sum(g_dn[j, zl, :, 0:96], rz_dn[j])
+                s_dn[2 * co + j] = g_dn[j, zl, co, 0:96]
+            return [send(g_dn.at[:, zl, oc, 0:96], s_dn.at[pl.ds(2 * co, 2)], sib)]
 
         def y(self):
             return [send(s_dn.at[(yy + k) % 4], ry_dn.at[k - 1], y_peer(k)) for k in (1, 2, 3)]
@@ -596,118 +597,110 @@
         def x(self):
             s_dn[yy] = low_sum(s_dn[yy], *[ry_dn[k] for k in range(3)])
             return [
-                send(s_dn.at[yy, quarter_dn((xx + k) % 4)], rx_dn.at[k - 1], x_peer(k))
+                send(s_dn.at[(yy,) + corner(0, (xx + k) % 4)], rx_dn.at[k - 1], x_peer(k))
                 for k in (1, 2, 3)
             ]
 
         def h(self):
-            rh_dn[1] = low_sum(s_dn[yy, quarter_dn(xx)], *[rx_dn[k] for k in range(3)])
-            return [send(rh_dn.at[1], rh_dn.at[0], h_peer)]
-
-        def a(self):
-            f2_dn[xx] = low_sum(rh_dn[0], rh_dn[1])
-            return [send(f2_dn.at[xx], f2_dn.at[xx], x_peer(k)) for k in (1, 2, 3)]
-
-    def quarter_dn(k):
-        return pl.ds(pl.multiple_of(k * 48, 16), 48)
-
-    class Near:
-        def __init__(self, j):
-            self.j, self.cols = j, slice(j * WIDTH + 512, (j + 1) * WIDTH)
+            rh_dn[0, 1] = low_sum(s_dn[(yy,) + corner(0, xx)], *[rx_dn[k] for k in range(3)])
+            return [send(rh_dn.at[0, 1], rh_dn.at[0, 0], h_peer)]
+
+        def a(self, i=0):
+            f2_dn[i, xx] = low_sum(rh_dn[i, 0], rh_dn[i, 1])
+            return [send(f2_dn.at[i, xx], f2_dn.at[i, xx], x_peer(k)) for k in (1, 2, 3)]
+
+    class DownFar:
+        def x(self, j):
+            return [
+                send(g_dn.at[(j, every, every) + corner(1, (xx + k) % 4)], fx.at[j, k - 1], x_peer(k))
+                for k in (1, 2, 3)
+            ]
+
+        def z(self):
+            for j in (0, 1):
+                own = g_dn[(j, every, every) + corner(1, xx)]
+                fg[j] = low_sum(own, *[fx[j, k] for k in range(3)])
+            return [send(fg.at[j, oz], fz.at[j], z_of[j]) for j in (0, 1)]
+
+        def c(self):
+            for j in (0, 1):
+                fg[j, zl] = low_sum(fg[j, zl], fz[j])
+                fs_dn[2 * co + j] = fg[j, zl, co]
+            return [send(fg.at[:, zl, oc], fs_dn.at[pl.ds(2 * co, 2)], sib)]
+
+        def y(self):
+            return [send(fs_dn.at[(yy + k) % 4], fy.at[k - 1], y_peer(k)) for k in (1, 2, 3)]
+
+        def h(self):
+            rh_dn[1, 1] = low_sum(fs_dn[yy], *[fy[k] for k in range(3)])
+            return [send(rh_dn.at[1, 1], rh_dn.at[1, 0], h_peer)]
+
+    class Up:
+        def __init__(self, j, start, width):
+            self.j, self.start, self.half = j, start, width // 2
+            self.cols = slice(start, start + width)
+            self.from_cols = slice(j * WIDTH + start, j * WIDTH + start + width)
+            self.quarter_cols = slice(start // 2, start // 2 + width // 2)
 
         def quarter(self, k):
-            return k // 2, slice(None), pl.ds(pl.multiple_of((k % 2) * BLK, BLK), BLK)
+            start = pl.multiple_of(self.start + (k % 2) * self.half, BLK)
+            return k // 2, every, pl.ds(start, self.half)
 
         def z(self):
             return [
                 send(
-                    g_up.at[pl.ds(2 * e, 2), oz, :, :, self.cols],
-                    rz_up.at[self.j, pl.ds(2 * e, 2)],
+                    g_up.at[pl.ds(2 * e, 2), oz, :, :, self.from_cols],
+                    rz_up.at[self.j, pl.ds(2 * e, 2), :, :, self.cols],
                     z_of[e],
                 )
                 for e in (0, 1)
             ]
 
         def c(self):
-            cols, j = self.cols, self.j
-            g_up[:, zl, :, :, cols] = low_sum(g_up[:, zl, :, :, cols], rz_up[j])
-            s_up[j, :, co] = g_up[:, zl, co, :, cols]
-            return [send(g_up.at[:, zl, oc, :, cols], s_up.at[j, :, co], sib)]
+            src, cols, j = self.from_cols, self.cols, self.j
+            g_up[:, zl, :, :, src] = low_sum(g_up[:, zl, :, :, src], rz_up[j, :, :, :, cols])
+            s_up[j, :, co, :, cols] = g_up[:, zl, co, :, src]
+            return [send(g_up.at[:, zl, oc, :, src], s_up.at[j, :, co, :, cols], sib)]
 
         def y(self):
-            j = self.j
+            j, cols = self.j, self.cols
             return [
-                send(s_up.at[j, (yy + k) % 4], ry_up.at[j, k - 1], y_peer(k)) for k in (1, 2, 3)
-            ]
-
-        def x(self):
-            j = self.j
-            s_up[j, yy] = low_sum(s_up[j, yy], *[ry_up[j, k] for k in range(3)])
-            return [
-                send(s_up.at[(j, yy) + self.quarter((xx + k) % 4)], rx_up.at[j, k - 1], x_peer(k))
+                send(s_up.at[j, (yy + k) % 4, :, :, cols], ry_up.at[j, k - 1, :, :, cols], y_peer(k))
                 for k in (1, 2, 3)
             ]
 
-        def h(self):
-            j = self.j
-            rh_up[j, 1] = low_sum(s_up[(j, yy) + self.quarter(xx)], *[rx_up[j, k] for k in range(3)])
-            return [send(rh_up.at[j, 1], rh_up.at[j, 0], h_peer)]
-
-        def a(self):
-            ref = f2_up.at[self.j, xx]
-            f2_up[self.j, xx] = low_sum(rh_up[self.j, 0], rh_up[self.j, 1])
-            return [send(ref, ref, x_peer(k)) for k in (1, 2, 3)]
-
-    class Far:
-        def __init__(self, j):
-            self.j = j
-
-        def quarter(self, k):
-            return pl.ds(pl.multiple_of(self.j * WIDTH + k * BLK, BLK), BLK)
-
         def x(self):
+            j, cols, part = self.j, self.cols, self.quarter_cols
+            s_up[j, yy, :, :, cols] = low_sum(
+                s_up[j, yy, :, :, cols], *[ry_up[j, k, :, :, cols] for k in range(3)]
+            )
             return [
-                send(g_up.at[:, :, :, :, self.quarter((xx + k) % 4)], fx.at[self.j, k - 1], x_peer(k))
+                send(
+                    s_up.at[(j, yy) + self.quarter((xx + k) % 4)],
+                    rx_up.at[j, k - 1, :, part],
+                    x_peer(k),
+                )
                 for k in (1, 2, 3)
             ]
 
-        def z(self):
-            j = self.j
-            fg[j] = low_sum(g_up[:, :, :, :, self.quarter(xx)], *[fx[j, k] for k in range(3)])
-            return [
-                send(fg.at[j, pl.ds(2 * e, 2), oz], fz.at[j, pl.ds(2 * e, 2)], z_of[e])
-                for e in (0, 1)
-            ]
-
-        def c(self):
-            j = self.j
-            fg[j, :, zl] = low_sum(fg[j, :, zl], fz[j])
-            fs_up[j, :, co] = fg[j, :, zl, co]
-            return [send(fg.at[j, :, zl, oc], fs_up.at[j, :, co], sib)]
-
-        def y(self):
-            j = self.j
-            return [
-                send(fs_up.at[j, (yy + k) % 4], fy.at[j, k - 1], y_peer(k)) for k in (1, 2, 3)
-            ]
-
         def h(self):
-            j = self.j
-            fh[j, 1] = low_sum(fs_up[j, yy], *[fy[j, k] for k in range(3)])
-            return [send(fh.at[j, 1], fh.at[j, 0], h_peer)]
+            j, part = self.j, self.quarter_cols
+            got = [rx_up[j, k, :, part] for k in range(3)]
+            rh_up[j, 1, :, part] = low_sum(s_up[(j, yy) + self.quarter(xx)], *got)
+            return [send(rh_up.at[j, 1, :, part], rh_up.at[j, 0, :, part], h_peer)]
 
         def a(self):
-            ref = fa.at[self.j, xx]
-            fa[self.j, xx] = low_sum(fh[self.j, 0], fh[self.j, 1])
+            j, part = self.j, self.quarter_cols
+            f2_up[j, xx, :, part] = low_sum(rh_up[j, 0, :, part], rh_up[j, 1, :, part])
+            ref = f2_up.at[j, xx, :, part]
             return [send(ref, ref, x_peer(k)) for k in (1, 2, 3)]
 
-    down = [Down(j) for j in (0, 1)]
-    downs = [
-        Chain(down[0].z, down[0].c),
-        Chain(down[1].z, down[1].c, down[1].y, down[1].x, down[1].h, down[1].a),
+    near, far = DownNear(), DownFar()
+    dn_near = Chain(near.c, near.y, near.x, near.h, near.a)
+    dn_far = Chain(far.z, far.c, far.y, far.h, functools.partial(near.a, 1))
+    ups = [
+        [Chain(u.z, u.c, u.y, u.x, u.h, u.a) for u in (Up(j, 0, 512), Up(j, 512, 256))] for j in (0, 1)
     ]
-    nears = [Chain(u.z, u.c, u.y, u.x, u.h, u.a) for u in map(Near, (0, 1))]
-    fars = [Chain(u.x, u.z, u.c, u.y, u.h, u.a) for u in map(Far, (0, 1))]
 
     def square(grad, rc, rz, ry, cx, ch):
         def c():
@@ -791,14 +784,15 @@
         for n in thirds:
             piece = dot(m_t, gos[:, :, n].reshape(2 * ROWS, 256))
             g_dn[j, :, :, :, n] = piece.astype(BF16).reshape(2, 2, 192, 256)
-        step(downs[j])
+        dn_near.flying += near.z(j)
+        dn_far.flying += far.x(j)
         for n in thirds:
             cols = slice(j * WIDTH + n.start, j * WIDTH + n.stop)
             piece = dot(n2_t[...], dup[:, cols])
             g_up[:, :, :, :, cols] = piece.astype(BF16).reshape(4, 2, 2, 48, 256)
             if n.stop == 512:
-                step(fars[j])
-        step(nears[j])
+                step(ups[j][0])
+        step(ups[j][1])
 
     step(dn_a, dn_b, up_a)
     middle(0)
@@ -831,13 +825,6 @@
         dot(att_t[...].reshape(WIDTH, ROWS), dmix_low).astype(BF16).reshape(4, 2, 2, 48, WIDTH)
     )
     step(out_w)
-
-    for n in thirds:
-        blocks = [f_dn[c, j, z, :, n] for j in (0, 1) for z in (0, 1) for c in (0, 1)]
-        piece = dot(mid[...], jnp.concatenate(blocks, 0))
-        dsec_own[:, n] = piece[:ROWS]
-        part_out[:, n] = piece[ROWS:].astype(BF16)
-    part_copy = send(part_out, part_in, sib)
 
     datt = dot(f_o[...].reshape(WIDTH, WIDTH), dmix_r.T.astype(BF16)).astype(BF16).astype(F32)
     deltas = []
@@ -879,15 +866,15 @@
         do_both[g, HD:BLK, 0:BLK] = dq[HD:, BLK:].astype(BF16)
         do_both[g, HD:BLK, BLK:ROWS] = dq[:HD, BLK:].astype(BF16)
 
-    step(downs[0])
+    step(ups[0][0])
     lax.fori_loop(0, 2, backward_group, 0)
-    step(nears[0], fars[0], out_w)
+    step(ups[0][1], ups[0][0], out_w)
     lax.fori_loop(2, 4, backward_group, 0)
     dq_a = do_both[0:4].reshape(512, ROWS).astype(F32).T
     sum_qa = jnp.sum(dq_a, 0, keepdims=True)
     dq_a = dq_a.astype(BF16)
     g_q[...] = dot(xn_t[...], dq_a).astype(BF16).reshape(4, 2, 2, 48, 512)
-    step(query_a, nears[0])
+    step(query_a, dn_near, dn_far, ups[0][1])
     lax.fori_loop(4, 6, functools.partial(backward_group, query=False), 0)
 
     def halves(item, second):
@@ -913,7 +900,14 @@
     dq_b = dq_b.astype(BF16)
     g_r[...] = dot(xn_t[...], dq_b).astype(BF16).reshape(4, 2, 2, 48, 256)
     step(query_b)
-    step(downs[1], downs[0], fars[1], query_a)
+    step(dn_near, ups[1][0], query_a, dn_far)
+    for n in thirds:
+        blocks = [f_dn[c, j, z, :, n] for j in (0, 1) for z in (0, 1) for c in (0, 1)]
+        piece = dot(mid[...], jnp.concatenate(blocks, 0))
+        dsec_own[:, n] = piece[:ROWS]
+        part_out[:, n] = piece[ROWS:].astype(BF16)
+    part_copy = send(part_out, part_in, sib)
+
     dfirst = dot_nt(dq_a, f_q[:, :, :, :, 0:512].reshape(WIDTH, 512))
     dfirst = dfirst + dot_nt(dq_b, f_q[:, :, :, :, 512:WIDTH].reshape(WIDTH, 256))
 
@@ -939,7 +933,7 @@
                 block = jnp.where(lanes == r, sums[at : at + 48], block)
             g_t[2 * co + j, k // 2, k % 2, :, BLK:ROWS] = block.astype(BF16)
 
-    step(fars[0], nears[1], query_b, downs[1], nears[0], fars[0], nears[1], out_w, fars[1], query_a)
+    step(ups[1][1], ups[0][0], ups[1][0], dn_far, query_b, out_w)
 
     top = halves(0, False) + halves(N_A + N_B + 1, True)
     dkv = jnp.concatenate([top, halves(N_A + N_B, False)], 0)
@@ -976,35 +970,38 @@
     tokens[1] = jnp.where(swap, res[:BLK], res[BLK:]).astype(BF16)
     done.append(keep(tokens, out_hbm))
 
-    step(tail, query_b, fars[1], out_w, downs[1], nears[0], fars[0], nears[1], query_a, query_b, out_w)
+    step(ups[0][1], ups[1][1], dn_near, ups[0][0], query_a)
+    step(tail, dn_far, ups[0][1], ups[1][0], query_b, out_w, ups[0][0], dn_near, ups[1][1], query_a)
     step(tail)
-    step(fars[1], downs[1], nears[0], nears[1], fars[0], query_a, query_b)
-    step(downs[1], nears[1], fars[1], query_b)
+    step(dn_far, ups[0][1], ups[1][0], dn_near, query_b, out_w, ups[1][1], query_a)
+    step(ups[1][0], query_b, ups[1][1])
     step(out_w)
     go_ref[...] = total_of(ch_o, 2)
     done.append(keep(go_ref, go_hbm))
-    step(downs[1], nears[1], fars[1], query_a)
+    step(ups[1][0], ups[1][1], query_a)
     step(query_b)
     gq_ref[:, 0:512] = total_of(ch_q, 2)
     gq_ref[:, 512:WIDTH] = total_of(ch_r, 2)
     done.append(keep(gq_ref, gq_hbm))
-    step(fars[0], nears[0], downs[1])
-    gdn_ref[...] = f2_dn[...].astype(F32).reshape(192, WIDTH)
+    step(dn_far, dn_near)
+    for half in (0, 1):
+        for k in range(4):
+            at, to = 96 * half + (k // 2) * 48, (k % 2) * 384
+            gdn_ref[at : at + 48, to : to + 384] = f2_dn[half, k].astype(F32)
     done.append(keep(gdn_ref, gdn_hbm))
-    step(nears[1], fars[1])
+    step(ups[0][0], ups[0][1], ups[1][0], ups[1][1])
     for j in (0, 1):
         for k in range(4):
-            at = (k // 2) * HALF + j * WIDTH + 512 + (k % 2) * BLK
-            gup_ref[:, at : at + BLK] = f2_up[j, k].astype(F32)
-            for half in (0, 1):
-                at = half * HALF + j * WIDTH + k * BLK
-                gup_ref[:, at : at + BLK] = fa[j, k, half].astype(F32)
+            for start, width in ((0, 256), (512, 128)):
+                at = (k // 2) * HALF + j * WIDTH + start + (k % 2) * width
+                got = f2_up[j, k, :, start // 2 : start // 2 + width]
+                gup_ref[:, at : at + width] = got.astype(F32)
     done.append(keep(gup_ref, gup_hbm))
     step(tail)
     gt_ref[...] = total_of(c_t, PEERS)
     done.append(keep(gt_ref, gt_hbm))
     gathers = (kvv, wq_in, wo_in, dn_a, dn_b, up_a, up_b)
-    for chain in gathers + (out_w, query_a, query_b, tail, *downs, *nears, *fars):
+    for chain in gathers + (out_w, query_a, query_b, tail, dn_near, dn_far, *ups[0], *ups[1]):
         assert not chain.steps and not chain.flying
     for copy in done:
         copy.wait()
@@ -1048,10 +1045,17 @@
     stages = (stage0, stage1, stage2, stage3, stage4, stage5)
     pairs = ((ing_in, ing), (gup_in, gup), (gdn_in, gdn), (out_in, out), (gq_in, gq), (go_in, go))
     loads, stores = [], []
-    for i, ((src, dst), stage) in enumerate(zip(pairs, stages)):
-        loads.append(pltpu.make_async_copy(src, stage, sems.at[i]))
-        stores.append(pltpu.make_async_copy(stage, dst, sems.at[6 + i]))
-        loads[i].start()
+    for (src, dst), stage in zip(pairs, stages):
+        if len(src.shape) == 3:
+            parts = [(i, pl.ds(64 * k, 64)) for i in (0, 1) for k in (0, 1)]
+        else:
+            size = src.shape[0] // 3
+            parts = [(pl.ds(size * k, size),) for k in range(3)]
+        for part in parts:
+            i = len(loads)
+            loads.append(pltpu.make_async_copy(src.at[part], stage.at[part], sems.at[i]))
+            stores.append(pltpu.make_async_copy(stage.at[part], dst.at[part], sems.at[20 + i]))
+            loads[i].start()
     fs = lax.axis_index("fsdp")
     gkv[...] = gt_in[:, 0:BLK]
     columns = gt_in[:, BLK : 2 * BLK]
@@ -1131,27 +1135,25 @@
         v(4, 2, 48, WIDTH),
         v(4, 48, 512),
         v(4, 48, WIDTH),
-        v(2, 4, 2, 48, 256),
-        v(2, 2, 192, WIDTH),
-        v(2, 4, 2, 48, 256),
-        v(4, 192, WIDTH),
+        v(2, 4, 2, 48, WIDTH),
+        v(2, 2, 96, WIDTH),
+        v(2, 4, 2, 48, WIDTH),
+        v(4, 96, WIDTH),
         v(3, 48, 512),
         v(3, 48, WIDTH),
-        v(2, 3, 2, 48, 256),
-        v(3, 192, WIDTH),
-        v(2, 3, 48, BLK),
-        v(3, 48, WIDTH),
-        v(2, 2, 48, BLK),
-        v(2, 48, WIDTH),
-        v(2, 4, 48, BLK),
-        v(4, 48, WIDTH),
-        v(2, 3, 4, 2, 2, 48, BLK),
-        v(2, 4, 2, 2, 48, BLK),
-        v(2, 4, 2, 48, BLK),
-        v(2, 4, 2, 48, BLK),
-        v(2, 3, 2, 48, BLK),
-        v(2, 2, 2, 48, BLK),
-        v(2, 4, 2, 48, BLK),
+        v(2, 3, 2, 48, WIDTH),
+        v(3, 96, WIDTH),
+        v(2, 3, 48, 384),
+        v(3, 48, 384),
+        v(2, 2, 48, 384),
+        v(2, 2, 48, 384),
+        v(2, 4, 48, 384),
+        v(2, 4, 48, 384),
+        v(2, 3, 2, 2, 48, 384),
+        v(2, 2, 2, 48, 384),
+        v(2, 2, 48, 384),
+        v(4, 48, 384),
+        v(3, 48, 384),
         v(4, 2, 2, 48, 256),
         v(4, 2, 48, 256),
         v(4, 48, 256),
@@ -1260,7 +1262,7 @@
         scratch_shapes=[
             pltpu.VMEM(shapes[i].shape, shapes[i].dtype) for i in (1, 5, 6, 0, 2, 3)
         ]
-        + [pltpu.SemaphoreType.DMA((12,))],
+        + [pltpu.SemaphoreType.DMA((40,))],
     )(*outs)
     return (results[0][None], results[1][None]) + tuple(results[2:])
 

time: 134 us -> 130 us (0.970)
  Pallas kernels: 132 us -> 128 us
    pallas_call x1, Pallas kernels: 128 us -> 124 us  [shards(): pl.pallas_call(layer_kernel, out_shape=shapes, in_specs=[smem, smem, hbm,...]
where the time goes in v4:
time: 130 us; the launch traced here: 129 us
  Pallas kernels  128 us (98%)
  between operations  1.49 us (1%)
    pallas_call x1, Pallas kernels, shards(): pl.pallas_call(layer_kernel, out_shape=shapes, in_specs=[smem, smem, hbm,...  124 us
    pallas_call x1, Pallas kernels, shards(): pl.pallas_call(finish_kernel, out_shape=(shapes[0], shapes[1], f(48), f(4...  4.29 us

profile of v4, /device:TPU:0, one launch (start us, length us, event | category | flops | bytes accessed | tf_op | source)
XLA Modules:
  0.0 129.3 jit_solution(11547586083732046744)
XLA Ops:
  1.3 123.5 %shard_map.297 = (bf16[2,128,768]{2,1,0:T(8,128)(2,1)}, f32[2,128,768]{2,1,0:T(8,128)}, f32[48,768]{1,0:T(8,128)}, f32[48,768]{1,0:T(8,128)}, f32[48,256]{1,0:T(...) custom-call(s32[1]{0:T(128)S(6)} %copy.34.lengths, s32[16]{0:T(128)} %block_map.1, bf16[2,128,768]{2,1,0:T(8,128)(2,1)} %bitcast.5, ...), custom_call_target="tpu_custom_call" | custom-call | tf_op jit(solution)/shard_map/pallas_call | solution.py:1205
  124.8 4.3 %shard_map.298 = (bf16[2,128,768]{2,1,0:T(8,128)(2,1)}, f32[2,128,768]{2,1,0:T(8,128)}, f32[48]{0:T(128)}, f32[48]{0:T(128)}, f32[48,768]{1,0:T(8,128)}, /*index...) custom-call(bf16[2,128,768]{2,1,0:T(8,128)(2,1)} %get-tuple-element., ...), custom_call_target="tpu_custom_call" | custom-call | tf_op jit(solution)/shard_map/pallas_call | solution.py:1238

commit v5 on v4

--- a/solution.py
+++ b/solution.py
@@ -546,7 +546,7 @@
     lax.fori_loop(2, 4, forward_group, 0)
     step(dn_b, wo_in)
     lax.fori_loop(4, 6, forward_group, 0)
-    step(up_b, up_a, dn_a, wo_in)
+    step(up_b, wo_in)
     attended = att_t[...].reshape(WIDTH, ROWS).astype(F32).T.astype(BF16)
     mixed = x_low[...].astype(F32) + dot(attended, f_o[...].reshape(WIDTH, WIDTH)) + obias
     mixed_s[...] = mixed
@@ -554,7 +554,7 @@
     n2s[0] = (n2 * gain2 + shift2).astype(BF16)
     n2_copy = send(n2s.at[0], n2s.at[1], sib)
 
-    step(dn_b, up_a, up_b)
+    step(up_a, dn_a, dn_b, up_a, up_b)
     arrived([go_copy, n2_copy])
 
     def unit_rows(j, start, size):
@@ -866,15 +866,14 @@
         do_both[g, HD:BLK, 0:BLK] = dq[HD:, BLK:].astype(BF16)
         do_both[g, HD:BLK, BLK:ROWS] = dq[:HD, BLK:].astype(BF16)
 
-    step(ups[0][0])
     lax.fori_loop(0, 2, backward_group, 0)
-    step(ups[0][1], ups[0][0], out_w)
+    step(ups[0][0], ups[0][1], ups[0][0], out_w)
     lax.fori_loop(2, 4, backward_group, 0)
     dq_a = do_both[0:4].reshape(512, ROWS).astype(F32).T
     sum_qa = jnp.sum(dq_a, 0, keepdims=True)
     dq_a = dq_a.astype(BF16)
     g_q[...] = dot(xn_t[...], dq_a).astype(BF16).reshape(4, 2, 2, 48, 512)
-    step(query_a, dn_near, dn_far, ups[0][1])
+    step(dn_far, dn_near, ups[0][1], query_a)
     lax.fori_loop(4, 6, functools.partial(backward_group, query=False), 0)
 
     def halves(item, second):

time: 130 us -> 129 us (level)
  no operation moved by 1% of the time
where the time goes in v5:
time: 129 us
  Pallas kernels  128 us (99%)
  between operations  1.49 us (1%)
    pallas_call x1, Pallas kernels, shards(): pl.pallas_call(layer_kernel, out_shape=shapes, in_specs=[smem, smem, hbm,...  123 us
    pallas_call x1, Pallas kernels, shards(): pl.pallas_call(finish_kernel, out_shape=(shapes[0], shapes[1], f(48), f(4...  4.29 us

profile of v5, /device:TPU:0, one launch (start us, length us, event | category | flops | bytes accessed | tf_op | source)
XLA Modules:
  0.0 129.2 jit_solution(3865365640363801822)
XLA Ops:
  1.3 123.4 %shard_map.297 = (bf16[2,128,768]{2,1,0:T(8,128)(2,1)}, f32[2,128,768]{2,1,0:T(8,128)}, f32[48,768]{1,0:T(8,128)}, f32[48,768]{1,0:T(8,128)}, f32[48,256]{1,0:T(...) custom-call(s32[1]{0:T(128)S(6)} %copy.34.lengths, s32[16]{0:T(128)} %block_map.1, bf16[2,128,768]{2,1,0:T(8,128)(2,1)} %bitcast.5, ...), custom_call_target="tpu_custom_call" | custom-call | tf_op jit(solution)/shard_map/pallas_call | solution.py:1204
  124.7 4.3 %shard_map.298 = (bf16[2,128,768]{2,1,0:T(8,128)(2,1)}, f32[2,128,768]{2,1,0:T(8,128)}, f32[48]{0:T(128)}, f32[48]{0:T(128)}, f32[48,768]{1,0:T(8,128)}, /*index...) custom-call(bf16[2,128,768]{2,1,0:T(8,128)(2,1)} %get-tuple-element., ...), custom_call_target="tpu_custom_call" | custom-call | tf_op jit(solution)/shard_map/pallas_call | solution.py:1237
